TPU v7x, 256 devices: a whole 4x4x8 slice. The times are simulated.
256 devices in a mesh: blk: 16 (over z, y_hi), tp: 16 (over x, y_lo, core).
Axes of the slice: x: 4, y: 4 (y_hi: 2, y_lo: 2; y = y_hi * 2 + y_lo), z: 8, core: 2. Of those that a mesh axis runs over, the one named last changes fastest.
Arguments:
- gate_pre: bfloat16 [8192, 13824], P('blk', 'tp'), may hold values from -6 to 6
- up_pre: bfloat16 [8192, 13824], P('blk', 'tp'), may hold values from -6 to 6
- down_weight: bfloat16 [5120, 13824], P('blk', 'tp'), may hold values from -0.0546875 to 0.0546875
- d_mixed: bfloat16 [8192, 5120], P('blk', 'tp'), may hold values from -6 to 6
Outputs:
- mixed: bfloat16 [8192, 5120], P('blk', 'tp')
- d_gate: bfloat16 [8192, 13824], P('blk', 'tp')
- d_up: bfloat16 [8192, 13824], P('blk', 'tp')
- grad_down: float32 [5120, 13824], P('blk', 'tp')
All inputs are finite; a program needn't handle non-finite values.
Results may differ from a plain program's by a relative error of at most 0.022.
Values may be sent and summed in bfloat16 or wider, within the bound.
No kernel may reach another device: no remote copies, remote signals or barrier semaphores. Data moves between devices by JAX's collectives and lax.ppermute only.
A program may use at most 128 MiB of HBM per device.

v0:
```python
import jax
import jax.numpy as jnp
from jax import lax
from jax.sharding import PartitionSpec as P


def against_rows(left, weight_rows):
    return lax.dot_general(
        left, weight_rows, (((1,), (1,)), ((), ())), preferred_element_type=jnp.float32
    )


def body(gate_pre, up_pre, down_weight, d_mixed):
    gate_value = gate_pre.astype(jnp.float32)
    up_value = up_pre.astype(jnp.float32)
    sigmoid_gate = jax.nn.sigmoid(gate_value)
    activated = gate_value * sigmoid_gate
    hidden = (activated * up_value).astype(jnp.bfloat16)
    partial_value = against_rows(hidden, lax.all_gather(down_weight, "blk", axis=0, tiled=True))
    mixed = lax.psum_scatter(
        partial_value.astype(jnp.bfloat16), "tp", scatter_dimension=1, tiled=True
    )
    cot_full = lax.all_gather(d_mixed, "tp", axis=1, tiled=True)
    columns = cot_full
    d_hidden = jnp.dot(
        columns,
        lax.all_gather(down_weight, "blk", axis=0, tiled=True),
        preferred_element_type=jnp.float32,
    )
    d_gate = (
        d_hidden * up_value * sigmoid_gate * (1.0 + gate_value * (1.0 - sigmoid_gate))
    ).astype(jnp.bfloat16)
    d_up = (d_hidden * activated).astype(jnp.bfloat16)
    columns = cot_full
    grad_down = lax.psum_scatter(
        lax.dot_general(
            columns, hidden, (((0,), (0,)), ((), ())), preferred_element_type=jnp.float32
        ).astype(jnp.bfloat16),
        "blk",
        scatter_dimension=0,
        tiled=True,
    ).astype(jnp.float32)
    return (mixed, d_gate, d_up, grad_down)


def solution(mesh):
    in_specs = (P("blk", "tp"), P("blk", "tp"), P("blk", "tp"), P("blk", "tp"))
    out_specs = (P("blk", "tp"), P("blk", "tp"), P("blk", "tp"), P("blk", "tp"))
    return jax.shard_map(body, mesh=mesh, in_specs=in_specs, out_specs=out_specs, check_vma=False)
```

profile of v0, /device:TPU:1, one launch (start us, length us, event | category | flops | bytes accessed | tf_op | source)
XLA Modules:
  0.0 512.5 jit_solution(11909043123784199449)
XLA Ops:
  7.2 0.0 all-gather.5.cloned.1.call-start
  7.2 0.7 all-gather.5.cloned.1.call-update
  7.9 0.0 all-gather.3.cloned.1.call-start
  7.9 0.7 all-gather.3.cloned.1.call-update
  8.6 0.0 reduce-scatter.7.cloned.1.call-start
  8.7 47.2 %all-gather.5.cloned.1.call-done = bf16[512,5120]{0,1:T(8,128)(2,1)} async-done(((bf16[512,320]{0,1:T(8,128)(2,1)}), bf16[512,5120]{0,1:T(8,128)(2,1)}) %all-gather.5.cloned.1.call-update) | async-done | bytes 5242896 | tf_op jit(solution)/shard_map/all_gather | solution.py:23
  55.9 11.4 %convert_bitcast_fusion = bf16[5120,864]{0,1:T(8,128)(2,1)} fusion(bf16[512,5120]{0,1:T(8,128)(2,1)} %all-gather.5.cloned.1.call-done, bf16[512,864]{0,1:T(8,128)(2,1)} %param.5, bf16[512,864]{0,1:T(8,128)(2,1)} %param.4), kind=kOutput, calls=%fused_computation | convolution fusion | flops 4537810944 | bytes 15859712 | tf_op jit(solution)/shard_map/dot_general | solution.py:36
  67.3 12.8 %copy.10 = bf16[5120,864]{1,0:T(8,128)(2,1)} copy(bf16[5120,864]{0,1:T(8,128)(2,1)} %convert_bitcast_fusion) | data formatting | bytes 17694720
  80.1 0.0 copy-start
  80.1 0.0 copy-start.1
  80.1 0.0 reduce-scatter.7.cloned.1.call-update
  80.1 0.2 reduce-scatter.5.cloned.1.call-start
  80.3 121.5 %all-gather.3.cloned.1.call-done = bf16[5120,864]{1,0:T(8,128)(2,1)} async-done(((bf16[320,864]{1,0:T(8,128)(2,1)}), bf16[5120,864]{1,0:T(8,128)(2,1)}) %all-gather.3.cloned.1.call-update) | async-done | bytes 8847376 | tf_op jit(solution)/shard_map/all_gather | solution.py:19
  201.8 0.0 copy-done
  201.8 0.0 copy-done.1
  201.8 11.2 %convolution_convert_fusion = bf16[512,5120]{0,1:T(8,128)(2,1)} fusion(bf16[5120,864]{1,0:T(8,128)(2,1)} %all-gather.3.cloned.1.call-done, bf16[512,864]{0,1:T(8,128)(2,1)S(1)} %copy-done, bf16[512,864]{0,1:T(8,128)(2,1)S(1)} %copy-done.1), kind=kOutput, calls=%fused_computation.1 | convolution fusion | flops 4536008704 | bytes 15859712 | tf_op jit(solution)/shard_map/dot_general | solution.py:8
  213.0 0.0 reduce-scatter.5.cloned.1.call-update
  213.0 12.2 %multiply_convert_fusion = (bf16[512,864]{0,1:T(8,128)(2,1)}, bf16[512,864]{0,1:T(8,128)(2,1)}) fusion(bf16[512,864]{0,1:T(8,128)(2,1)S(1)} %copy-done.1, bf16[512,864]{0,1:T(8,128)(2,1)S(1)} %copy-done, bf16[512,5120]{0,1:T(8,128)(2,1)} %all-gather.5.cloned.1.call-done, bf16[5120,864]{1,0:T(8,128)(2,1)} %all-gather.3.cloned.1.call-done), kind=kOutput, calls=%fused_computation.15 | convolution fusion | flops 4536483840 | bytes 17629184 | tf_op jit(solution)/shard_map/dot_general | solution.py:25
  225.2 204.9 %reduce-scatter.7.cloned.1.call-done = bf16[320,864]{1,0:T(8,128)(2,1)} async-done(((bf16[5120,864]{1,0:T(8,128)(2,1)}), bf16[320,864]{1,0:T(8,128)(2,1)}) %reduce-scatter.7.cloned.1.call-update) | async-done | bytes 552976
  430.1 1.4 copy.11
  431.5 1.3 copy.9
  432.8 73.2 %reduce-scatter.5.cloned.1.call-done = bf16[512,320]{0,1:T(8,128)(2,1)} async-done(((bf16[512,5120]{0,1:T(8,128)(2,1)}), bf16[512,320]{0,1:T(8,128)(2,1)}) %reduce-scatter.5.cloned.1.call-update) | async-done | bytes 327696 | tf_op jit(solution)/shard_map/reduce_scatter | solution.py:20
Async XLA Ops:
  7.2 48.7 %all-gather.5.cloned.1.call-start = ((), (), s32[]{:S(2)}) async-start(), calls=%async_computation.4 | async-start | bytes 5570560 | tf_op jit(solution)/shard_map/all_gather | solution.py:23
  7.9 193.9 %all-gather.3.cloned.1.call-start = ((), (), s32[]{:S(2)}) async-start(), calls=%async_computation.2 | async-start | bytes 9748480 | tf_op jit(solution)/shard_map/all_gather | solution.py:19
  8.6 421.5 %reduce-scatter.7.cloned.1.call-start = ((), (), s32[]{:S(2)}) async-start(), calls=%async_computation.5 | async-start | bytes 9748480
  80.1 121.7 %copy-start = (bf16[512,864]{0,1:T(8,128)(2,1)S(1)}, bf16[512,864]{0,1:T(8,128)(2,1)}, u32[]{:S(2)}) copy-start(bf16[512,864]{0,1:T(8,128)(2,1)} %param.5) | copy-start | bytes 2654212
  80.1 121.7 %copy-start.1 = (bf16[512,864]{0,1:T(8,128)(2,1)S(1)}, bf16[512,864]{0,1:T(8,128)(2,1)}, u32[]{:S(2)}) copy-start(bf16[512,864]{0,1:T(8,128)(2,1)} %param.4) | copy-start | bytes 2654212
  80.1 425.9 %reduce-scatter.5.cloned.1.call-start = ((), (), s32[]{:S(2)}) async-start(), calls=%async_computation.3 | async-start | bytes 5570560 | tf_op jit(solution)/shard_map/reduce_scatter | solution.py:20
Sparse Core Ops, SparseCore 0:
  9.8 45.9 all-gather.4
  58.5 143.2 all-gather.2
  206.0 224.0 reduce-scatter.6
  433.3 72.6 reduce-scatter.4
where the time goes:
time: 514 us; the launch traced here: 512 us
  waiting for transfers between devices  448 us (87%)
  matrix products  34.8 us (7%)
  local copies, waits for them, and re-layouts  15.5 us (3%)
  between operations  13.8 us (3%)
    unnamed x5, waiting for transfers between devices  206 us
    all_gather x1, waiting for transfers between devices, body(): lax.all_gather(down_weight, 'blk', axis=0, tiled=True)  121 us
    reduce_scatter x1, waiting for transfers between devices, body(): lax.psum_scatter(partial_value.astype(jnp.bfloat16), 'tp', scatter_dimens...  73.2 us
    all_gather x1, waiting for transfers between devices, body(): cot_full = lax.all_gather(d_mixed, 'tp', axis=1, tiled=True)  47.2 us
    unnamed x7, local copies, waits for them, and re-layouts  15.5 us
    dot_general x1, matrix products, body(): jnp.dot(columns, lax.all_gather(down_weight, 'blk', axis=0, tiled=True),...  12.2 us
    dot_general x1, matrix products, body(): lax.dot_general(columns, hidden, (((0,), (0,)), ((), ())), preferred_elem...  11.4 us
    dot_general x1, matrix products, against_rows(): lax.dot_general(left, weight_rows, (((1,), (1,)), ((), ())), preferred_el...  11.2 us
  transfers between devices with their start and end apart: 4, of which 4 were waited for; matrix products, arithmetic and copies ran while one was open for 10% of the time, Pallas kernels for 0%

commit v1 on v0

v1 whole, which is shorter than its diff:
```python
import jax
import jax.numpy as jnp
from jax import lax
from jax.sharding import PartitionSpec as P

AXES = ("blk", "tp")
PLANES = [[2 * z + half for z in range(8)] for half in range(2)]


def route(move):
    pairs = []
    for x in range(4):
        for hi in range(2):
            for lo in range(2):
                for z in range(8):
                    for core in range(2):
                        tx, thi, tlo, tz, tcore = move(x, hi, lo, z, core)
                        source = (z * 2 + hi) * 16 + x * 4 + lo * 2 + core
                        target = (tz * 2 + thi) * 16 + (tx % 4) * 4 + tlo * 2 + tcore
                        pairs.append((source, target))
    return pairs


SIBLING = route(lambda x, hi, lo, z, c: (x, hi, lo, z, 1 - c))
PARTNER = route(lambda x, hi, lo, z, c: (x, 1 - hi, lo, z, c))
TURN = route(lambda x, hi, lo, z, c: (x, c, lo, z, hi))
TURN_LO = route(lambda x, hi, lo, z, c: (x, c, 1 - lo, z, hi))
ALONG_X = {d: route(lambda x, hi, lo, z, c, d=d: (x + d, hi, lo, z, c)) for d in (1, 2, 3)}


def send(value, pairs):
    return lax.ppermute(value, AXES, pairs)


def f32(value):
    return value.astype(jnp.float32)


def bf16(value):
    return value.astype(jnp.bfloat16)


def dot(left, right, dims):
    return lax.dot_general(left, right, ((dims[0], dims[1]), ((), ())), preferred_element_type=jnp.float32)


def first(value, *after):
    return lax.optimization_barrier((value, *after))[0]


def body(gate_pre, up_pre, down_weight, d_mixed):
    blk, tp = lax.axis_index("blk").astype(jnp.uint32), lax.axis_index("tp").astype(jnp.uint32)
    hi, core, lo, x = blk & 1, tp & 1, (tp >> 1) & 1, tp >> 2
    same = hi == core
    zero = jnp.uint32(0)

    def rows(step):
        return ((x + step) & 3) * 640

    weight = lax.all_gather(down_weight, "blk", axis_index_groups=PLANES, axis=0, tiled=True)

    cot = d_mixed.T
    mine, other = send(cot, TURN), send(cot, TURN_LO)

    gate, up = f32(gate_pre.T), f32(up_pre.T)
    sig = jax.nn.sigmoid(gate)
    act = gate * sig
    hid_own = lax.optimization_barrier(bf16(act * up))
    hid_oth = send(hid_own, PARTNER)

    pair = jnp.where(lo == 0, jnp.stack([mine, other]), jnp.stack([other, mine])).reshape(640, 512)
    pair = first(pair, hid_own)
    cot_a = jnp.zeros((2560, 512), jnp.bfloat16)
    cot_a = lax.dynamic_update_slice(cot_a, pair, (rows(0), zero))
    for d in (1, 3, 2):
        piece = send(pair, ALONG_X[d])
        if d == 2:
            piece, hid_oth = lax.optimization_barrier((piece, hid_oth))
        cot_a = lax.dynamic_update_slice(cot_a, piece, (rows(4 - d), zero))
    cot_b = send(cot_a, SIBLING)

    hid_a = jnp.where(same, hid_own, hid_oth)
    hid_b = jnp.where(same, hid_oth, hid_own)
    hid_a, hid_b = lax.optimization_barrier((hid_a, hid_b))

    grad = dot(cot_a, hid_a, ((1,), (1,))) + dot(cot_b, hid_b, ((1,), (1,)))
    grad = bf16(grad)
    grad_down = f32(
        lax.psum_scatter(grad, "blk", axis_index_groups=PLANES, scatter_dimension=0, tiled=True)
    )
    weight = first(weight, grad[:8, :128])

    part_b = bf16(dot(weight, hid_b, ((1,), (0,))))
    got = send(part_b, SIBLING)
    weight = first(weight, part_b)
    part_a = bf16(dot(weight, hid_a, ((1,), (0,))) + f32(got))
    total = f32(lax.dynamic_slice(part_a, (rows(0), zero), (640, 512)))
    for d in (1, 3, 2):
        piece = lax.dynamic_slice(part_a, (rows(d), zero), (640, 512))
        total = total + f32(send(piece, ALONG_X[d]))
    total = bf16(total)
    keep = lax.dynamic_slice(total, (lo * 320, zero), (320, 512))
    give = lax.dynamic_slice(total, ((1 - lo) * 320, zero), (320, 512))
    mixed = bf16(f32(send(keep, TURN)) + f32(send(give, TURN_LO))).T

    weight = first(weight, part_a)
    dh_a = dot(weight, cot_a, ((0,), (0,)))
    dh_b = dot(weight, cot_b, ((0,), (0,)))
    away = send(bf16(jnp.where(same, dh_b, dh_a)), PARTNER)
    d_hidden = jnp.where(same, dh_a, dh_b) + f32(away)
    d_gate = bf16(d_hidden * up * sig * (1.0 + gate * (1.0 - sig))).T
    d_up = bf16(d_hidden * act).T
    return (mixed, d_gate, d_up, grad_down)


def solution(mesh):
    in_specs = (P("blk", "tp"), P("blk", "tp"), P("blk", "tp"), P("blk", "tp"))
    out_specs = (P("blk", "tp"), P("blk", "tp"), P("blk", "tp"), P("blk", "tp"))
    return jax.shard_map(body, mesh=mesh, in_specs=in_specs, out_specs=out_specs, check_vma=False)
```

time: 514 us -> 154 us (0.30)
  waiting for transfers between devices: 448 us -> 53.4 us
  starting transfers between devices: 0.34 us -> 38.7 us
  other arithmetic: 0 us -> 12.5 us
  matrix products: 34.8 us -> 25.9 us
  local copies, waits for them, and re-layouts: 15.5 us -> 8.47 us
    unnamed x5 -> x2, waiting for transfers between devices: 206 us -> 0.7 us
    all_gather x2 -> x1, waiting for transfers between devices: 169 us -> 0.02 us  [body(): lax.all_gather(down_weight, 'blk', axis_index_groups=PLANES, axis=0, tile...]
    reduce_scatter x1, waiting for transfers between devices: 73.2 us -> 0.01 us  [body(): lax.psum_scatter(grad, 'blk', axis_index_groups=PLANES, scatter_dimension...]
    ppermute x0 -> x14, waiting for transfers between devices: none -> 52.7 us  [send(): return lax.ppermute(value, AXES, pairs)]
    ppermute x0 -> x14, starting transfers between devices: none -> 38.6 us  [send(): return lax.ppermute(value, AXES, pairs)]
    unnamed x7 -> x21, local copies, waits for them, and re-layouts: 15.5 us -> 2.04 us
    dot_general x3 -> x6, matrix products: 34.8 us -> 25.9 us  [dot(): lax.dot_general(left, right, ((dims[0], dims[1]), ((), ())), preferred_el...]
    convert_element_type x0 -> x3, other arithmetic: none -> 6.14 us  [the longest x2 4.01 us: bf16(): return value.astype(jnp.bfloat16)]
  transfers between devices with their start and end apart: 4 -> 16, of which waited for: 4 -> 11; matrix products, arithmetic and copies ran while one was open for 10% -> 28% of each run, Pallas kernels for 0% -> 0%
where the time goes in v1:
time: 154 us; the launch traced here: 153 us
  waiting for transfers between devices  53.4 us (35%)
  starting transfers between devices  38.7 us (25%)
  matrix products  25.9 us (17%)
  between operations  14.2 us (9%)
  other arithmetic  12.5 us (8%)
  local copies, waits for them, and re-layouts  8.47 us (6%)
    ppermute x14, waiting for transfers between devices, send(): return lax.ppermute(value, AXES, pairs)  52.7 us
    ppermute x14, starting transfers between devices, send(): return lax.ppermute(value, AXES, pairs)  38.6 us
    dot_general x6, matrix products, dot(): lax.dot_general(left, right, ((dims[0], dims[1]), ((), ())), preferred_el...  25.9 us
    convert_element_type x2, other arithmetic, bf16(): return value.astype(jnp.bfloat16)  4.01 us
    dynamic_update_slice x3, local copies, waits for them, and re-layouts, body(): cot_a = lax.dynamic_update_slice(cot_a, piece, (rows(4 - d), zero))  3.42 us
    transpose x1, other arithmetic, body(): d_up = bf16(d_hidden * act).T  3.41 us
  transfers between devices with their start and end apart: 16, of which 11 were waited for; matrix products, arithmetic and copies ran while one was open for 28% of the time, Pallas kernels for 0%

profile of v1, /device:TPU:1, one launch (start us, length us, event | category | flops | bytes accessed | tf_op | source)
XLA Modules:
  0.0 153.3 jit_solution(4437131695418901540)
XLA Ops:
  7.2 0.7 all-gather.2.cloned.1.call-update
  7.9 0.0 reduce-scatter.2.cloned.1.call-start
  7.9 4.2 %collective-permute-start.1 = (bf16[320,512]{1,0:T(8,128)(2,1)}, bf16[320,512]{1,0:T(8,128)(2,1)S(1)}, u32[]{:S(2)}, u32[]{:S(2)}) collective-permute-start(bf16[320,512]{1,0:T(8,128)(2,1)} %bitcast.63), channel_id=1, source_target_pairs={{0,2},{1,18},{32,34},{33,50},{64,66},{65,82},{96,98},{97,114},{128... | collective-permute-start | bytes 983048 | tf_op jit(solution)/shard_map/ppermute | solution.py:32
  12.2 2.1 %collective-permute-start = (bf16[320,512]{1,0:T(8,128)(2,1)}, bf16[320,512]{1,0:T(8,128)(2,1)S(1)}, u32[]{:S(2)}, u32[]{:S(2)}) collective-permute-start(bf16[320,512]{1,0:T(8,128)(2,1)} %bitcast.64), channel_id=1, source_target_pairs={{0,0},{1,16},{32,32},{33,48},{64,64},{65,80},{96,96},{97,112},{128... | collective-permute-start | bytes 983048 | tf_op jit(solution)/shard_map/ppermute | solution.py:32
  14.3 2.0 %fusion.1 = bf16[864,512]{1,0:T(8,128)(2,1)S(1)} fusion(bf16[512,864]{0,1:T(8,128)(2,1)} %param.5, bf16[512,864]{0,1:T(8,128)(2,1)} %param.4), kind=kLoop, calls=%fused_computation.6 | loop fusion | flops 3538944 | bytes 2654208 | tf_op jit(solution)/shard_map/convert_element_type | solution.py:40
  16.3 0.2 collective-permute-start.3
  16.5 1.1 collective-permute-done.1
  17.6 6.6 %collective-permute-done = bf16[320,512]{1,0:T(8,128)(2,1)S(1)} collective-permute-done((bf16[320,512]{1,0:T(8,128)(2,1)}, bf16[320,512]{1,0:T(8,128)(2,1)S(1)}, u32[]{:S(2)}, u32[]{:S(2)}) %collective-permute-start) | collective-permute-done | bytes 327712 | tf_op jit(solution)/shard_map/ppermute | solution.py:32
  24.2 0.9 maximum_select_fusion
  25.1 17.6 %collective-permute-start.2 = (bf16[640,512]{1,0:T(8,128)(2,1)}, bf16[640,512]{1,0:T(8,128)(2,1)}, u32[]{:S(2)}, u32[]{:S(2)}) collective-permute-start(bf16[640,512]{1,0:T(8,128)(2,1)} %bitcast.5), channel_id=1, source_target_pairs={{0,8},{1,9},{32,40},{33,41},{64,72},{65,73},{96,104},{97,105},{128... | collective-permute-start | bytes 1966088 | tf_op jit(solution)/shard_map/ppermute | solution.py:32
  42.7 0.3 collective-permute-start.10
  43.0 2.4 %collective-permute-start.11 = (bf16[640,512]{1,0:T(8,128)(2,1)}, bf16[640,512]{1,0:T(8,128)(2,1)}, u32[]{:S(2)}, u32[]{:S(2)}) collective-permute-start(bf16[640,512]{1,0:T(8,128)(2,1)} %bitcast.5), channel_id=1, source_target_pairs={{0,12},{1,13},{32,44},{33,45},{64,76},{65,77},{96,108},{97,109},{1... | collective-permute-start | bytes 1966088 | tf_op jit(solution)/shard_map/ppermute | solution.py:32
  45.4 0.2 broadcast_in_dim.3
  45.5 1.1 constant_dynamic-update-slice_fusion.3
  46.7 4.4 %collective-permute-done.2 = bf16[640,512]{1,0:T(8,128)(2,1)} collective-permute-done((bf16[640,512]{1,0:T(8,128)(2,1)}, bf16[640,512]{1,0:T(8,128)(2,1)}, u32[]{:S(2)}, u32[]{:S(2)}) %collective-permute-start.2) | collective-permute-done | bytes 655392 | tf_op jit(solution)/shard_map/ppermute | solution.py:32
  51.1 7.2 %collective-permute-done.10 = bf16[640,512]{1,0:T(8,128)(2,1)} collective-permute-done((bf16[640,512]{1,0:T(8,128)(2,1)}, bf16[640,512]{1,0:T(8,128)(2,1)}, u32[]{:S(2)}, u32[]{:S(2)}) %collective-permute-start.10) | collective-permute-done | bytes 655392 | tf_op jit(solution)/shard_map/ppermute | solution.py:32
  58.3 1.1 constant_dynamic-update-slice_fusion.2
  59.4 1.1 constant_dynamic-update-slice_fusion.1
  60.6 1.1 constant_dynamic-update-slice_fusion
  61.7 0.1 collective-permute-start.12
  61.8 1.9 %broadcast_select_fusion = (bf16[864,512]{1,0:T(8,128)(2,1)S(1)}, bf16[864,512]{1,0:T(8,128)(2,1)S(1)}) fusion(bf16[864,512]{1,0:T(8,128)(2,1)} %collective-permute-done.3, bf16[864,512]{1,0:T(8,128)(2,1)S(1)} %fusion.1, pred[]{:T(512)S(6)} %eq.6), kind=kLoop, calls=%fused_computation.22 | loop fusion | flops 884736 | bytes 3538945 | tf_op jit(solution)/shard_map/jit(_where)/select_n | solution.py:83
  63.8 3.0 %collective-permute-done.12 = bf16[2560,512]{1,0:T(8,128)(2,1)} collective-permute-done((bf16[2560,512]{1,0:T(8,128)(2,1)S(1)}, bf16[2560,512]{1,0:T(8,128)(2,1)}, u32[]{:S(2)}, u32[]{:S(2)}) %collective-permute-start.12) | collective-permute-done | bytes 2621472 | tf_op jit(solution)/shard_map/ppermute | solution.py:32
  66.9 4.7 %fusion.13 = f32[2560,864]{1,0:T(8,128)S(1)} fusion(bf16[2560,512]{1,0:T(8,128)(2,1)} %collective-permute-done.12, bf16[864,512]{1,0:T(8,128)(2,1)S(1)} %get-tuple-element.13), kind=kOutput, calls=%fused_computation.38 | convolution fusion | flops 2264924160 | bytes 12353536 | tf_op jit(solution)/shard_map/dot_general | solution.py:44
  71.5 4.6 %add_convert_fusion = bf16[2560,864]{1,0:T(8,128)(2,1)} fusion(f32[2560,864]{1,0:T(8,128)S(1)} %fusion.13, bf16[2560,512]{1,0:T(8,128)(2,1)S(1)} %constant_dynamic-update-slice_fusion, bf16[864,512]{1,0:T(8,128)(2,1)S(1)} %get-tuple-element.15), kind=kOutput, calls=%fused_computation | convolution fusion | flops 2269347840 | bytes 16777216 | tf_op jit(solution)/shard_map/dot_general | solution.py:44
  76.2 1.1 copy-done.9
  77.3 5.7 %fusion = bf16[2560,512]{0,1:T(8,128)(2,1)S(1)} fusion(bf16[864,512]{1,0:T(8,128)(2,1)S(1)} %copy-done.9, bf16[2560,864]{1,0:T(8,128)(2,1)} %all-gather.2.cloned.1.call-done), kind=kOutput, calls=%fused_computation.3 | convolution fusion | flops 2266234880 | bytes 7929856 | tf_op jit(solution)/shard_map/dot_general | solution.py:44
  83.0 0.4 collective-permute-start.4
  83.4 4.7 %collective-permute-done.4 = bf16[2560,512]{0,1:T(8,128)(2,1)S(1)} collective-permute-done((bf16[2560,512]{0,1:T(8,128)(2,1)S(1)}, bf16[2560,512]{0,1:T(8,128)(2,1)S(1)}, u32[]{:S(2)}, u32[]{:S(2)}) %collective-permute-start.4) | collective-permute-done | bytes 2621472 | tf_op jit(solution)/shard_map/ppermute | solution.py:32
  88.2 3.3 %add_convert_fusion.1 = bf16[2560,512]{0,1:T(8,128)(2,1)S(1)} fusion(bf16[2560,512]{0,1:T(8,128)(2,1)S(1)} %collective-permute-done.4, bf16[2560,864]{1,0:T(8,128)(2,1)S(1)} %copy-done, bf16[864,512]{1,0:T(8,128)(2,1)S(1)} %copy-done.7), kind=kOutput, calls=%fused_computation.1 | convolution fusion | flops 2268856320 | bytes 10551296 | tf_op jit(solution)/shard_map/dot_general | solution.py:44
  91.5 1.4 constant_dynamic-slice_fusion.4
  92.8 1.5 collective-permute-start.5
  94.4 1.3 collective-permute-start.7
  95.6 1.4 collective-permute-start.6
  97.1 2.5 %fusion.12 = f32[864,512]{1,0:T(8,128)S(1)} fusion(bf16[2560,864]{1,0:T(8,128)(2,1)S(1)} %copy-done, bf16[2560,512]{1,0:T(8,128)(2,1)S(1)} %copy-done.2), kind=kOutput, calls=%fused_computation.37 | convolution fusion | flops 2264924160 | bytes 8814592 | tf_op jit(solution)/shard_map/dot_general | solution.py:44
  99.6 5.2 %select_convert_fusion = (bf16[864,512]{1,0:T(8,128)(2,1)}, f32[864,512]{1,0:T(8,128)S(1)}) fusion(f32[864,512]{1,0:T(8,128)S(1)} %fusion.12, pred[]{:T(512)S(6)} %eq.6, bf16[2560,864]{1,0:T(8,128)(2,1)S(1)} %copy-done, bf16[2560,512]{1,0:T(8,128)(2,1)} %collective-permute-done.12), kind=kOutput, calls=%fused_computation.19 | convolution fusion | flops 2265366528 | bytes 11468801 | tf_op jit(solution)/shard_map/dot_general | solution.py:44
  104.8 5.8 %collective-permute-done.5 = bf16[640,512]{0,1:T(8,128)(2,1)} collective-permute-done((bf16[640,512]{0,1:T(8,128)(2,1)}, bf16[640,512]{0,1:T(8,128)(2,1)}, u32[]{:S(2)}, u32[]{:S(2)}) %collective-permute-start.5) | collective-permute-done | bytes 655392 | tf_op jit(solution)/shard_map/ppermute | solution.py:32
  110.5 14.2 %collective-permute-done.7 = bf16[640,512]{0,1:T(8,128)(2,1)} collective-permute-done((bf16[640,512]{0,1:T(8,128)(2,1)}, bf16[640,512]{0,1:T(8,128)(2,1)}, u32[]{:S(2)}, u32[]{:S(2)}) %collective-permute-start.7) | collective-permute-done | bytes 655392 | tf_op jit(solution)/shard_map/ppermute | solution.py:32
  124.7 0.2 collective-permute-done.6
  124.9 2.0 %add_convert_fusion.2 = bf16[640,512]{0,1:T(8,128)(2,1)S(1)} fusion(bf16[640,512]{0,1:T(8,128)(2,1)} %collective-permute-done.7, bf16[640,512]{0,1:T(8,128)(2,1)} %collective-permute-done.6, bf16[640,512]{0,1:T(8,128)(2,1)} %collective-permute-done.5, bf16[2560,512]{0,1:T(8,128)(2,1)} %copy-done.5, u32[]{:T(128)S(6)} %mul.45), kind=kLoop, calls=%fused_computation.20 | loop fusion | flops 2621440 | bytes 3276804 | tf_op jit(solution)/shard_map/convert_element_type | solution.py:40
  126.9 0.3 constant_dynamic-slice_fusion.1
  127.3 1.9 %collective-permute-start.8 = (bf16[320,512]{0,1:T(8,128)(2,1)S(1)}, bf16[320,512]{0,1:T(8,128)(2,1)S(1)}, u32[]{:S(2)}, u32[]{:S(2)}) collective-permute-start(bf16[320,512]{0,1:T(8,128)(2,1)S(1)} %get-tuple-element.29), channel_id=1, source_target_pairs={{0,0},{1,16},{32,32},{33,48},{64,64},{65,80},{96,96},{97,112},{128... | collective-permute-start | bytes 983048 | tf_op jit(solution)/shard_map/ppermute | solution.py:32
  129.2 5.2 %collective-permute-start.9 = (bf16[320,512]{0,1:T(8,128)(2,1)S(1)}, bf16[320,512]{0,1:T(8,128)(2,1)S(1)}, u32[]{:S(2)}, u32[]{:S(2)}) collective-permute-start(bf16[320,512]{0,1:T(8,128)(2,1)S(1)} %get-tuple-element.30), channel_id=1, source_target_pairs={{0,2},{1,18},{32,34},{33,50},{64,66},{65,82},{96,98},{97,114},{128... | collective-permute-start | bytes 983048 | tf_op jit(solution)/shard_map/ppermute | solution.py:32
  134.4 3.4 %fusion.9 = (bf16[512,864]{0,1:T(8,128)(2,1)}, bf16[512,864]{0,1:T(8,128)(2,1)}) fusion(bf16[512,864]{0,1:T(8,128)(2,1)S(1)} %copy-done.4, bf16[864,512]{1,0:T(8,128)(2,1)} %collective-permute-done.13, f32[864,512]{1,0:T(8,128)S(1)} %fusion.12, f32[864,512]{1,0:T(8,128)S(1)} %get-tuple-element.32, pred[]{:T(512)S(6)} %eq.6, bf16[512,864]{0,1:T(8,128)(2,1)S(1)} %copy-done.3), kind=kLoop, calls=%fused_computation.21 | loop fusion | flops 7962624 | bytes 7962625 | tf_op jit(solution)/shard_map/transpose | solution.py:112
  137.8 4.1 %collective-permute-done.8 = bf16[320,512]{0,1:T(8,128)(2,1)S(1)} collective-permute-done((bf16[320,512]{0,1:T(8,128)(2,1)S(1)}, bf16[320,512]{0,1:T(8,128)(2,1)S(1)}, u32[]{:S(2)}, u32[]{:S(2)}) %collective-permute-start.8) | collective-permute-done | bytes 327712 | tf_op jit(solution)/shard_map/ppermute | solution.py:32
  141.8 1.5 collective-permute-done.9
  143.3 0.1 fusion.11
  143.4 0.9 copy.9
  144.3 2.1 %convert_element_type.99 = f32[320,864]{1,0:T(8,128)} convert(bf16[320,864]{1,0:T(8,128)(2,1)} %reduce-scatter.2.cloned.1.call-done) | non-fusion elementwise | flops 276480 | bytes 1658880 | tf_op jit(solution)/shard_map/convert_element_type | solution.py:36
  (27 shorter events, 0.1 us)
Async XLA Ops:
  7.2 69.0 %all-gather.2.cloned.1.call-start = ((), (), s32[]{:S(2)}) async-start(), calls=%async_computation.1 | async-start | bytes 5160960 | tf_op jit(solution)/shard_map/all_gather | solution.py:60
  7.9 136.4 %reduce-scatter.2.cloned.1.call-start = ((), (), s32[]{:S(2)}) async-start(), calls=%async_computation.2 | async-start | bytes 5160960 | tf_op jit(solution)/shard_map/reduce_scatter | solution.py:89
  7.9 9.6 %collective-permute-start.1 = (bf16[320,512]{1,0:T(8,128)(2,1)}, bf16[320,512]{1,0:T(8,128)(2,1)S(1)}, u32[]{:S(2)}, u32[]{:S(2)}) collective-permute-start(bf16[320,512]{1,0:T(8,128)(2,1)} %bitcast.63), channel_id=1, source_target_pairs={{0,2},{1,18},{32,34},{33,50},{64,66},{65,82},{96,98},{97,114},{128... | collective-permute-start | bytes 983048 | tf_op jit(solution)/shard_map/ppermute | solution.py:32
  12.2 12.0 %collective-permute-start = (bf16[320,512]{1,0:T(8,128)(2,1)}, bf16[320,512]{1,0:T(8,128)(2,1)S(1)}, u32[]{:S(2)}, u32[]{:S(2)}) collective-permute-start(bf16[320,512]{1,0:T(8,128)(2,1)} %bitcast.64), channel_id=1, source_target_pairs={{0,0},{1,16},{32,32},{33,48},{64,64},{65,80},{96,96},{97,112},{128... | collective-permute-start | bytes 983048 | tf_op jit(solution)/shard_map/ppermute | solution.py:32
  16.3 30.4 %collective-permute-start.3 = (bf16[864,512]{1,0:T(8,128)(2,1)S(1)}, bf16[864,512]{1,0:T(8,128)(2,1)}, u32[]{:S(2)}, u32[]{:S(2)}) collective-permute-start(bf16[864,512]{1,0:T(8,128)(2,1)S(1)} %fusion.1), channel_id=1, source_target_pairs={{0,16},{1,17},{32,48},{33,49},{64,80},{65,81},{96,112},{97,113},{1... | collective-permute-start | bytes 2654216 | tf_op jit(solution)/shard_map/ppermute | solution.py:32
  25.1 26.0 %collective-permute-start.2 = (bf16[640,512]{1,0:T(8,128)(2,1)}, bf16[640,512]{1,0:T(8,128)(2,1)}, u32[]{:S(2)}, u32[]{:S(2)}) collective-permute-start(bf16[640,512]{1,0:T(8,128)(2,1)} %bitcast.5), channel_id=1, source_target_pairs={{0,8},{1,9},{32,40},{33,41},{64,72},{65,73},{96,104},{97,105},{128... | collective-permute-start | bytes 1966088 | tf_op jit(solution)/shard_map/ppermute | solution.py:32
  42.7 15.6 %collective-permute-start.10 = (bf16[640,512]{1,0:T(8,128)(2,1)}, bf16[640,512]{1,0:T(8,128)(2,1)}, u32[]{:S(2)}, u32[]{:S(2)}) collective-permute-start(bf16[640,512]{1,0:T(8,128)(2,1)} %bitcast.5), channel_id=1, source_target_pairs={{0,4},{1,5},{32,36},{33,37},{64,68},{65,69},{96,100},{97,101},{128... | collective-permute-start | bytes 1966088 | tf_op jit(solution)/shard_map/ppermute | solution.py:32
  43.0 16.4 %collective-permute-start.11 = (bf16[640,512]{1,0:T(8,128)(2,1)}, bf16[640,512]{1,0:T(8,128)(2,1)}, u32[]{:S(2)}, u32[]{:S(2)}) collective-permute-start(bf16[640,512]{1,0:T(8,128)(2,1)} %bitcast.5), channel_id=1, source_target_pairs={{0,12},{1,13},{32,44},{33,45},{64,76},{65,77},{96,108},{97,109},{1... | collective-permute-start | bytes 1966088 | tf_op jit(solution)/shard_map/ppermute | solution.py:32
  61.7 9.8 %copy-start.1 = (bf16[2560,512]{1,0:T(8,128)(2,1)}, bf16[2560,512]{1,0:T(8,128)(2,1)S(1)}, u32[]{:S(2)}) copy-start(bf16[2560,512]{1,0:T(8,128)(2,1)S(1)} %constant_dynamic-update-slice_fusion) | copy-start | bytes 7864324
  61.7 5.1 %collective-permute-start.12 = (bf16[2560,512]{1,0:T(8,128)(2,1)S(1)}, bf16[2560,512]{1,0:T(8,128)(2,1)}, u32[]{:S(2)}, u32[]{:S(2)}) collective-permute-start(bf16[2560,512]{1,0:T(8,128)(2,1)S(1)} %constant_dynamic-update-slice_fusion), channel_id=1, source_target_pairs={{0,1},{1,0},{32,33},{33,32},{64,65},{65,64},{96,97},{97,96},{128,1... | collective-permute-start | bytes 7864328 | tf_op jit(solution)/shard_map/ppermute | solution.py:32
  63.8 3.1 %copy-start.8 = (bf16[864,512]{1,0:T(8,128)(2,1)}, bf16[864,512]{1,0:T(8,128)(2,1)S(1)}, u32[]{:S(2)}) copy-start(bf16[864,512]{1,0:T(8,128)(2,1)S(1)} %get-tuple-element.13) | copy-start | bytes 2654212
  63.8 7.7 %copy-start.6 = (bf16[864,512]{1,0:T(8,128)(2,1)}, bf16[864,512]{1,0:T(8,128)(2,1)S(1)}, u32[]{:S(2)}) copy-start(bf16[864,512]{1,0:T(8,128)(2,1)S(1)} %get-tuple-element.15) | copy-start | bytes 2654212
  76.1 1.2 copy-start.9
  76.1 12.0 %copy-start.7 = (bf16[864,512]{1,0:T(8,128)(2,1)S(1)}, bf16[864,512]{1,0:T(8,128)(2,1)}, u32[]{:S(2)}) copy-start(bf16[864,512]{1,0:T(8,128)(2,1)} %copy-done.6) | copy-start | bytes 2654212
  77.3 10.9 %copy-start = (bf16[2560,864]{1,0:T(8,128)(2,1)S(1)}, bf16[2560,864]{1,0:T(8,128)(2,1)}, u32[]{:S(2)}) copy-start(bf16[2560,864]{1,0:T(8,128)(2,1)} %all-gather.2.cloned.1.call-done) | copy-start | bytes 13271044
  83.0 5.2 %collective-permute-start.4 = (bf16[2560,512]{0,1:T(8,128)(2,1)S(1)}, bf16[2560,512]{0,1:T(8,128)(2,1)S(1)}, u32[]{:S(2)}, u32[]{:S(2)}) collective-permute-start(bf16[2560,512]{0,1:T(8,128)(2,1)S(1)} %fusion), channel_id=1, source_target_pairs={{0,1},{1,0},{32,33},{33,32},{64,65},{65,64},{96,97},{97,96},{128,1... | collective-permute-start | bytes 7864328 | tf_op jit(solution)/shard_map/ppermute | solution.py:32
  91.5 8.1 %copy-start.5 = (bf16[2560,512]{0,1:T(8,128)(2,1)}, bf16[2560,512]{0,1:T(8,128)(2,1)S(1)}, u32[]{:S(2)}) copy-start(bf16[2560,512]{0,1:T(8,128)(2,1)S(1)} %add_convert_fusion.1) | copy-start | bytes 7864324
  91.5 5.6 %copy-start.2 = (bf16[2560,512]{1,0:T(8,128)(2,1)S(1)}, bf16[2560,512]{1,0:T(8,128)(2,1)}, u32[]{:S(2)}) copy-start(bf16[2560,512]{1,0:T(8,128)(2,1)} %copy-done.1) | copy-start | bytes 7864324
  92.8 17.7 %collective-permute-start.5 = (bf16[640,512]{0,1:T(8,128)(2,1)}, bf16[640,512]{0,1:T(8,128)(2,1)}, u32[]{:S(2)}, u32[]{:S(2)}) collective-permute-start(bf16[640,512]{0,1:T(8,128)(2,1)} %get-tuple-element.24), channel_id=1, source_target_pairs={{0,4},{1,5},{32,36},{33,37},{64,68},{65,69},{96,100},{97,101},{128... | collective-permute-start | bytes 1966088 | tf_op jit(solution)/shard_map/ppermute | solution.py:32
  94.4 30.4 %collective-permute-start.7 = (bf16[640,512]{0,1:T(8,128)(2,1)}, bf16[640,512]{0,1:T(8,128)(2,1)}, u32[]{:S(2)}, u32[]{:S(2)}) collective-permute-start(bf16[640,512]{0,1:T(8,128)(2,1)} %get-tuple-element.25), channel_id=1, source_target_pairs={{0,8},{1,9},{32,40},{33,41},{64,72},{65,73},{96,104},{97,105},{128... | collective-permute-start | bytes 1966088 | tf_op jit(solution)/shard_map/ppermute | solution.py:32
  95.6 29.3 %collective-permute-start.6 = (bf16[640,512]{0,1:T(8,128)(2,1)}, bf16[640,512]{0,1:T(8,128)(2,1)}, u32[]{:S(2)}, u32[]{:S(2)}) collective-permute-start(bf16[640,512]{0,1:T(8,128)(2,1)} %get-tuple-element.26), channel_id=1, source_target_pairs={{0,12},{1,13},{32,44},{33,45},{64,76},{65,77},{96,108},{97,109},{1... | collective-permute-start | bytes 1966088 | tf_op jit(solution)/shard_map/ppermute | solution.py:32
  104.8 29.6 %collective-permute-start.13 = (bf16[864,512]{1,0:T(8,128)(2,1)}, bf16[864,512]{1,0:T(8,128)(2,1)}, u32[]{:S(2)}, u32[]{:S(2)}) collective-permute-start(bf16[864,512]{1,0:T(8,128)(2,1)} %get-tuple-element.31), channel_id=1, source_target_pairs={{0,16},{1,17},{32,48},{33,49},{64,80},{65,81},{96,112},{97,113},{1... | collective-permute-start | bytes 2654216 | tf_op jit(solution)/shard_map/ppermute | solution.py:32
  104.8 29.6 %copy-start.3 = (bf16[512,864]{0,1:T(8,128)(2,1)S(1)}, bf16[512,864]{0,1:T(8,128)(2,1)}, u32[]{:S(2)}) copy-start(bf16[512,864]{0,1:T(8,128)(2,1)} %param.5) | copy-start | bytes 2654212
  104.8 29.6 %copy-start.4 = (bf16[512,864]{0,1:T(8,128)(2,1)S(1)}, bf16[512,864]{0,1:T(8,128)(2,1)}, u32[]{:S(2)}) copy-start(bf16[512,864]{0,1:T(8,128)(2,1)} %param.4) | copy-start | bytes 2654212
  127.3 14.6 %collective-permute-start.8 = (bf16[320,512]{0,1:T(8,128)(2,1)S(1)}, bf16[320,512]{0,1:T(8,128)(2,1)S(1)}, u32[]{:S(2)}, u32[]{:S(2)}) collective-permute-start(bf16[320,512]{0,1:T(8,128)(2,1)S(1)} %get-tuple-element.29), channel_id=1, source_target_pairs={{0,0},{1,16},{32,32},{33,48},{64,64},{65,80},{96,96},{97,112},{128... | collective-permute-start | bytes 983048 | tf_op jit(solution)/shard_map/ppermute | solution.py:32
  129.2 14.1 %collective-permute-start.9 = (bf16[320,512]{0,1:T(8,128)(2,1)S(1)}, bf16[320,512]{0,1:T(8,128)(2,1)S(1)}, u32[]{:S(2)}, u32[]{:S(2)}) collective-permute-start(bf16[320,512]{0,1:T(8,128)(2,1)S(1)} %get-tuple-element.30), channel_id=1, source_target_pairs={{0,2},{1,18},{32,34},{33,50},{64,66},{65,82},{96,98},{97,114},{128... | collective-permute-start | bytes 983048 | tf_op jit(solution)/shard_map/ppermute | solution.py:32
Sparse Core Ops, SparseCore 0:
  9.8 62.2 all-gather.1
  76.3 62.3 reduce-scatter.1

commit v2 on v1

--- a/solution.py
+++ b/solution.py
@@ -25,7 +25,9 @@
 PARTNER = route(lambda x, hi, lo, z, c: (x, 1 - hi, lo, z, c))
 TURN = route(lambda x, hi, lo, z, c: (x, c, lo, z, hi))
 TURN_LO = route(lambda x, hi, lo, z, c: (x, c, 1 - lo, z, hi))
-ALONG_X = {d: route(lambda x, hi, lo, z, c, d=d: (x + d, hi, lo, z, c)) for d in (1, 2, 3)}
+X_FAR = route(lambda x, hi, lo, z, c: (x + 2, hi, lo, z, c))
+X_UP = route(lambda x, hi, lo, z, c: (x + 1, hi, lo, z, c))
+X_DOWN = route(lambda x, hi, lo, z, c: (x - 1, hi, lo, z, c))
 
 
 def send(value, pairs):
@@ -54,8 +56,14 @@
     same = hi == core
     zero = jnp.uint32(0)
 
-    def rows(step):
-        return ((x + step) & 3) * 640
+    def x_rows(step):
+        return ((x + (step & 3)) & 3) * 640
+
+    def put(whole, part, row):
+        return lax.dynamic_update_slice(whole, part, (row, zero))
+
+    def rows_of(whole, row, count):
+        return lax.dynamic_slice(whole, (row, zero), (count, whole.shape[1]))
 
     weight = lax.all_gather(down_weight, "blk", axis_index_groups=PLANES, axis=0, tiled=True)
 
@@ -70,13 +78,14 @@
 
     pair = jnp.where(lo == 0, jnp.stack([mine, other]), jnp.stack([other, mine])).reshape(640, 512)
     pair = first(pair, hid_own)
-    cot_a = jnp.zeros((2560, 512), jnp.bfloat16)
-    cot_a = lax.dynamic_update_slice(cot_a, pair, (rows(0), zero))
-    for d in (1, 3, 2):
-        piece = send(pair, ALONG_X[d])
-        if d == 2:
-            piece, hid_oth = lax.optimization_barrier((piece, hid_oth))
-        cot_a = lax.dynamic_update_slice(cot_a, piece, (rows(4 - d), zero))
+    left, right = send(pair, X_UP), send(pair, X_DOWN)
+    far_l, far_r = send(left[:320], X_UP), send(right[320:], X_DOWN)
+    cot_a = put(jnp.zeros((2560, 512), jnp.bfloat16), pair, x_rows(0))
+    cot_a = put(cot_a, left, x_rows(-1))
+    cot_a = put(cot_a, right, x_rows(1))
+    cot_a, far_l, far_r, hid_oth = lax.optimization_barrier((cot_a, far_l, far_r, hid_oth))
+    cot_a = put(cot_a, far_l, x_rows(2))
+    cot_a = put(cot_a, far_r, x_rows(2) + 320)
     cot_b = send(cot_a, SIBLING)
 
     hid_a = jnp.where(same, hid_own, hid_oth)
@@ -94,13 +103,11 @@
     got = send(part_b, SIBLING)
     weight = first(weight, part_b)
     part_a = bf16(dot(weight, hid_a, ((1,), (0,))) + f32(got))
-    total = f32(lax.dynamic_slice(part_a, (rows(0), zero), (640, 512)))
-    for d in (1, 3, 2):
-        piece = lax.dynamic_slice(part_a, (rows(d), zero), (640, 512))
-        total = total + f32(send(piece, ALONG_X[d]))
+    total = f32(rows_of(part_a, x_rows(0), 640))
+    for d, pairs in ((1, X_UP), (3, X_DOWN), (2, X_FAR)):
+        total = total + f32(send(rows_of(part_a, x_rows(d), 640), pairs))
     total = bf16(total)
-    keep = lax.dynamic_slice(total, (lo * 320, zero), (320, 512))
-    give = lax.dynamic_slice(total, ((1 - lo) * 320, zero), (320, 512))
+    keep, give = rows_of(total, lo * 320, 320), rows_of(total, (1 - lo) * 320, 320)
     mixed = bf16(f32(send(keep, TURN)) + f32(send(give, TURN_LO))).T
 
     weight = first(weight, part_a)

time: 154 us -> 150 us (0.974)
  waiting for transfers between devices: 53.4 us -> 67.9 us
  starting transfers between devices: 38.7 us -> 24.8 us
  local copies, waits for them, and re-layouts: 8.47 us -> 5.04 us
    ppermute x14 -> x15, starting transfers between devices: 38.6 us -> 24.7 us  [send(): return lax.ppermute(value, AXES, pairs)]
    all_gather x1, waiting for transfers between devices: 0.02 us -> 7.9 us  [body(): lax.all_gather(down_weight, 'blk', axis_index_groups=PLANES, axis=0, tile...]
    ppermute x14 -> x15, waiting for transfers between devices: 52.7 us -> 59.3 us  [send(): return lax.ppermute(value, AXES, pairs)]
    dynamic_update_slice x4 -> x5, local copies, waits for them, and re-layouts: 4.55 us -> 0.19 us  [put(): return lax.dynamic_update_slice(whole, part, (row, zero))]
  transfers between devices with their start and end apart: 16 -> 17, of which waited for: 11 -> 14; matrix products, arithmetic and copies ran while one was open for 28% -> 26% of each run, Pallas kernels for 0% -> 0%
where the time goes in v2:
time: 150 us
  waiting for transfers between devices  67.9 us (45%)
  matrix products  25.9 us (17%)
  starting transfers between devices  24.8 us (17%)
  between operations  14.3 us (10%)
  other arithmetic  11.8 us (8%)
  local copies, waits for them, and re-layouts  5.04 us (3%)
    ppermute x15, waiting for transfers between devices, send(): return lax.ppermute(value, AXES, pairs)  59.3 us
    dot_general x6, matrix products, dot(): lax.dot_general(left, right, ((dims[0], dims[1]), ((), ())), preferred_el...  25.9 us
    ppermute x15, starting transfers between devices, send(): return lax.ppermute(value, AXES, pairs)  24.7 us
    all_gather x1, waiting for transfers between devices, body(): lax.all_gather(down_weight, 'blk', axis_index_groups=PLANES, axis=0, tile...  7.9 us
    convert_element_type x2, other arithmetic, bf16(): return value.astype(jnp.bfloat16)  4.02 us
    transpose x1, other arithmetic, body(): d_up = bf16(d_hidden * act).T  3.43 us
  transfers between devices with their start and end apart: 17, of which 14 were waited for; matrix products, arithmetic and copies ran while one was open for 26% of the time, Pallas kernels for 0%

profile of v2, /device:TPU:1, one launch (start us, length us, event | category | flops | bytes accessed | tf_op | source)
XLA Modules:
  0.0 149.8 jit_solution(569750344271214106)
XLA Ops:
  7.2 0.7 all-gather.2.cloned.1.call-update
  7.9 4.2 %collective-permute-start.1 = (bf16[320,512]{1,0:T(8,128)(2,1)}, bf16[320,512]{1,0:T(8,128)(2,1)S(1)}, u32[]{:S(2)}, u32[]{:S(2)}) collective-permute-start(bf16[320,512]{1,0:T(8,128)(2,1)} %bitcast.66), channel_id=1, source_target_pairs={{0,2},{1,18},{32,34},{33,50},{64,66},{65,82},{96,98},{97,114},{128... | collective-permute-start | bytes 983048 | tf_op jit(solution)/shard_map/ppermute | solution.py:34
  12.2 2.1 %collective-permute-start = (bf16[320,512]{1,0:T(8,128)(2,1)}, bf16[320,512]{1,0:T(8,128)(2,1)S(1)}, u32[]{:S(2)}, u32[]{:S(2)}) collective-permute-start(bf16[320,512]{1,0:T(8,128)(2,1)} %bitcast.67), channel_id=1, source_target_pairs={{0,0},{1,16},{32,32},{33,48},{64,64},{65,80},{96,96},{97,112},{128... | collective-permute-start | bytes 983048 | tf_op jit(solution)/shard_map/ppermute | solution.py:34
  14.3 2.0 %fusion.1 = bf16[864,512]{1,0:T(8,128)(2,1)S(1)} fusion(bf16[512,864]{0,1:T(8,128)(2,1)} %param.5, bf16[512,864]{0,1:T(8,128)(2,1)} %param.4), kind=kLoop, calls=%fused_computation.6 | loop fusion | flops 3538944 | bytes 2654208 | tf_op jit(solution)/shard_map/convert_element_type | solution.py:42
  16.3 1.3 collective-permute-done.1
  17.6 4.7 %collective-permute-done = bf16[320,512]{1,0:T(8,128)(2,1)S(1)} collective-permute-done((bf16[320,512]{1,0:T(8,128)(2,1)}, bf16[320,512]{1,0:T(8,128)(2,1)S(1)}, u32[]{:S(2)}, u32[]{:S(2)}) %collective-permute-start) | collective-permute-done | bytes 327712 | tf_op jit(solution)/shard_map/ppermute | solution.py:34
  22.3 0.1 maximum_select_fusion
  22.4 2.6 %collective-permute-start.3 = (bf16[640,512]{1,0:T(8,128)(2,1)S(1)}, bf16[640,512]{1,0:T(8,128)(2,1)S(1)}, u32[]{:S(2)}, u32[]{:S(2)}) collective-permute-start(bf16[640,512]{1,0:T(8,128)(2,1)S(1)} %bitcast.61), channel_id=1, source_target_pairs={{0,12},{1,13},{32,44},{33,45},{64,76},{65,77},{96,108},{97,109},{1... | collective-permute-start | bytes 1966088 | tf_op jit(solution)/shard_map/ppermute | solution.py:34
  24.9 13.2 %collective-permute-done.3 = bf16[640,512]{1,0:T(8,128)(2,1)S(1)} collective-permute-done((bf16[640,512]{1,0:T(8,128)(2,1)S(1)}, bf16[640,512]{1,0:T(8,128)(2,1)S(1)}, u32[]{:S(2)}, u32[]{:S(2)}) %collective-permute-start.3) | collective-permute-done | bytes 655392 | tf_op jit(solution)/shard_map/ppermute | solution.py:34
  38.1 1.0 collective-permute-start.5
  39.1 0.3 collective-permute-done.2
  39.4 0.8 copy-done.10
  40.2 0.4 collective-permute-start.4
  40.7 0.2 broadcast_in_dim.3
  40.9 0.9 copy-done.7
  41.8 0.1 copy-done.11
  42.0 0.2 copy-done.9
  42.2 4.1 %collective-permute-done.6 = bf16[864,512]{1,0:T(8,128)(2,1)} collective-permute-done((bf16[864,512]{1,0:T(8,128)(2,1)S(1)}, bf16[864,512]{1,0:T(8,128)(2,1)}, u32[]{:S(2)}, u32[]{:S(2)}) %collective-permute-start.6) | collective-permute-done | bytes 884768 | tf_op jit(solution)/shard_map/ppermute | solution.py:34
  46.3 1.2 collective-permute-done.5
  47.5 2.2 %collective-permute-done.4 = bf16[320,512]{1,0:T(8,128)(2,1)S(1)} collective-permute-done((bf16[320,512]{1,0:T(8,128)(2,1)S(1)}, bf16[320,512]{1,0:T(8,128)(2,1)S(1)}, u32[]{:S(2)}, u32[]{:S(2)}) %collective-permute-start.4) | collective-permute-done | bytes 327712 | tf_op jit(solution)/shard_map/ppermute | solution.py:34
  49.9 2.0 %broadcast_select_fusion = (bf16[864,512]{1,0:T(8,128)(2,1)S(1)}, bf16[864,512]{1,0:T(8,128)(2,1)S(1)}) fusion(bf16[864,512]{1,0:T(8,128)(2,1)} %collective-permute-done.6, bf16[864,512]{1,0:T(8,128)(2,1)S(1)} %fusion.1, pred[]{:T(512)S(6)} %eq.6), kind=kLoop, calls=%fused_computation.22 | loop fusion | flops 884736 | bytes 3538945 | tf_op jit(solution)/shard_map/jit(_where)/select_n | solution.py:92
  51.9 3.0 %collective-permute-done.13 = bf16[2560,512]{1,0:T(8,128)(2,1)} collective-permute-done((bf16[2560,512]{1,0:T(8,128)(2,1)S(1)}, bf16[2560,512]{1,0:T(8,128)(2,1)}, u32[]{:S(2)}, u32[]{:S(2)}) %collective-permute-start.13) | collective-permute-done | bytes 2621472 | tf_op jit(solution)/shard_map/ppermute | solution.py:34
  54.9 4.7 %fusion.13 = f32[2560,864]{1,0:T(8,128)S(1)} fusion(bf16[2560,512]{1,0:T(8,128)(2,1)} %collective-permute-done.13, bf16[864,512]{1,0:T(8,128)(2,1)S(1)} %get-tuple-element.15), kind=kOutput, calls=%fused_computation.39 | convolution fusion | flops 2264924160 | bytes 12353536 | tf_op jit(solution)/shard_map/dot_general | solution.py:46
  59.6 4.6 %add_convert_fusion = bf16[2560,864]{1,0:T(8,128)(2,1)} fusion(f32[2560,864]{1,0:T(8,128)S(1)} %fusion.13, bf16[2560,512]{1,0:T(8,128)(2,1)S(1)} %constant_dynamic-update-slice_fusion, bf16[864,512]{1,0:T(8,128)(2,1)S(1)} %get-tuple-element.17), kind=kOutput, calls=%fused_computation | convolution fusion | flops 2269347840 | bytes 16777216 | tf_op jit(solution)/shard_map/dot_general | solution.py:46
  64.2 7.9 %all-gather.2.cloned.1.call-done = bf16[2560,864]{1,0:T(8,128)(2,1)} async-done(((bf16[320,864]{1,0:T(8,128)(2,1)}), bf16[2560,864]{1,0:T(8,128)(2,1)}) %all-gather.2.cloned.1.call-update) | async-done | bytes 4423696 | tf_op jit(solution)/shard_map/all_gather | solution.py:68
  72.1 5.7 %fusion = bf16[2560,512]{0,1:T(8,128)(2,1)S(1)} fusion(bf16[864,512]{1,0:T(8,128)(2,1)S(1)} %copy-done.15, bf16[2560,864]{1,0:T(8,128)(2,1)} %all-gather.2.cloned.1.call-done), kind=kOutput, calls=%fused_computation.3 | convolution fusion | flops 2266234880 | bytes 7929856 | tf_op jit(solution)/shard_map/dot_general | solution.py:46
  77.8 0.9 collective-permute-start.7
  78.8 4.5 %collective-permute-done.7 = bf16[2560,512]{0,1:T(8,128)(2,1)S(1)} collective-permute-done((bf16[2560,512]{0,1:T(8,128)(2,1)S(1)}, bf16[2560,512]{0,1:T(8,128)(2,1)S(1)}, u32[]{:S(2)}, u32[]{:S(2)}) %collective-permute-start.7) | collective-permute-done | bytes 2621472 | tf_op jit(solution)/shard_map/ppermute | solution.py:34
  83.3 3.3 %add_convert_fusion.1 = bf16[2560,512]{0,1:T(8,128)(2,1)S(1)} fusion(bf16[2560,512]{0,1:T(8,128)(2,1)S(1)} %collective-permute-done.7, bf16[2560,864]{1,0:T(8,128)(2,1)S(1)} %copy-done, bf16[864,512]{1,0:T(8,128)(2,1)S(1)} %copy-done.13), kind=kOutput, calls=%fused_computation.1 | convolution fusion | flops 2268856320 | bytes 10551296 | tf_op jit(solution)/shard_map/dot_general | solution.py:46
  86.7 1.3 constant_dynamic-slice_fusion.4
  88.0 1.2 collective-permute-start.8
  89.2 2.4 %collective-permute-start.10 = (bf16[640,512]{0,1:T(8,128)(2,1)}, bf16[640,512]{0,1:T(8,128)(2,1)}, u32[]{:S(2)}, u32[]{:S(2)}) collective-permute-start(bf16[640,512]{0,1:T(8,128)(2,1)} %get-tuple-element.29), channel_id=1, source_target_pairs={{0,8},{1,9},{32,40},{33,41},{64,72},{65,73},{96,104},{97,105},{128... | collective-permute-start | bytes 1966088 | tf_op jit(solution)/shard_map/ppermute | solution.py:34
  91.6 1.2 collective-permute-start.9
  92.8 2.5 %fusion.12 = f32[864,512]{1,0:T(8,128)S(1)} fusion(bf16[2560,864]{1,0:T(8,128)(2,1)S(1)} %copy-done, bf16[2560,512]{1,0:T(8,128)(2,1)S(1)} %copy-done.2), kind=kOutput, calls=%fused_computation.38 | convolution fusion | flops 2264924160 | bytes 8814592 | tf_op jit(solution)/shard_map/dot_general | solution.py:46
  95.3 5.2 %select_convert_fusion = (bf16[864,512]{1,0:T(8,128)(2,1)}, f32[864,512]{1,0:T(8,128)S(1)}) fusion(f32[864,512]{1,0:T(8,128)S(1)} %fusion.12, pred[]{:T(512)S(6)} %eq.6, bf16[2560,864]{1,0:T(8,128)(2,1)S(1)} %copy-done, bf16[2560,512]{1,0:T(8,128)(2,1)} %collective-permute-done.13), kind=kOutput, calls=%fused_computation.19 | convolution fusion | flops 2265366528 | bytes 11468801 | tf_op jit(solution)/shard_map/dot_general | solution.py:46
  100.4 2.7 %collective-permute-start.14 = (bf16[864,512]{1,0:T(8,128)(2,1)}, bf16[864,512]{1,0:T(8,128)(2,1)}, u32[]{:S(2)}, u32[]{:S(2)}) collective-permute-start(bf16[864,512]{1,0:T(8,128)(2,1)} %get-tuple-element.35), channel_id=1, source_target_pairs={{0,16},{1,17},{32,48},{33,49},{64,80},{65,81},{96,112},{97,113},{1... | collective-permute-start | bytes 2654216 | tf_op jit(solution)/shard_map/ppermute | solution.py:34
  103.2 2.3 %collective-permute-done.8 = bf16[640,512]{0,1:T(8,128)(2,1)} collective-permute-done((bf16[640,512]{0,1:T(8,128)(2,1)}, bf16[640,512]{0,1:T(8,128)(2,1)}, u32[]{:S(2)}, u32[]{:S(2)}) %collective-permute-start.8) | collective-permute-done | bytes 655392 | tf_op jit(solution)/shard_map/ppermute | solution.py:34
  105.5 15.0 %collective-permute-done.10 = bf16[640,512]{0,1:T(8,128)(2,1)} collective-permute-done((bf16[640,512]{0,1:T(8,128)(2,1)}, bf16[640,512]{0,1:T(8,128)(2,1)}, u32[]{:S(2)}, u32[]{:S(2)}) %collective-permute-start.10) | collective-permute-done | bytes 655392 | tf_op jit(solution)/shard_map/ppermute | solution.py:34
  120.4 2.0 %add_convert_fusion.2 = bf16[640,512]{0,1:T(8,128)(2,1)S(1)} fusion(bf16[640,512]{0,1:T(8,128)(2,1)} %collective-permute-done.10, bf16[640,512]{0,1:T(8,128)(2,1)} %collective-permute-done.9, bf16[640,512]{0,1:T(8,128)(2,1)} %collective-permute-done.8, bf16[2560,512]{0,1:T(8,128)(2,1)} %copy-done.5, u32[]{:T(128)S(6)} %mul.46), kind=kLoop, calls=%fused_computation.20 | loop fusion | flops 2621440 | bytes 3276804 | tf_op jit(solution)/shard_map/convert_element_type | solution.py:42
  122.5 0.3 constant_dynamic-slice_fusion.1
  122.8 5.8 %collective-permute-start.11 = (bf16[320,512]{0,1:T(8,128)(2,1)S(1)}, bf16[320,512]{0,1:T(8,128)(2,1)S(1)}, u32[]{:S(2)}, u32[]{:S(2)}) collective-permute-start(bf16[320,512]{0,1:T(8,128)(2,1)S(1)} %get-tuple-element.33), channel_id=1, source_target_pairs={{0,0},{1,16},{32,32},{33,48},{64,64},{65,80},{96,96},{97,112},{128... | collective-permute-start | bytes 983048 | tf_op jit(solution)/shard_map/ppermute | solution.py:34
  128.6 0.1 collective-permute-start.12
  128.7 3.4 %fusion.9 = (bf16[512,864]{0,1:T(8,128)(2,1)}, bf16[512,864]{0,1:T(8,128)(2,1)}) fusion(bf16[512,864]{0,1:T(8,128)(2,1)S(1)} %copy-done.4, bf16[864,512]{1,0:T(8,128)(2,1)} %collective-permute-done.14, f32[864,512]{1,0:T(8,128)S(1)} %fusion.12, f32[864,512]{1,0:T(8,128)S(1)} %get-tuple-element.36, pred[]{:T(512)S(6)} %eq.6, bf16[512,864]{0,1:T(8,128)(2,1)S(1)} %copy-done.3), kind=kLoop, calls=%fused_computation.21 | loop fusion | flops 7962624 | bytes 7962625 | tf_op jit(solution)/shard_map/transpose | solution.py:119
  132.1 4.6 %collective-permute-done.11 = bf16[320,512]{0,1:T(8,128)(2,1)S(1)} collective-permute-done((bf16[320,512]{0,1:T(8,128)(2,1)S(1)}, bf16[320,512]{0,1:T(8,128)(2,1)S(1)}, u32[]{:S(2)}, u32[]{:S(2)}) %collective-permute-start.11) | collective-permute-done | bytes 327712 | tf_op jit(solution)/shard_map/ppermute | solution.py:34
  136.7 3.1 %collective-permute-done.12 = bf16[320,512]{0,1:T(8,128)(2,1)S(1)} collective-permute-done((bf16[320,512]{0,1:T(8,128)(2,1)S(1)}, bf16[320,512]{0,1:T(8,128)(2,1)S(1)}, u32[]{:S(2)}, u32[]{:S(2)}) %collective-permute-start.12) | collective-permute-done | bytes 327712 | tf_op jit(solution)/shard_map/ppermute | solution.py:34
  139.8 0.1 fusion.11
  139.9 0.9 copy.9
  140.8 2.1 %convert_element_type.99 = f32[320,864]{1,0:T(8,128)} convert(bf16[320,864]{1,0:T(8,128)(2,1)} %reduce-scatter.2.cloned.1.call-done) | non-fusion elementwise | flops 276480 | bytes 1658880 | tf_op jit(solution)/shard_map/convert_element_type | solution.py:38
  (44 shorter events, 0.5 us)
Async XLA Ops:
  7.2 65.0 %all-gather.2.cloned.1.call-start = ((), (), s32[]{:S(2)}) async-start(), calls=%async_computation.1 | async-start | bytes 5160960 | tf_op jit(solution)/shard_map/all_gather | solution.py:68
  7.9 132.9 %reduce-scatter.2.cloned.1.call-start = ((), (), s32[]{:S(2)}) async-start(), calls=%async_computation.2 | async-start | bytes 5160960 | tf_op jit(solution)/shard_map/reduce_scatter | solution.py:98
  7.9 9.6 %collective-permute-start.1 = (bf16[320,512]{1,0:T(8,128)(2,1)}, bf16[320,512]{1,0:T(8,128)(2,1)S(1)}, u32[]{:S(2)}, u32[]{:S(2)}) collective-permute-start(bf16[320,512]{1,0:T(8,128)(2,1)} %bitcast.66), channel_id=1, source_target_pairs={{0,2},{1,18},{32,34},{33,50},{64,66},{65,82},{96,98},{97,114},{128... | collective-permute-start | bytes 983048 | tf_op jit(solution)/shard_map/ppermute | solution.py:34
  12.2 10.1 %collective-permute-start = (bf16[320,512]{1,0:T(8,128)(2,1)}, bf16[320,512]{1,0:T(8,128)(2,1)S(1)}, u32[]{:S(2)}, u32[]{:S(2)}) collective-permute-start(bf16[320,512]{1,0:T(8,128)(2,1)} %bitcast.67), channel_id=1, source_target_pairs={{0,0},{1,16},{32,32},{33,48},{64,64},{65,80},{96,96},{97,112},{128... | collective-permute-start | bytes 983048 | tf_op jit(solution)/shard_map/ppermute | solution.py:34
  22.4 17.1 %copy-start.6 = (bf16[2,320,512]{2,1,0:T(8,128)(2,1)}, bf16[2,320,512]{2,1,0:T(8,128)(2,1)S(1)}, u32[]{:S(2)}) copy-start(bf16[2,320,512]{2,1,0:T(8,128)(2,1)S(1)} %maximum_select_fusion) | copy-start | bytes 1966084
  22.4 15.7 %collective-permute-start.3 = (bf16[640,512]{1,0:T(8,128)(2,1)S(1)}, bf16[640,512]{1,0:T(8,128)(2,1)S(1)}, u32[]{:S(2)}, u32[]{:S(2)}) collective-permute-start(bf16[640,512]{1,0:T(8,128)(2,1)S(1)} %bitcast.61), channel_id=1, source_target_pairs={{0,12},{1,13},{32,44},{33,45},{64,76},{65,77},{96,108},{97,109},{1... | collective-permute-start | bytes 1966088 | tf_op jit(solution)/shard_map/ppermute | solution.py:34
  24.9 14.5 %collective-permute-start.2 = (bf16[640,512]{1,0:T(8,128)(2,1)S(1)}, bf16[640,512]{1,0:T(8,128)(2,1)S(1)}, u32[]{:S(2)}, u32[]{:S(2)}) collective-permute-start(bf16[640,512]{1,0:T(8,128)(2,1)S(1)} %bitcast.62), channel_id=1, source_target_pairs={{0,4},{1,5},{32,36},{33,37},{64,68},{65,69},{96,100},{97,101},{128... | collective-permute-start | bytes 1966088 | tf_op jit(solution)/shard_map/ppermute | solution.py:34
  24.9 21.4 %collective-permute-start.6 = (bf16[864,512]{1,0:T(8,128)(2,1)S(1)}, bf16[864,512]{1,0:T(8,128)(2,1)}, u32[]{:S(2)}, u32[]{:S(2)}) collective-permute-start(bf16[864,512]{1,0:T(8,128)(2,1)S(1)} %fusion.1), channel_id=1, source_target_pairs={{0,16},{1,17},{32,48},{33,49},{64,80},{65,81},{96,112},{97,113},{1... | collective-permute-start | bytes 2654216 | tf_op jit(solution)/shard_map/ppermute | solution.py:34
  38.1 1.3 copy-start.8
  38.1 9.4 %collective-permute-start.5 = (bf16[320,512]{1,0:T(8,128)(2,1)S(1)}, bf16[320,512]{1,0:T(8,128)(2,1)S(1)}, u32[]{:S(2)}, u32[]{:S(2)}) collective-permute-start(bf16[320,512]{1,0:T(8,128)(2,1)S(1)} %slice.10), channel_id=1, source_target_pairs={{0,12},{1,13},{32,44},{33,45},{64,76},{65,77},{96,108},{97,109},{1... | collective-permute-start | bytes 983048 | tf_op jit(solution)/shard_map/ppermute | solution.py:34
  39.4 0.8 copy-start.10
  40.2 9.5 %collective-permute-start.4 = (bf16[320,512]{1,0:T(8,128)(2,1)S(1)}, bf16[320,512]{1,0:T(8,128)(2,1)S(1)}, u32[]{:S(2)}, u32[]{:S(2)}) collective-permute-start(bf16[320,512]{1,0:T(8,128)(2,1)S(1)} %slice.9), channel_id=1, source_target_pairs={{0,4},{1,5},{32,36},{33,37},{64,68},{65,69},{96,100},{97,101},{128... | collective-permute-start | bytes 983048 | tf_op jit(solution)/shard_map/ppermute | solution.py:34
  40.7 1.1 copy-start.7
  40.7 1.3 copy-start.11
  40.7 1.5 copy-start.9
  49.7 9.8 %copy-start.1 = (bf16[2560,512]{1,0:T(8,128)(2,1)}, bf16[2560,512]{1,0:T(8,128)(2,1)S(1)}, u32[]{:S(2)}) copy-start(bf16[2560,512]{1,0:T(8,128)(2,1)S(1)} %constant_dynamic-update-slice_fusion) | copy-start | bytes 7864324
  49.8 5.1 %collective-permute-start.13 = (bf16[2560,512]{1,0:T(8,128)(2,1)S(1)}, bf16[2560,512]{1,0:T(8,128)(2,1)}, u32[]{:S(2)}, u32[]{:S(2)}) collective-permute-start(bf16[2560,512]{1,0:T(8,128)(2,1)S(1)} %constant_dynamic-update-slice_fusion), channel_id=1, source_target_pairs={{0,1},{1,0},{32,33},{33,32},{64,65},{65,64},{96,97},{97,96},{128,1... | collective-permute-start | bytes 7864328 | tf_op jit(solution)/shard_map/ppermute | solution.py:34
  51.8 3.1 %copy-start.14 = (bf16[864,512]{1,0:T(8,128)(2,1)}, bf16[864,512]{1,0:T(8,128)(2,1)S(1)}, u32[]{:S(2)}) copy-start(bf16[864,512]{1,0:T(8,128)(2,1)S(1)} %get-tuple-element.15) | copy-start | bytes 2654212
  51.9 7.8 %copy-start.12 = (bf16[864,512]{1,0:T(8,128)(2,1)}, bf16[864,512]{1,0:T(8,128)(2,1)S(1)}, u32[]{:S(2)}) copy-start(bf16[864,512]{1,0:T(8,128)(2,1)S(1)} %get-tuple-element.17) | copy-start | bytes 2654212
  64.2 7.9 %copy-start.15 = (bf16[864,512]{1,0:T(8,128)(2,1)S(1)}, bf16[864,512]{1,0:T(8,128)(2,1)}, u32[]{:S(2)}) copy-start(bf16[864,512]{1,0:T(8,128)(2,1)} %copy-done.14) | copy-start | bytes 2654212
  64.2 19.1 %copy-start.13 = (bf16[864,512]{1,0:T(8,128)(2,1)S(1)}, bf16[864,512]{1,0:T(8,128)(2,1)}, u32[]{:S(2)}) copy-start(bf16[864,512]{1,0:T(8,128)(2,1)} %copy-done.12) | copy-start | bytes 2654212
  72.1 11.2 %copy-start = (bf16[2560,864]{1,0:T(8,128)(2,1)S(1)}, bf16[2560,864]{1,0:T(8,128)(2,1)}, u32[]{:S(2)}) copy-start(bf16[2560,864]{1,0:T(8,128)(2,1)} %all-gather.2.cloned.1.call-done) | copy-start | bytes 13271044
  77.8 5.5 %collective-permute-start.7 = (bf16[2560,512]{0,1:T(8,128)(2,1)S(1)}, bf16[2560,512]{0,1:T(8,128)(2,1)S(1)}, u32[]{:S(2)}, u32[]{:S(2)}) collective-permute-start(bf16[2560,512]{0,1:T(8,128)(2,1)S(1)} %fusion), channel_id=1, source_target_pairs={{0,1},{1,0},{32,33},{33,32},{64,65},{65,64},{96,97},{97,96},{128,1... | collective-permute-start | bytes 7864328 | tf_op jit(solution)/shard_map/ppermute | solution.py:34
  86.6 8.6 %copy-start.5 = (bf16[2560,512]{0,1:T(8,128)(2,1)}, bf16[2560,512]{0,1:T(8,128)(2,1)S(1)}, u32[]{:S(2)}) copy-start(bf16[2560,512]{0,1:T(8,128)(2,1)S(1)} %add_convert_fusion.1) | copy-start | bytes 7864324
  86.6 6.1 %copy-start.2 = (bf16[2560,512]{1,0:T(8,128)(2,1)S(1)}, bf16[2560,512]{1,0:T(8,128)(2,1)}, u32[]{:S(2)}) copy-start(bf16[2560,512]{1,0:T(8,128)(2,1)} %copy-done.1) | copy-start | bytes 7864324
  88.0 17.5 %collective-permute-start.8 = (bf16[640,512]{0,1:T(8,128)(2,1)}, bf16[640,512]{0,1:T(8,128)(2,1)}, u32[]{:S(2)}, u32[]{:S(2)}) collective-permute-start(bf16[640,512]{0,1:T(8,128)(2,1)} %get-tuple-element.28), channel_id=1, source_target_pairs={{0,4},{1,5},{32,36},{33,37},{64,68},{65,69},{96,100},{97,101},{128... | collective-permute-start | bytes 1966088 | tf_op jit(solution)/shard_map/ppermute | solution.py:34
  89.2 31.2 %collective-permute-start.10 = (bf16[640,512]{0,1:T(8,128)(2,1)}, bf16[640,512]{0,1:T(8,128)(2,1)}, u32[]{:S(2)}, u32[]{:S(2)}) collective-permute-start(bf16[640,512]{0,1:T(8,128)(2,1)} %get-tuple-element.29), channel_id=1, source_target_pairs={{0,8},{1,9},{32,40},{33,41},{64,72},{65,73},{96,104},{97,105},{128... | collective-permute-start | bytes 1966088 | tf_op jit(solution)/shard_map/ppermute | solution.py:34
  91.6 28.8 %collective-permute-start.9 = (bf16[640,512]{0,1:T(8,128)(2,1)}, bf16[640,512]{0,1:T(8,128)(2,1)}, u32[]{:S(2)}, u32[]{:S(2)}) collective-permute-start(bf16[640,512]{0,1:T(8,128)(2,1)} %get-tuple-element.30), channel_id=1, source_target_pairs={{0,12},{1,13},{32,44},{33,45},{64,76},{65,77},{96,108},{97,109},{1... | collective-permute-start | bytes 1966088 | tf_op jit(solution)/shard_map/ppermute | solution.py:34
  100.4 28.3 %collective-permute-start.14 = (bf16[864,512]{1,0:T(8,128)(2,1)}, bf16[864,512]{1,0:T(8,128)(2,1)}, u32[]{:S(2)}, u32[]{:S(2)}) collective-permute-start(bf16[864,512]{1,0:T(8,128)(2,1)} %get-tuple-element.35), channel_id=1, source_target_pairs={{0,16},{1,17},{32,48},{33,49},{64,80},{65,81},{96,112},{97,113},{1... | collective-permute-start | bytes 2654216 | tf_op jit(solution)/shard_map/ppermute | solution.py:34
  103.2 25.5 %copy-start.3 = (bf16[512,864]{0,1:T(8,128)(2,1)S(1)}, bf16[512,864]{0,1:T(8,128)(2,1)}, u32[]{:S(2)}) copy-start(bf16[512,864]{0,1:T(8,128)(2,1)} %param.5) | copy-start | bytes 2654212
  103.2 25.5 %copy-start.4 = (bf16[512,864]{0,1:T(8,128)(2,1)S(1)}, bf16[512,864]{0,1:T(8,128)(2,1)}, u32[]{:S(2)}) copy-start(bf16[512,864]{0,1:T(8,128)(2,1)} %param.4) | copy-start | bytes 2654212
  122.8 13.9 %collective-permute-start.11 = (bf16[320,512]{0,1:T(8,128)(2,1)S(1)}, bf16[320,512]{0,1:T(8,128)(2,1)S(1)}, u32[]{:S(2)}, u32[]{:S(2)}) collective-permute-start(bf16[320,512]{0,1:T(8,128)(2,1)S(1)} %get-tuple-element.33), channel_id=1, source_target_pairs={{0,0},{1,16},{32,32},{33,48},{64,64},{65,80},{96,96},{97,112},{128... | collective-permute-start | bytes 983048 | tf_op jit(solution)/shard_map/ppermute | solution.py:34
  128.6 11.2 %collective-permute-start.12 = (bf16[320,512]{0,1:T(8,128)(2,1)S(1)}, bf16[320,512]{0,1:T(8,128)(2,1)S(1)}, u32[]{:S(2)}, u32[]{:S(2)}) collective-permute-start(bf16[320,512]{0,1:T(8,128)(2,1)S(1)} %get-tuple-element.34), channel_id=1, source_target_pairs={{0,2},{1,18},{32,34},{33,50},{64,66},{65,82},{96,98},{97,114},{128... | collective-permute-start | bytes 983048 | tf_op jit(solution)/shard_map/ppermute | solution.py:34
Sparse Core Ops, SparseCore 0:
  9.8 62.2 all-gather.1
  74.7 57.6 reduce-scatter.1

commit v3 on v2

--- a/solution.py
+++ b/solution.py
@@ -1,6 +1,7 @@
 import jax
 import jax.numpy as jnp
 from jax import lax
+from jax.experimental.layout import Layout, with_layout_constraint
 from jax.sharding import PartitionSpec as P
 
 AXES = ("blk", "tp")
@@ -40,6 +41,10 @@
 
 def bf16(value):
     return value.astype(jnp.bfloat16)
+
+
+def row_major(value):
+    return with_layout_constraint(value, Layout((0, 1)))
 
 
 def dot(left, right, dims):
@@ -99,16 +104,18 @@
     )
     weight = first(weight, grad[:8, :128])
 
-    part_b = bf16(dot(weight, hid_b, ((1,), (0,))))
+    part_b = row_major(bf16(dot(weight, hid_b, ((1,), (0,)))))
     got = send(part_b, SIBLING)
     weight = first(weight, part_b)
-    part_a = bf16(dot(weight, hid_a, ((1,), (0,))) + f32(got))
+    part_a = row_major(bf16(dot(weight, hid_a, ((1,), (0,))) + f32(got)))
     total = f32(rows_of(part_a, x_rows(0), 640))
     for d, pairs in ((1, X_UP), (3, X_DOWN), (2, X_FAR)):
         total = total + f32(send(rows_of(part_a, x_rows(d), 640), pairs))
     total = bf16(total)
     keep, give = rows_of(total, lo * 320, 320), rows_of(total, (1 - lo) * 320, 320)
-    mixed = bf16(f32(send(keep, TURN)) + f32(send(give, TURN_LO))).T
+    keep, give = send(keep, TURN), send(give, TURN_LO)
+    keep, give, grad_down = lax.optimization_barrier((keep, give, grad_down))
+    mixed = bf16(f32(keep) + f32(give)).T
 
     weight = first(weight, part_a)
     dh_a = dot(weight, cot_a, ((0,), (0,)))

time: 150 us -> 146 us (0.973)
  waiting for transfers between devices: 67.9 us -> 62.7 us
  other arithmetic: 11.8 us -> 13.5 us
    ppermute x15, waiting for transfers between devices: 59.3 us -> 53.8 us  [send(): return lax.ppermute(value, AXES, pairs)]
    transpose x1, other arithmetic: 0.1 us -> 1.88 us  [body(): mixed = bf16(f32(keep) + f32(give)).T]
  transfers between devices with their start and end apart: 17 -> 17, of which waited for: 14 -> 14; matrix products, arithmetic and copies ran while one was open for 26% -> 27% of each run, Pallas kernels for 0% -> 0%
where the time goes in v3:
time: 146 us; the launch traced here: 145 us
  waiting for transfers between devices  62.7 us (43%)
  matrix products  25.5 us (17%)
  starting transfers between devices  24.7 us (17%)
  between operations  14.3 us (10%)
  other arithmetic  13.5 us (9%)
  local copies, waits for them, and re-layouts  4.66 us (3%)
    ppermute x15, waiting for transfers between devices, send(): return lax.ppermute(value, AXES, pairs)  53.8 us
    dot_general x6, matrix products, dot(): lax.dot_general(left, right, ((dims[0], dims[1]), ((), ())), preferred_el...  25.5 us
    ppermute x15, starting transfers between devices, send(): return lax.ppermute(value, AXES, pairs)  24.6 us
    all_gather x1, waiting for transfers between devices, body(): lax.all_gather(down_weight, 'blk', axis_index_groups=PLANES, axis=0, tile...  7.9 us
    convert_element_type x2, other arithmetic, bf16(): return value.astype(jnp.bfloat16)  4.03 us
    transpose x1, other arithmetic, body(): d_up = bf16(d_hidden * act).T  3.43 us
  transfers between devices with their start and end apart: 17, of which 14 were waited for; matrix products, arithmetic and copies ran while one was open for 27% of the time, Pallas kernels for 0%

profile of v3, /device:TPU:1, one launch (start us, length us, event | category | flops | bytes accessed | tf_op | source)
XLA Modules:
  0.0 145.4 jit_solution(9809173613600626804)
XLA Ops:
  7.2 0.7 all-gather.2.cloned.1.call-update
  7.9 4.2 %collective-permute-start.1 = (bf16[320,512]{1,0:T(8,128)(2,1)}, bf16[320,512]{1,0:T(8,128)(2,1)S(1)}, u32[]{:S(2)}, u32[]{:S(2)}) collective-permute-start(bf16[320,512]{1,0:T(8,128)(2,1)} %bitcast.66), channel_id=1, source_target_pairs={{0,2},{1,18},{32,34},{33,50},{64,66},{65,82},{96,98},{97,114},{128... | collective-permute-start | bytes 983048 | tf_op jit(solution)/shard_map/ppermute | solution.py:35
  12.2 2.1 %collective-permute-start = (bf16[320,512]{1,0:T(8,128)(2,1)}, bf16[320,512]{1,0:T(8,128)(2,1)S(1)}, u32[]{:S(2)}, u32[]{:S(2)}) collective-permute-start(bf16[320,512]{1,0:T(8,128)(2,1)} %bitcast.67), channel_id=1, source_target_pairs={{0,0},{1,16},{32,32},{33,48},{64,64},{65,80},{96,96},{97,112},{128... | collective-permute-start | bytes 983048 | tf_op jit(solution)/shard_map/ppermute | solution.py:35
  14.3 2.0 %fusion.1 = bf16[864,512]{1,0:T(8,128)(2,1)S(1)} fusion(bf16[512,864]{0,1:T(8,128)(2,1)} %param.5, bf16[512,864]{0,1:T(8,128)(2,1)} %param.4), kind=kLoop, calls=%fused_computation.6 | loop fusion | flops 3538944 | bytes 2654208 | tf_op jit(solution)/shard_map/convert_element_type | solution.py:43
  16.3 1.3 collective-permute-done.1
  17.6 4.7 %collective-permute-done = bf16[320,512]{1,0:T(8,128)(2,1)S(1)} collective-permute-done((bf16[320,512]{1,0:T(8,128)(2,1)}, bf16[320,512]{1,0:T(8,128)(2,1)S(1)}, u32[]{:S(2)}, u32[]{:S(2)}) %collective-permute-start) | collective-permute-done | bytes 327712 | tf_op jit(solution)/shard_map/ppermute | solution.py:35
  22.3 0.1 maximum_select_fusion
  22.4 2.6 %collective-permute-start.3 = (bf16[640,512]{1,0:T(8,128)(2,1)S(1)}, bf16[640,512]{1,0:T(8,128)(2,1)S(1)}, u32[]{:S(2)}, u32[]{:S(2)}) collective-permute-start(bf16[640,512]{1,0:T(8,128)(2,1)S(1)} %bitcast.61), channel_id=1, source_target_pairs={{0,12},{1,13},{32,44},{33,45},{64,76},{65,77},{96,108},{97,109},{1... | collective-permute-start | bytes 1966088 | tf_op jit(solution)/shard_map/ppermute | solution.py:35
  24.9 13.2 %collective-permute-done.3 = bf16[640,512]{1,0:T(8,128)(2,1)S(1)} collective-permute-done((bf16[640,512]{1,0:T(8,128)(2,1)S(1)}, bf16[640,512]{1,0:T(8,128)(2,1)S(1)}, u32[]{:S(2)}, u32[]{:S(2)}) %collective-permute-start.3) | collective-permute-done | bytes 655392 | tf_op jit(solution)/shard_map/ppermute | solution.py:35
  38.1 1.0 collective-permute-start.5
  39.1 0.3 collective-permute-done.2
  39.4 0.8 copy-done.10
  40.2 0.4 collective-permute-start.4
  40.7 0.2 broadcast_in_dim.3
  40.9 0.9 copy-done.7
  41.8 0.1 copy-done.11
  42.0 0.2 copy-done.9
  42.2 4.1 %collective-permute-done.6 = bf16[864,512]{1,0:T(8,128)(2,1)} collective-permute-done((bf16[864,512]{1,0:T(8,128)(2,1)S(1)}, bf16[864,512]{1,0:T(8,128)(2,1)}, u32[]{:S(2)}, u32[]{:S(2)}) %collective-permute-start.6) | collective-permute-done | bytes 884768 | tf_op jit(solution)/shard_map/ppermute | solution.py:35
  46.3 1.2 collective-permute-done.5
  47.5 2.2 %collective-permute-done.4 = bf16[320,512]{1,0:T(8,128)(2,1)S(1)} collective-permute-done((bf16[320,512]{1,0:T(8,128)(2,1)S(1)}, bf16[320,512]{1,0:T(8,128)(2,1)S(1)}, u32[]{:S(2)}, u32[]{:S(2)}) %collective-permute-start.4) | collective-permute-done | bytes 327712 | tf_op jit(solution)/shard_map/ppermute | solution.py:35
  49.8 0.1 collective-permute-start.13
  49.9 2.0 %broadcast_select_fusion = (bf16[864,512]{1,0:T(8,128)(2,1)S(1)}, bf16[864,512]{1,0:T(8,128)(2,1)S(1)}) fusion(bf16[864,512]{1,0:T(8,128)(2,1)} %collective-permute-done.6, bf16[864,512]{1,0:T(8,128)(2,1)S(1)} %fusion.1, pred[]{:T(512)S(6)} %eq.6), kind=kLoop, calls=%fused_computation.22 | loop fusion | flops 884736 | bytes 3538945 | tf_op jit(solution)/shard_map/jit(_where)/select_n | solution.py:97
  51.9 3.0 %collective-permute-done.13 = bf16[2560,512]{1,0:T(8,128)(2,1)} collective-permute-done((bf16[2560,512]{1,0:T(8,128)(2,1)S(1)}, bf16[2560,512]{1,0:T(8,128)(2,1)}, u32[]{:S(2)}, u32[]{:S(2)}) %collective-permute-start.13) | collective-permute-done | bytes 2621472 | tf_op jit(solution)/shard_map/ppermute | solution.py:35
  54.9 4.7 %fusion.12 = f32[2560,864]{1,0:T(8,128)S(1)} fusion(bf16[2560,512]{1,0:T(8,128)(2,1)} %collective-permute-done.13, bf16[864,512]{1,0:T(8,128)(2,1)S(1)} %get-tuple-element.18), kind=kOutput, calls=%fused_computation.38 | convolution fusion | flops 2264924160 | bytes 12353536 | tf_op jit(solution)/shard_map/dot_general | solution.py:51
  59.6 4.6 %add_convert_fusion = bf16[2560,864]{1,0:T(8,128)(2,1)} fusion(f32[2560,864]{1,0:T(8,128)S(1)} %fusion.12, bf16[2560,512]{1,0:T(8,128)(2,1)S(1)} %constant_dynamic-update-slice_fusion, bf16[864,512]{1,0:T(8,128)(2,1)S(1)} %get-tuple-element.20), kind=kOutput, calls=%fused_computation | convolution fusion | flops 2269347840 | bytes 16777216 | tf_op jit(solution)/shard_map/dot_general | solution.py:51
  64.2 7.9 %all-gather.2.cloned.1.call-done = bf16[2560,864]{1,0:T(8,128)(2,1)} async-done(((bf16[320,864]{1,0:T(8,128)(2,1)}), bf16[2560,864]{1,0:T(8,128)(2,1)}) %all-gather.2.cloned.1.call-update) | async-done | bytes 4423696 | tf_op jit(solution)/shard_map/all_gather | solution.py:73
  72.1 5.5 %fusion = bf16[2560,512]{1,0:T(8,128)(2,1)S(1)} fusion(bf16[2560,864]{1,0:T(8,128)(2,1)} %all-gather.2.cloned.1.call-done, bf16[864,512]{1,0:T(8,128)(2,1)S(1)} %copy-done.15), kind=kOutput, calls=%fused_computation.3 | convolution fusion | flops 2266234880 | bytes 7929856 | tf_op jit(solution)/shard_map/dot_general | solution.py:51
  77.7 0.9 collective-permute-start.7
  78.6 4.5 %collective-permute-done.7 = bf16[2560,512]{1,0:T(8,128)(2,1)S(1)} collective-permute-done((bf16[2560,512]{1,0:T(8,128)(2,1)S(1)}, bf16[2560,512]{1,0:T(8,128)(2,1)S(1)}, u32[]{:S(2)}, u32[]{:S(2)}) %collective-permute-start.7) | collective-permute-done | bytes 2621472 | tf_op jit(solution)/shard_map/ppermute | solution.py:35
  83.1 3.1 %add_convert_fusion.1 = bf16[2560,512]{1,0:T(8,128)(2,1)S(1)} fusion(bf16[2560,512]{1,0:T(8,128)(2,1)S(1)} %collective-permute-done.7, bf16[2560,864]{1,0:T(8,128)(2,1)S(1)} %copy-done, bf16[864,512]{1,0:T(8,128)(2,1)S(1)} %copy-done.13), kind=kOutput, calls=%fused_computation.1 | convolution fusion | flops 2268856320 | bytes 10551296 | tf_op jit(solution)/shard_map/dot_general | solution.py:51
  86.2 1.3 constant_dynamic-slice_fusion.4
  87.6 1.2 collective-permute-start.8
  88.7 2.4 %collective-permute-start.10 = (bf16[640,512]{1,0:T(8,128)(2,1)}, bf16[640,512]{1,0:T(8,128)(2,1)}, u32[]{:S(2)}, u32[]{:S(2)}) collective-permute-start(bf16[640,512]{1,0:T(8,128)(2,1)} %get-tuple-element.31), channel_id=1, source_target_pairs={{0,8},{1,9},{32,40},{33,41},{64,72},{65,73},{96,104},{97,105},{128... | collective-permute-start | bytes 1966088 | tf_op jit(solution)/shard_map/ppermute | solution.py:35
  91.2 1.2 collective-permute-start.9
  92.3 2.5 %fusion.13 = f32[864,512]{1,0:T(8,128)S(1)} fusion(bf16[2560,864]{1,0:T(8,128)(2,1)S(1)} %copy-done, bf16[2560,512]{1,0:T(8,128)(2,1)S(1)} %copy-done.2), kind=kOutput, calls=%fused_computation.39 | convolution fusion | flops 2264924160 | bytes 8814592 | tf_op jit(solution)/shard_map/dot_general | solution.py:51
  94.8 5.2 %select_convert_fusion = (bf16[864,512]{1,0:T(8,128)(2,1)}, f32[864,512]{1,0:T(8,128)S(1)}) fusion(f32[864,512]{1,0:T(8,128)S(1)} %fusion.13, pred[]{:T(512)S(6)} %eq.6, bf16[2560,864]{1,0:T(8,128)(2,1)S(1)} %copy-done, bf16[2560,512]{1,0:T(8,128)(2,1)} %collective-permute-done.13), kind=kOutput, calls=%fused_computation.19 | convolution fusion | flops 2265366528 | bytes 11468801 | tf_op jit(solution)/shard_map/dot_general | solution.py:51
  100.0 2.7 %collective-permute-start.14 = (bf16[864,512]{1,0:T(8,128)(2,1)}, bf16[864,512]{1,0:T(8,128)(2,1)}, u32[]{:S(2)}, u32[]{:S(2)}) collective-permute-start(bf16[864,512]{1,0:T(8,128)(2,1)} %get-tuple-element.37), channel_id=1, source_target_pairs={{0,16},{1,17},{32,48},{33,49},{64,80},{65,81},{96,112},{97,113},{1... | collective-permute-start | bytes 2654216 | tf_op jit(solution)/shard_map/ppermute | solution.py:35
  102.7 2.3 %collective-permute-done.8 = bf16[640,512]{1,0:T(8,128)(2,1)} collective-permute-done((bf16[640,512]{1,0:T(8,128)(2,1)}, bf16[640,512]{1,0:T(8,128)(2,1)}, u32[]{:S(2)}, u32[]{:S(2)}) %collective-permute-start.8) | collective-permute-done | bytes 655392 | tf_op jit(solution)/shard_map/ppermute | solution.py:35
  105.0 15.0 %collective-permute-done.10 = bf16[640,512]{1,0:T(8,128)(2,1)} collective-permute-done((bf16[640,512]{1,0:T(8,128)(2,1)}, bf16[640,512]{1,0:T(8,128)(2,1)}, u32[]{:S(2)}, u32[]{:S(2)}) %collective-permute-start.10) | collective-permute-done | bytes 655392 | tf_op jit(solution)/shard_map/ppermute | solution.py:35
  120.0 2.0 %add_convert_fusion.2 = bf16[640,512]{1,0:T(8,128)(2,1)S(1)} fusion(bf16[640,512]{1,0:T(8,128)(2,1)} %collective-permute-done.10, bf16[640,512]{1,0:T(8,128)(2,1)} %collective-permute-done.9, bf16[640,512]{1,0:T(8,128)(2,1)} %collective-permute-done.8, bf16[2560,512]{1,0:T(8,128)(2,1)} %copy-done.5, u32[]{:T(128)S(6)} %mul.46), kind=kLoop, calls=%fused_computation.20 | loop fusion | flops 2621440 | bytes 3276804 | tf_op jit(solution)/shard_map/convert_element_type | solution.py:43
  122.0 0.9 constant_dynamic-slice_fusion
  122.9 3.6 %collective-permute-start.12 = (bf16[320,512]{1,0:T(8,128)(2,1)}, bf16[320,512]{1,0:T(8,128)(2,1)}, u32[]{:S(2)}, u32[]{:S(2)}) collective-permute-start(bf16[320,512]{1,0:T(8,128)(2,1)} %get-tuple-element.35), channel_id=1, source_target_pairs={{0,2},{1,18},{32,34},{33,50},{64,66},{65,82},{96,98},{97,114},{128... | collective-permute-start | bytes 983048 | tf_op jit(solution)/shard_map/ppermute | solution.py:35
  126.5 2.2 %collective-permute-start.11 = (bf16[320,512]{1,0:T(8,128)(2,1)}, bf16[320,512]{1,0:T(8,128)(2,1)}, u32[]{:S(2)}, u32[]{:S(2)}) collective-permute-start(bf16[320,512]{1,0:T(8,128)(2,1)} %get-tuple-element.36), channel_id=1, source_target_pairs={{0,0},{1,16},{32,32},{33,48},{64,64},{65,80},{96,96},{97,112},{128... | collective-permute-start | bytes 983048 | tf_op jit(solution)/shard_map/ppermute | solution.py:35
  128.7 3.4 %fusion.9 = (bf16[512,864]{0,1:T(8,128)(2,1)}, bf16[512,864]{0,1:T(8,128)(2,1)}) fusion(bf16[512,864]{0,1:T(8,128)(2,1)S(1)} %copy-done.4, bf16[864,512]{1,0:T(8,128)(2,1)} %collective-permute-done.14, f32[864,512]{1,0:T(8,128)S(1)} %fusion.13, f32[864,512]{1,0:T(8,128)S(1)} %get-tuple-element.38, pred[]{:T(512)S(6)} %eq.6, bf16[512,864]{0,1:T(8,128)(2,1)S(1)} %copy-done.3), kind=kLoop, calls=%fused_computation.21 | loop fusion | flops 7962624 | bytes 7962625 | tf_op jit(solution)/shard_map/transpose | solution.py:126
  132.1 0.3 reduce-scatter.2.cloned.1.call-done
  132.4 2.1 %convert_element_type.92 = f32[320,864]{1,0:T(8,128)} convert(bf16[320,864]{1,0:T(8,128)(2,1)} %reduce-scatter.2.cloned.1.call-done) | non-fusion elementwise | flops 276480 | bytes 1658880 | tf_op jit(solution)/shard_map/convert_element_type | solution.py:39
  134.6 2.1 %collective-permute-done.11 = bf16[320,512]{1,0:T(8,128)(2,1)} collective-permute-done((bf16[320,512]{1,0:T(8,128)(2,1)}, bf16[320,512]{1,0:T(8,128)(2,1)}, u32[]{:S(2)}, u32[]{:S(2)}) %collective-permute-start.11) | collective-permute-done | bytes 327712 | tf_op jit(solution)/shard_map/ppermute | solution.py:35
  136.7 1.9 %fusion.11 = bf16[512,320]{0,1:T(8,128)(2,1)} fusion(bf16[320,512]{1,0:T(8,128)(2,1)} %collective-permute-done.12, bf16[320,512]{1,0:T(8,128)(2,1)} %collective-permute-done.11), kind=kLoop, calls=%fused_computation.27 | loop fusion | flops 655360 | bytes 983040 | tf_op jit(solution)/shard_map/transpose | solution.py:118
  (43 shorter events, 0.4 us)
Async XLA Ops:
  7.2 65.0 %all-gather.2.cloned.1.call-start = ((), (), s32[]{:S(2)}) async-start(), calls=%async_computation.1 | async-start | bytes 5160960 | tf_op jit(solution)/shard_map/all_gather | solution.py:73
  7.9 124.5 %reduce-scatter.2.cloned.1.call-start = ((), (), s32[]{:S(2)}) async-start(), calls=%async_computation.2 | async-start | bytes 5160960 | tf_op jit(solution)/shard_map/reduce_scatter | solution.py:103
  7.9 9.6 %collective-permute-start.1 = (bf16[320,512]{1,0:T(8,128)(2,1)}, bf16[320,512]{1,0:T(8,128)(2,1)S(1)}, u32[]{:S(2)}, u32[]{:S(2)}) collective-permute-start(bf16[320,512]{1,0:T(8,128)(2,1)} %bitcast.66), channel_id=1, source_target_pairs={{0,2},{1,18},{32,34},{33,50},{64,66},{65,82},{96,98},{97,114},{128... | collective-permute-start | bytes 983048 | tf_op jit(solution)/shard_map/ppermute | solution.py:35
  12.2 10.1 %collective-permute-start = (bf16[320,512]{1,0:T(8,128)(2,1)}, bf16[320,512]{1,0:T(8,128)(2,1)S(1)}, u32[]{:S(2)}, u32[]{:S(2)}) collective-permute-start(bf16[320,512]{1,0:T(8,128)(2,1)} %bitcast.67), channel_id=1, source_target_pairs={{0,0},{1,16},{32,32},{33,48},{64,64},{65,80},{96,96},{97,112},{128... | collective-permute-start | bytes 983048 | tf_op jit(solution)/shard_map/ppermute | solution.py:35
  22.4 17.1 %copy-start.6 = (bf16[2,320,512]{2,1,0:T(8,128)(2,1)}, bf16[2,320,512]{2,1,0:T(8,128)(2,1)S(1)}, u32[]{:S(2)}) copy-start(bf16[2,320,512]{2,1,0:T(8,128)(2,1)S(1)} %maximum_select_fusion) | copy-start | bytes 1966084
  22.4 15.7 %collective-permute-start.3 = (bf16[640,512]{1,0:T(8,128)(2,1)S(1)}, bf16[640,512]{1,0:T(8,128)(2,1)S(1)}, u32[]{:S(2)}, u32[]{:S(2)}) collective-permute-start(bf16[640,512]{1,0:T(8,128)(2,1)S(1)} %bitcast.61), channel_id=1, source_target_pairs={{0,12},{1,13},{32,44},{33,45},{64,76},{65,77},{96,108},{97,109},{1... | collective-permute-start | bytes 1966088 | tf_op jit(solution)/shard_map/ppermute | solution.py:35
  24.9 14.5 %collective-permute-start.2 = (bf16[640,512]{1,0:T(8,128)(2,1)S(1)}, bf16[640,512]{1,0:T(8,128)(2,1)S(1)}, u32[]{:S(2)}, u32[]{:S(2)}) collective-permute-start(bf16[640,512]{1,0:T(8,128)(2,1)S(1)} %bitcast.62), channel_id=1, source_target_pairs={{0,4},{1,5},{32,36},{33,37},{64,68},{65,69},{96,100},{97,101},{128... | collective-permute-start | bytes 1966088 | tf_op jit(solution)/shard_map/ppermute | solution.py:35
  24.9 21.4 %collective-permute-start.6 = (bf16[864,512]{1,0:T(8,128)(2,1)S(1)}, bf16[864,512]{1,0:T(8,128)(2,1)}, u32[]{:S(2)}, u32[]{:S(2)}) collective-permute-start(bf16[864,512]{1,0:T(8,128)(2,1)S(1)} %fusion.1), channel_id=1, source_target_pairs={{0,16},{1,17},{32,48},{33,49},{64,80},{65,81},{96,112},{97,113},{1... | collective-permute-start | bytes 2654216 | tf_op jit(solution)/shard_map/ppermute | solution.py:35
  38.1 1.3 copy-start.8
  38.1 9.4 %collective-permute-start.5 = (bf16[320,512]{1,0:T(8,128)(2,1)S(1)}, bf16[320,512]{1,0:T(8,128)(2,1)S(1)}, u32[]{:S(2)}, u32[]{:S(2)}) collective-permute-start(bf16[320,512]{1,0:T(8,128)(2,1)S(1)} %slice.10), channel_id=1, source_target_pairs={{0,12},{1,13},{32,44},{33,45},{64,76},{65,77},{96,108},{97,109},{1... | collective-permute-start | bytes 983048 | tf_op jit(solution)/shard_map/ppermute | solution.py:35
  39.4 0.8 copy-start.10
  40.2 9.5 %collective-permute-start.4 = (bf16[320,512]{1,0:T(8,128)(2,1)S(1)}, bf16[320,512]{1,0:T(8,128)(2,1)S(1)}, u32[]{:S(2)}, u32[]{:S(2)}) collective-permute-start(bf16[320,512]{1,0:T(8,128)(2,1)S(1)} %slice.9), channel_id=1, source_target_pairs={{0,4},{1,5},{32,36},{33,37},{64,68},{65,69},{96,100},{97,101},{128... | collective-permute-start | bytes 983048 | tf_op jit(solution)/shard_map/ppermute | solution.py:35
  40.7 1.1 copy-start.7
  40.7 1.3 copy-start.11
  40.7 1.5 %copy-start.9 = (bf16[640,512]{1,0:T(8,128)(2,1)S(1)}, bf16[640,512]{1,0:T(8,128)(2,1)}, u32[]{:S(2)}) copy-start(bf16[640,512]{1,0:T(8,128)(2,1)} %copy-done.8) | copy-start | bytes 1966084
  49.7 9.8 %copy-start.1 = (bf16[2560,512]{1,0:T(8,128)(2,1)}, bf16[2560,512]{1,0:T(8,128)(2,1)S(1)}, u32[]{:S(2)}) copy-start(bf16[2560,512]{1,0:T(8,128)(2,1)S(1)} %constant_dynamic-update-slice_fusion) | copy-start | bytes 7864324
  49.8 5.1 %collective-permute-start.13 = (bf16[2560,512]{1,0:T(8,128)(2,1)S(1)}, bf16[2560,512]{1,0:T(8,128)(2,1)}, u32[]{:S(2)}, u32[]{:S(2)}) collective-permute-start(bf16[2560,512]{1,0:T(8,128)(2,1)S(1)} %constant_dynamic-update-slice_fusion), channel_id=1, source_target_pairs={{0,1},{1,0},{32,33},{33,32},{64,65},{65,64},{96,97},{97,96},{128,1... | collective-permute-start | bytes 7864328 | tf_op jit(solution)/shard_map/ppermute | solution.py:35
  51.8 3.1 %copy-start.14 = (bf16[864,512]{1,0:T(8,128)(2,1)}, bf16[864,512]{1,0:T(8,128)(2,1)S(1)}, u32[]{:S(2)}) copy-start(bf16[864,512]{1,0:T(8,128)(2,1)S(1)} %get-tuple-element.18) | copy-start | bytes 2654212
  51.9 7.8 %copy-start.12 = (bf16[864,512]{1,0:T(8,128)(2,1)}, bf16[864,512]{1,0:T(8,128)(2,1)S(1)}, u32[]{:S(2)}) copy-start(bf16[864,512]{1,0:T(8,128)(2,1)S(1)} %get-tuple-element.20) | copy-start | bytes 2654212
  64.2 7.9 %copy-start.15 = (bf16[864,512]{1,0:T(8,128)(2,1)S(1)}, bf16[864,512]{1,0:T(8,128)(2,1)}, u32[]{:S(2)}) copy-start(bf16[864,512]{1,0:T(8,128)(2,1)} %copy-done.14) | copy-start | bytes 2654212
  64.2 18.9 %copy-start.13 = (bf16[864,512]{1,0:T(8,128)(2,1)S(1)}, bf16[864,512]{1,0:T(8,128)(2,1)}, u32[]{:S(2)}) copy-start(bf16[864,512]{1,0:T(8,128)(2,1)} %copy-done.12) | copy-start | bytes 2654212
  72.1 11.0 %copy-start = (bf16[2560,864]{1,0:T(8,128)(2,1)S(1)}, bf16[2560,864]{1,0:T(8,128)(2,1)}, u32[]{:S(2)}) copy-start(bf16[2560,864]{1,0:T(8,128)(2,1)} %all-gather.2.cloned.1.call-done) | copy-start | bytes 13271044
  77.7 5.5 %collective-permute-start.7 = (bf16[2560,512]{1,0:T(8,128)(2,1)S(1)}, bf16[2560,512]{1,0:T(8,128)(2,1)S(1)}, u32[]{:S(2)}, u32[]{:S(2)}) collective-permute-start(bf16[2560,512]{1,0:T(8,128)(2,1)S(1)} %fusion), channel_id=1, source_target_pairs={{0,1},{1,0},{32,33},{33,32},{64,65},{65,64},{96,97},{97,96},{128,1... | collective-permute-start | bytes 7864328 | tf_op jit(solution)/shard_map/ppermute | solution.py:35
  86.2 8.6 %copy-start.5 = (bf16[2560,512]{1,0:T(8,128)(2,1)}, bf16[2560,512]{1,0:T(8,128)(2,1)S(1)}, u32[]{:S(2)}) copy-start(bf16[2560,512]{1,0:T(8,128)(2,1)S(1)} %add_convert_fusion.1) | copy-start | bytes 7864324
  86.2 6.1 %copy-start.2 = (bf16[2560,512]{1,0:T(8,128)(2,1)S(1)}, bf16[2560,512]{1,0:T(8,128)(2,1)}, u32[]{:S(2)}) copy-start(bf16[2560,512]{1,0:T(8,128)(2,1)} %copy-done.1) | copy-start | bytes 7864324
  87.6 17.5 %collective-permute-start.8 = (bf16[640,512]{1,0:T(8,128)(2,1)}, bf16[640,512]{1,0:T(8,128)(2,1)}, u32[]{:S(2)}, u32[]{:S(2)}) collective-permute-start(bf16[640,512]{1,0:T(8,128)(2,1)} %get-tuple-element.30), channel_id=1, source_target_pairs={{0,4},{1,5},{32,36},{33,37},{64,68},{65,69},{96,100},{97,101},{128... | collective-permute-start | bytes 1966088 | tf_op jit(solution)/shard_map/ppermute | solution.py:35
  88.7 31.2 %collective-permute-start.10 = (bf16[640,512]{1,0:T(8,128)(2,1)}, bf16[640,512]{1,0:T(8,128)(2,1)}, u32[]{:S(2)}, u32[]{:S(2)}) collective-permute-start(bf16[640,512]{1,0:T(8,128)(2,1)} %get-tuple-element.31), channel_id=1, source_target_pairs={{0,8},{1,9},{32,40},{33,41},{64,72},{65,73},{96,104},{97,105},{128... | collective-permute-start | bytes 1966088 | tf_op jit(solution)/shard_map/ppermute | solution.py:35
  91.2 28.8 %collective-permute-start.9 = (bf16[640,512]{1,0:T(8,128)(2,1)}, bf16[640,512]{1,0:T(8,128)(2,1)}, u32[]{:S(2)}, u32[]{:S(2)}) collective-permute-start(bf16[640,512]{1,0:T(8,128)(2,1)} %get-tuple-element.32), channel_id=1, source_target_pairs={{0,12},{1,13},{32,44},{33,45},{64,76},{65,77},{96,108},{97,109},{1... | collective-permute-start | bytes 1966088 | tf_op jit(solution)/shard_map/ppermute | solution.py:35
  100.0 28.7 %collective-permute-start.14 = (bf16[864,512]{1,0:T(8,128)(2,1)}, bf16[864,512]{1,0:T(8,128)(2,1)}, u32[]{:S(2)}, u32[]{:S(2)}) collective-permute-start(bf16[864,512]{1,0:T(8,128)(2,1)} %get-tuple-element.37), channel_id=1, source_target_pairs={{0,16},{1,17},{32,48},{33,49},{64,80},{65,81},{96,112},{97,113},{1... | collective-permute-start | bytes 2654216 | tf_op jit(solution)/shard_map/ppermute | solution.py:35
  102.7 25.9 %copy-start.3 = (bf16[512,864]{0,1:T(8,128)(2,1)S(1)}, bf16[512,864]{0,1:T(8,128)(2,1)}, u32[]{:S(2)}) copy-start(bf16[512,864]{0,1:T(8,128)(2,1)} %param.5) | copy-start | bytes 2654212
  102.7 25.9 %copy-start.4 = (bf16[512,864]{0,1:T(8,128)(2,1)S(1)}, bf16[512,864]{0,1:T(8,128)(2,1)}, u32[]{:S(2)}) copy-start(bf16[512,864]{0,1:T(8,128)(2,1)} %param.4) | copy-start | bytes 2654212
  122.9 11.6 %collective-permute-start.12 = (bf16[320,512]{1,0:T(8,128)(2,1)}, bf16[320,512]{1,0:T(8,128)(2,1)}, u32[]{:S(2)}, u32[]{:S(2)}) collective-permute-start(bf16[320,512]{1,0:T(8,128)(2,1)} %get-tuple-element.35), channel_id=1, source_target_pairs={{0,2},{1,18},{32,34},{33,50},{64,66},{65,82},{96,98},{97,114},{128... | collective-permute-start | bytes 983048 | tf_op jit(solution)/shard_map/ppermute | solution.py:35
  126.5 10.2 %collective-permute-start.11 = (bf16[320,512]{1,0:T(8,128)(2,1)}, bf16[320,512]{1,0:T(8,128)(2,1)}, u32[]{:S(2)}, u32[]{:S(2)}) collective-permute-start(bf16[320,512]{1,0:T(8,128)(2,1)} %get-tuple-element.36), channel_id=1, source_target_pairs={{0,0},{1,16},{32,32},{33,48},{64,64},{65,80},{96,96},{97,112},{128... | collective-permute-start | bytes 983048 | tf_op jit(solution)/shard_map/ppermute | solution.py:35
Sparse Core Ops, SparseCore 0:
  9.8 62.2 all-gather.1
  74.7 57.6 reduce-scatter.1

commit v4 on v3

--- a/solution.py
+++ b/solution.py
@@ -102,26 +102,40 @@
     grad_down = f32(
         lax.psum_scatter(grad, "blk", axis_index_groups=PLANES, scatter_dimension=0, tiled=True)
     )
-    weight = first(weight, grad[:8, :128])
+    cot_keep, cot_away = jnp.where(same, cot_a, cot_b), jnp.where(same, cot_b, cot_a)
+    cot_keep, cot_away = lax.optimization_barrier((cot_keep, cot_away, grad[:8, :128]))[:2]
+    weight = first(weight, cot_keep, cot_away)
 
     part_b = row_major(bf16(dot(weight, hid_b, ((1,), (0,)))))
     got = send(part_b, SIBLING)
     weight = first(weight, part_b)
     part_a = row_major(bf16(dot(weight, hid_a, ((1,), (0,))) + f32(got)))
-    total = f32(rows_of(part_a, x_rows(0), 640))
-    for d, pairs in ((1, X_UP), (3, X_DOWN), (2, X_FAR)):
-        total = total + f32(send(rows_of(part_a, x_rows(d), 640), pairs))
-    total = bf16(total)
-    keep, give = rows_of(total, lo * 320, 320), rows_of(total, (1 - lo) * 320, 320)
+    def cut(step, row):
+        return rows_of(part_a, x_rows(step) + row, 320)
+
+    slices = (cut(2, 0), cut(2, 320), cut(1, 320), cut(3, 0), cut(1, 0), cut(3, 320))
+    far_l, far_r, plain_l, plain_r, joint_l, joint_r = lax.optimization_barrier(slices)
+    weight = first(weight, far_l, far_r, plain_l, plain_r, joint_l, joint_r)
+    far_l, far_r = send(far_l, X_UP), send(far_r, X_DOWN)
+    plain_l, plain_r = send(plain_l, X_UP), send(plain_r, X_DOWN)
+
+    away = bf16(dot(weight, cot_away, ((0,), (0,))))
+    far_l, far_r, away = lax.optimization_barrier((far_l, far_r, away))
+    joint_l, joint_r = bf16(f32(joint_l) + f32(far_l)), bf16(f32(joint_r) + f32(far_r))
+    joint_l, joint_r, weight = lax.optimization_barrier((joint_l, joint_r, weight))
+    keep_dh = dot(weight, cot_keep, ((0,), (0,)))
+    joint_l, joint_r = send(joint_l, X_UP), send(joint_r, X_DOWN)
+    joint_l, joint_r, plain_l, plain_r, keep_dh = lax.optimization_barrier((joint_l, joint_r, plain_l, plain_r, keep_dh))
+
+    def block(lower):
+        left, right = jnp.where(lower, joint_l, plain_l), jnp.where(lower, plain_r, joint_r)
+        return bf16(f32(cut(0, jnp.where(lower, zero, jnp.uint32(320)))) + f32(left) + f32(right))
+
+    keep, give = block(lo == 0), block(lo == 1)
     keep, give = send(keep, TURN), send(give, TURN_LO)
-    keep, give, grad_down = lax.optimization_barrier((keep, give, grad_down))
     mixed = bf16(f32(keep) + f32(give)).T
 
-    weight = first(weight, part_a)
-    dh_a = dot(weight, cot_a, ((0,), (0,)))
-    dh_b = dot(weight, cot_b, ((0,), (0,)))
-    away = send(bf16(jnp.where(same, dh_b, dh_a)), PARTNER)
-    d_hidden = jnp.where(same, dh_a, dh_b) + f32(away)
+    d_hidden = keep_dh + f32(send(away, PARTNER))
     d_gate = bf16(d_hidden * up * sig * (1.0 + gate * (1.0 - sig))).T
     d_up = bf16(d_hidden * act).T
     return (mixed, d_gate, d_up, grad_down)

time: 146 us -> 150 us (1.027)
  starting transfers between devices: 24.7 us -> 29.7 us
  local copies, waits for them, and re-layouts: 4.66 us -> 2.72 us
    ppermute x15 -> x18, waiting for transfers between devices: 53.8 us -> 61.8 us  [send(): return lax.ppermute(value, AXES, pairs)]
    all_gather x1, waiting for transfers between devices: 7.9 us -> 0.01 us  [body(): lax.all_gather(down_weight, 'blk', axis_index_groups=PLANES, axis=0, tile...]
    ppermute x15 -> x18, starting transfers between devices: 24.6 us -> 29.6 us  [send(): return lax.ppermute(value, AXES, pairs)]
    select_n x0 -> x1, other arithmetic: none -> 4.54 us  [body(): jnp.where(same, cot_b, cot_a)]
    dynamic_slice x2 -> x1, local copies, waits for them, and re-layouts: 2.2 us -> 0.14 us  [rows_of(): return lax.dynamic_slice(whole, (row, zero), (count, whole.shape[1]))]
    convert_element_type x2 -> x3, other arithmetic: 4.03 us -> 2.5 us  [bf16(): return value.astype(jnp.bfloat16)]
  transfers between devices with their start and end apart: 17 -> 20, of which waited for: 14 -> 12; matrix products, arithmetic and copies ran while one was open for 27% -> 26% of each run, Pallas kernels for 0% -> 0%
where the time goes in v4:
time: 150 us
  waiting for transfers between devices  62.5 us (42%)
  starting transfers between devices  29.7 us (20%)
  matrix products  26.7 us (18%)
  between operations  14.3 us (10%)
  other arithmetic  13.6 us (9%)
  local copies, waits for them, and re-layouts  2.72 us (2%)
    ppermute x18, waiting for transfers between devices, send(): return lax.ppermute(value, AXES, pairs)  61.8 us
    ppermute x18, starting transfers between devices, send(): return lax.ppermute(value, AXES, pairs)  29.6 us
    dot_general x6, matrix products, dot(): lax.dot_general(left, right, ((dims[0], dims[1]), ((), ())), preferred_el...  26.7 us
    select_n x1, other arithmetic, body(): jnp.where(same, cot_b, cot_a)  4.54 us
  transfers between devices with their start and end apart: 20, of which 12 were waited for; matrix products, arithmetic and copies ran while one was open for 26% of the time, Pallas kernels for 0%

profile of v4, /device:TPU:1, one launch (start us, length us, event | category | flops | bytes accessed | tf_op | source)
XLA Modules:
  0.0 149.6 jit_solution(10215179328025308161)
XLA Ops:
  7.2 0.7 all-gather.2.cloned.1.call-update
  7.9 6.2 %collective-permute-start = (bf16[320,512]{1,0:T(8,128)(2,1)}, bf16[320,512]{1,0:T(8,128)(2,1)S(1)}, u32[]{:S(2)}, u32[]{:S(2)}) collective-permute-start(bf16[320,512]{1,0:T(8,128)(2,1)} %bitcast.66), channel_id=1, source_target_pairs={{0,0},{1,16},{32,32},{33,48},{64,64},{65,80},{96,96},{97,112},{128... | collective-permute-start | bytes 983048 | tf_op jit(solution)/shard_map/ppermute | solution.py:35
  14.2 0.6 collective-permute-start.1
  14.7 2.0 %fusion = bf16[864,512]{1,0:T(8,128)(2,1)S(1)} fusion(bf16[512,864]{0,1:T(8,128)(2,1)} %param.5, bf16[512,864]{0,1:T(8,128)(2,1)} %param.4), kind=kLoop, calls=%fused_computation.7 | loop fusion | flops 3538944 | bytes 2654208 | tf_op jit(solution)/shard_map/convert_element_type | solution.py:43
  16.7 5.9 %collective-permute-done = bf16[320,512]{1,0:T(8,128)(2,1)S(1)} collective-permute-done((bf16[320,512]{1,0:T(8,128)(2,1)}, bf16[320,512]{1,0:T(8,128)(2,1)S(1)}, u32[]{:S(2)}, u32[]{:S(2)}) %collective-permute-start) | collective-permute-done | bytes 327712 | tf_op jit(solution)/shard_map/ppermute | solution.py:35
  22.6 1.5 %collective-permute-done.1 = bf16[320,512]{1,0:T(8,128)(2,1)S(1)} collective-permute-done((bf16[320,512]{1,0:T(8,128)(2,1)}, bf16[320,512]{1,0:T(8,128)(2,1)S(1)}, u32[]{:S(2)}, u32[]{:S(2)}) %collective-permute-start.1) | collective-permute-done | bytes 327712 | tf_op jit(solution)/shard_map/ppermute | solution.py:35
  24.2 0.1 maximum_select_fusion
  24.3 1.3 collective-permute-start.2
  25.6 1.5 collective-permute-start.3
  27.0 15.1 %collective-permute-done.2 = bf16[640,512]{1,0:T(8,128)(2,1)S(1)} collective-permute-done((bf16[640,512]{1,0:T(8,128)(2,1)S(1)}, bf16[640,512]{1,0:T(8,128)(2,1)S(1)}, u32[]{:S(2)}, u32[]{:S(2)}) %collective-permute-start.2) | collective-permute-done | bytes 655392 | tf_op jit(solution)/shard_map/ppermute | solution.py:35
  42.3 0.7 copy-done.6
  43.0 0.2 copy-done.8
  43.2 2.7 %collective-permute-start.5 = (bf16[320,512]{1,0:T(8,128)(2,1)S(1)}, bf16[320,512]{1,0:T(8,128)(2,1)S(1)}, u32[]{:S(2)}, u32[]{:S(2)}) collective-permute-start(bf16[320,512]{1,0:T(8,128)(2,1)S(1)} %slice.10), channel_id=1, source_target_pairs={{0,12},{1,13},{32,44},{33,45},{64,76},{65,77},{96,108},{97,109},{1... | collective-permute-start | bytes 983048 | tf_op jit(solution)/shard_map/ppermute | solution.py:35
  45.9 0.2 broadcast_in_dim.3
  46.1 0.9 copy-done.4
  47.1 0.2 copy-done.7
  47.3 0.2 copy-done.9
  47.5 2.5 %collective-permute-done.6 = bf16[864,512]{1,0:T(8,128)(2,1)} collective-permute-done((bf16[864,512]{1,0:T(8,128)(2,1)S(1)}, bf16[864,512]{1,0:T(8,128)(2,1)}, u32[]{:S(2)}, u32[]{:S(2)}) %collective-permute-start.6) | collective-permute-done | bytes 884768 | tf_op jit(solution)/shard_map/ppermute | solution.py:35
  50.0 2.9 %collective-permute-done.4 = bf16[320,512]{1,0:T(8,128)(2,1)S(1)} collective-permute-done((bf16[320,512]{1,0:T(8,128)(2,1)S(1)}, bf16[320,512]{1,0:T(8,128)(2,1)S(1)}, u32[]{:S(2)}, u32[]{:S(2)}) %collective-permute-start.4) | collective-permute-done | bytes 327712 | tf_op jit(solution)/shard_map/ppermute | solution.py:35
  53.0 1.2 collective-permute-start.7
  54.2 1.3 broadcast_select_fusion.2
  55.5 3.3 %collective-permute-done.7 = bf16[2560,512]{1,0:T(8,128)(2,1)} collective-permute-done((bf16[2560,512]{1,0:T(8,128)(2,1)S(1)}, bf16[2560,512]{1,0:T(8,128)(2,1)}, u32[]{:S(2)}, u32[]{:S(2)}) %collective-permute-start.7) | collective-permute-done | bytes 2621472 | tf_op jit(solution)/shard_map/ppermute | solution.py:35
  58.9 4.7 %fusion.12 = f32[2560,864]{1,0:T(8,128)S(1)} fusion(bf16[2560,512]{1,0:T(8,128)(2,1)} %collective-permute-done.7, bf16[864,512]{1,0:T(8,128)(2,1)S(1)} %get-tuple-element.41), kind=kOutput, calls=%fused_computation.44 | convolution fusion | flops 2264924160 | bytes 12353536 | tf_op jit(solution)/shard_map/dot_general | solution.py:51
  63.5 4.6 %add_convert_fusion = bf16[2560,864]{1,0:T(8,128)(2,1)} fusion(f32[2560,864]{1,0:T(8,128)S(1)} %fusion.12, bf16[2560,512]{1,0:T(8,128)(2,1)S(1)} %constant_dynamic-update-slice_fusion, bf16[864,512]{1,0:T(8,128)(2,1)S(1)} %get-tuple-element.43), kind=kOutput, calls=%fused_computation | convolution fusion | flops 2269347840 | bytes 16777216 | tf_op jit(solution)/shard_map/dot_general | solution.py:51
  68.2 4.5 %broadcast_select_fusion = (bf16[2560,512]{1,0:T(8,128)(2,1)}, bf16[2560,512]{1,0:T(8,128)(2,1)}) fusion(bf16[2560,512]{1,0:T(8,128)(2,1)} %collective-permute-done.7, bf16[2560,512]{1,0:T(8,128)(2,1)S(1)} %constant_dynamic-update-slice_fusion, pred[]{:T(512)S(6)} %eq.10), kind=kLoop, calls=%fused_computation.3 | loop fusion | flops 2621440 | bytes 10485761 | tf_op jit(solution)/shard_map/jit(_where)/select_n | solution.py:105
  72.7 6.6 %convolution_convert_fusion = bf16[2560,512]{1,0:T(8,128)(2,1)} fusion(bf16[2560,864]{1,0:T(8,128)(2,1)} %all-gather.2.cloned.1.call-done, bf16[864,512]{1,0:T(8,128)(2,1)S(1)} %copy-done.13), kind=kOutput, calls=%fused_computation.2 | convolution fusion | flops 2266234880 | bytes 7929856 | tf_op jit(solution)/shard_map/dot_general | solution.py:51
  79.3 0.4 collective-permute-start.8
  79.7 4.9 %collective-permute-done.8 = bf16[2560,512]{1,0:T(8,128)(2,1)} collective-permute-done((bf16[2560,512]{1,0:T(8,128)(2,1)}, bf16[2560,512]{1,0:T(8,128)(2,1)}, u32[]{:S(2)}, u32[]{:S(2)}) %collective-permute-start.8) | collective-permute-done | bytes 2621472 | tf_op jit(solution)/shard_map/ppermute | solution.py:35
  84.6 5.9 %add_convert_fusion.1 = bf16[2560,512]{1,0:T(8,128)(2,1)S(1)} fusion(bf16[2560,512]{1,0:T(8,128)(2,1)} %collective-permute-done.8, bf16[2560,864]{1,0:T(8,128)(2,1)} %all-gather.2.cloned.1.call-done, bf16[864,512]{1,0:T(8,128)(2,1)S(1)} %copy-done.11), kind=kOutput, calls=%fused_computation.1 | convolution fusion | flops 2268856320 | bytes 10551296 | tf_op jit(solution)/shard_map/dot_general | solution.py:51
  90.5 0.1 constant_dynamic-slice_fusion
  90.7 3.4 %collective-permute-start.10 = (bf16[320,512]{1,0:T(8,128)(2,1)S(1)}, bf16[320,512]{1,0:T(8,128)(2,1)S(1)}, u32[]{:S(2)}, u32[]{:S(2)}) collective-permute-start(bf16[320,512]{1,0:T(8,128)(2,1)S(1)} %get-tuple-element.46), channel_id=1, source_target_pairs={{0,12},{1,13},{32,44},{33,45},{64,76},{65,77},{96,108},{97,109},{1... | collective-permute-start | bytes 983048 | tf_op jit(solution)/shard_map/ppermute | solution.py:35
  94.1 2.7 %collective-permute-start.14 = (bf16[320,512]{1,0:T(8,128)(2,1)S(1)}, bf16[320,512]{1,0:T(8,128)(2,1)S(1)}, u32[]{:S(2)}, u32[]{:S(2)}) collective-permute-start(bf16[320,512]{1,0:T(8,128)(2,1)S(1)} %get-tuple-element.48), channel_id=1, source_target_pairs={{0,12},{1,13},{32,44},{33,45},{64,76},{65,77},{96,108},{97,109},{1... | collective-permute-start | bytes 983048 | tf_op jit(solution)/shard_map/ppermute | solution.py:35
  96.8 2.5 %convolution_convert_fusion.1 = bf16[864,512]{1,0:T(8,128)(2,1)S(1)} fusion(bf16[2560,864]{1,0:T(8,128)(2,1)S(1)} %bitcast.60, bf16[2560,512]{1,0:T(8,128)(2,1)S(1)} %copy-done.5), kind=kOutput, calls=%fused_computation.20 | convolution fusion | flops 2265366528 | bytes 7929856 | tf_op jit(solution)/shard_map/dot_general | solution.py:51
  99.3 1.5 %collective-permute-done.10 = bf16[320,512]{1,0:T(8,128)(2,1)S(1)} collective-permute-done((bf16[320,512]{1,0:T(8,128)(2,1)S(1)}, bf16[320,512]{1,0:T(8,128)(2,1)S(1)}, u32[]{:S(2)}, u32[]{:S(2)}) %collective-permute-start.10) | collective-permute-done | bytes 327712 | tf_op jit(solution)/shard_map/ppermute | solution.py:35
  100.8 3.2 %collective-permute-done.9 = bf16[320,512]{1,0:T(8,128)(2,1)S(1)} collective-permute-done((bf16[320,512]{1,0:T(8,128)(2,1)S(1)}, bf16[320,512]{1,0:T(8,128)(2,1)S(1)}, u32[]{:S(2)}, u32[]{:S(2)}) %collective-permute-start.9) | collective-permute-done | bytes 327712 | tf_op jit(solution)/shard_map/ppermute | solution.py:35
  104.0 0.2 add_convert_fusion.5
  104.3 2.7 %collective-permute-start.12 = (bf16[320,512]{1,0:T(8,128)(2,1)S(1)}, bf16[320,512]{1,0:T(8,128)(2,1)S(1)}, u32[]{:S(2)}, u32[]{:S(2)}) collective-permute-start(bf16[320,512]{1,0:T(8,128)(2,1)S(1)} %get-tuple-element.54), channel_id=1, source_target_pairs={{0,12},{1,13},{32,44},{33,45},{64,76},{65,77},{96,108},{97,109},{1... | collective-permute-start | bytes 983048 | tf_op jit(solution)/shard_map/ppermute | solution.py:35
  106.9 1.7 %collective-permute-start.17 = (bf16[864,512]{1,0:T(8,128)(2,1)S(1)}, bf16[864,512]{1,0:T(8,128)(2,1)S(1)}, u32[]{:S(2)}, u32[]{:S(2)}) collective-permute-start(bf16[864,512]{1,0:T(8,128)(2,1)S(1)} %convolution_convert_fusion.1), channel_id=1, source_target_pairs={{0,16},{1,17},{32,48},{33,49},{64,80},{65,81},{96,112},{97,113},{1... | collective-permute-start | bytes 2654216 | tf_op jit(solution)/shard_map/ppermute | solution.py:35
  108.7 2.5 %fusion.11 = f32[864,512]{1,0:T(8,128)S(1)} fusion(bf16[2560,864]{1,0:T(8,128)(2,1)S(1)} %bitcast.60, bf16[2560,512]{1,0:T(8,128)(2,1)S(1)} %copy-done), kind=kOutput, calls=%fused_computation.43 | convolution fusion | flops 2264924160 | bytes 8814592 | tf_op jit(solution)/shard_map/dot_general | solution.py:51
  111.2 6.8 %collective-permute-done.11 = bf16[320,512]{1,0:T(8,128)(2,1)S(1)} collective-permute-done((bf16[320,512]{1,0:T(8,128)(2,1)S(1)}, bf16[320,512]{1,0:T(8,128)(2,1)S(1)}, u32[]{:S(2)}, u32[]{:S(2)}) %collective-permute-start.11) | collective-permute-done | bytes 327712 | tf_op jit(solution)/shard_map/ppermute | solution.py:35
  118.0 0.3 add_convert_fusion.4
  118.4 4.9 %collective-permute-start.15 = (bf16[320,512]{1,0:T(8,128)(2,1)S(1)}, bf16[320,512]{1,0:T(8,128)(2,1)S(1)}, u32[]{:S(2)}, u32[]{:S(2)}) collective-permute-start(bf16[320,512]{1,0:T(8,128)(2,1)S(1)} %get-tuple-element.64), channel_id=1, source_target_pairs={{0,0},{1,16},{32,32},{33,48},{64,64},{65,80},{96,96},{97,112},{128... | collective-permute-start | bytes 983048 | tf_op jit(solution)/shard_map/ppermute | solution.py:35
  123.3 0.1 collective-permute-start.16
  123.4 13.5 %collective-permute-done.15 = bf16[320,512]{1,0:T(8,128)(2,1)S(1)} collective-permute-done((bf16[320,512]{1,0:T(8,128)(2,1)S(1)}, bf16[320,512]{1,0:T(8,128)(2,1)S(1)}, u32[]{:S(2)}, u32[]{:S(2)}) %collective-permute-start.15) | collective-permute-done | bytes 327712 | tf_op jit(solution)/shard_map/ppermute | solution.py:35
  136.9 0.6 collective-permute-done.16
  137.5 0.8 fusion.10
  138.4 2.2 %fusion.8 = (bf16[512,864]{0,1:T(8,128)(2,1)}, bf16[512,864]{0,1:T(8,128)(2,1)}) fusion(f32[864,512]{1,0:T(8,128)S(1)} %fusion.11, bf16[864,512]{1,0:T(8,128)(2,1)S(1)} %collective-permute-done.17, bf16[512,864]{0,1:T(8,128)(2,1)S(1)} %copy-done.2, bf16[512,864]{0,1:T(8,128)(2,1)S(1)} %copy-done.1), kind=kLoop, calls=%fused_computation.21 | loop fusion | flops 7520256 | bytes 6193152 | tf_op jit(solution)/shard_map/transpose | solution.py:140
  140.6 2.1 %convert_element_type.131 = f32[320,864]{1,0:T(8,128)} convert(bf16[320,864]{1,0:T(8,128)(2,1)} %reduce-scatter.2.cloned.1.call-done) | non-fusion elementwise | flops 276480 | bytes 1658880 | tf_op jit(solution)/shard_map/convert_element_type | solution.py:39
  (51 shorter events, 0.6 us)
Async XLA Ops:
  7.2 65.6 %all-gather.2.cloned.1.call-start = ((), (), s32[]{:S(2)}) async-start(), calls=%async_computation.1 | async-start | bytes 5160960 | tf_op jit(solution)/shard_map/all_gather | solution.py:73
  7.9 132.7 %reduce-scatter.2.cloned.1.call-start = ((), (), s32[]{:S(2)}) async-start(), calls=%async_computation.2 | async-start | bytes 5160960 | tf_op jit(solution)/shard_map/reduce_scatter | solution.py:103
  7.9 14.7 %collective-permute-start = (bf16[320,512]{1,0:T(8,128)(2,1)}, bf16[320,512]{1,0:T(8,128)(2,1)S(1)}, u32[]{:S(2)}, u32[]{:S(2)}) collective-permute-start(bf16[320,512]{1,0:T(8,128)(2,1)} %bitcast.66), channel_id=1, source_target_pairs={{0,0},{1,16},{32,32},{33,48},{64,64},{65,80},{96,96},{97,112},{128... | collective-permute-start | bytes 983048 | tf_op jit(solution)/shard_map/ppermute | solution.py:35
  14.2 10.0 %collective-permute-start.1 = (bf16[320,512]{1,0:T(8,128)(2,1)}, bf16[320,512]{1,0:T(8,128)(2,1)S(1)}, u32[]{:S(2)}, u32[]{:S(2)}) collective-permute-start(bf16[320,512]{1,0:T(8,128)(2,1)} %bitcast.67), channel_id=1, source_target_pairs={{0,2},{1,18},{32,34},{33,50},{64,66},{65,82},{96,98},{97,114},{128... | collective-permute-start | bytes 983048 | tf_op jit(solution)/shard_map/ppermute | solution.py:35
  24.3 18.0 %copy-start.3 = (bf16[2,320,512]{2,1,0:T(8,128)(2,1)}, bf16[2,320,512]{2,1,0:T(8,128)(2,1)S(1)}, u32[]{:S(2)}) copy-start(bf16[2,320,512]{2,1,0:T(8,128)(2,1)S(1)} %maximum_select_fusion) | copy-start | bytes 1966084
  24.3 17.9 %collective-permute-start.2 = (bf16[640,512]{1,0:T(8,128)(2,1)S(1)}, bf16[640,512]{1,0:T(8,128)(2,1)S(1)}, u32[]{:S(2)}, u32[]{:S(2)}) collective-permute-start(bf16[640,512]{1,0:T(8,128)(2,1)S(1)} %bitcast.61), channel_id=1, source_target_pairs={{0,4},{1,5},{32,36},{33,37},{64,68},{65,69},{96,100},{97,101},{128... | collective-permute-start | bytes 1966088 | tf_op jit(solution)/shard_map/ppermute | solution.py:35
  25.6 16.7 %collective-permute-start.3 = (bf16[640,512]{1,0:T(8,128)(2,1)S(1)}, bf16[640,512]{1,0:T(8,128)(2,1)S(1)}, u32[]{:S(2)}, u32[]{:S(2)}) collective-permute-start(bf16[640,512]{1,0:T(8,128)(2,1)S(1)} %bitcast.62), channel_id=1, source_target_pairs={{0,12},{1,13},{32,44},{33,45},{64,76},{65,77},{96,108},{97,109},{1... | collective-permute-start | bytes 1966088 | tf_op jit(solution)/shard_map/ppermute | solution.py:35
  27.0 23.0 %collective-permute-start.6 = (bf16[864,512]{1,0:T(8,128)(2,1)S(1)}, bf16[864,512]{1,0:T(8,128)(2,1)}, u32[]{:S(2)}, u32[]{:S(2)}) collective-permute-start(bf16[864,512]{1,0:T(8,128)(2,1)S(1)} %fusion), channel_id=1, source_target_pairs={{0,16},{1,17},{32,48},{33,49},{64,80},{65,81},{96,112},{97,113},{1... | collective-permute-start | bytes 2654216 | tf_op jit(solution)/shard_map/ppermute | solution.py:35
  42.1 0.8 copy-start.6
  42.2 10.7 %collective-permute-start.4 = (bf16[320,512]{1,0:T(8,128)(2,1)S(1)}, bf16[320,512]{1,0:T(8,128)(2,1)S(1)}, u32[]{:S(2)}, u32[]{:S(2)}) collective-permute-start(bf16[320,512]{1,0:T(8,128)(2,1)S(1)} %slice.9), channel_id=1, source_target_pairs={{0,4},{1,5},{32,36},{33,37},{64,68},{65,69},{96,100},{97,101},{128... | collective-permute-start | bytes 983048 | tf_op jit(solution)/shard_map/ppermute | solution.py:35
  42.3 0.9 copy-start.8
  43.2 9.7 %collective-permute-start.5 = (bf16[320,512]{1,0:T(8,128)(2,1)S(1)}, bf16[320,512]{1,0:T(8,128)(2,1)S(1)}, u32[]{:S(2)}, u32[]{:S(2)}) collective-permute-start(bf16[320,512]{1,0:T(8,128)(2,1)S(1)} %slice.10), channel_id=1, source_target_pairs={{0,12},{1,13},{32,44},{33,45},{64,76},{65,77},{96,108},{97,109},{1... | collective-permute-start | bytes 983048 | tf_op jit(solution)/shard_map/ppermute | solution.py:35
  45.9 1.1 copy-start.4
  45.9 1.3 copy-start.7
  45.9 1.5 %copy-start.9 = (bf16[640,512]{1,0:T(8,128)(2,1)S(1)}, bf16[640,512]{1,0:T(8,128)(2,1)}, u32[]{:S(2)}) copy-start(bf16[640,512]{1,0:T(8,128)(2,1)} %copy-done.8) | copy-start | bytes 1966084
  53.0 5.9 %collective-permute-start.7 = (bf16[2560,512]{1,0:T(8,128)(2,1)S(1)}, bf16[2560,512]{1,0:T(8,128)(2,1)}, u32[]{:S(2)}, u32[]{:S(2)}) collective-permute-start(bf16[2560,512]{1,0:T(8,128)(2,1)S(1)} %constant_dynamic-update-slice_fusion), channel_id=1, source_target_pairs={{0,1},{1,0},{32,33},{33,32},{64,65},{65,64},{96,97},{97,96},{128,1... | collective-permute-start | bytes 7864328 | tf_op jit(solution)/shard_map/ppermute | solution.py:35
  55.5 3.4 %copy-start.12 = (bf16[864,512]{1,0:T(8,128)(2,1)}, bf16[864,512]{1,0:T(8,128)(2,1)S(1)}, u32[]{:S(2)}) copy-start(bf16[864,512]{1,0:T(8,128)(2,1)S(1)} %get-tuple-element.41) | copy-start | bytes 2654212
  55.5 8.0 %copy-start.10 = (bf16[864,512]{1,0:T(8,128)(2,1)}, bf16[864,512]{1,0:T(8,128)(2,1)S(1)}, u32[]{:S(2)}) copy-start(bf16[864,512]{1,0:T(8,128)(2,1)S(1)} %get-tuple-element.43) | copy-start | bytes 2654212
  68.2 4.6 %copy-start.13 = (bf16[864,512]{1,0:T(8,128)(2,1)S(1)}, bf16[864,512]{1,0:T(8,128)(2,1)}, u32[]{:S(2)}) copy-start(bf16[864,512]{1,0:T(8,128)(2,1)} %copy-done.12) | copy-start | bytes 2654212
  72.7 11.9 %copy-start.11 = (bf16[864,512]{1,0:T(8,128)(2,1)S(1)}, bf16[864,512]{1,0:T(8,128)(2,1)}, u32[]{:S(2)}) copy-start(bf16[864,512]{1,0:T(8,128)(2,1)} %copy-done.10) | copy-start | bytes 2654212
  72.7 24.1 %slice-start = ((s8[4587520]{0:T(1024)(128)(4,1)}), s8[393216]{0:T(1024)(128)(4,1)S(1)}, s32[]{:S(2)}) async-start(s8[4587520]{0:T(1024)(128)(4,1)} %bitcast.59), calls=%async_computation.3 | async-start | bytes 786432
  79.3 5.3 %collective-permute-start.8 = (bf16[2560,512]{1,0:T(8,128)(2,1)}, bf16[2560,512]{1,0:T(8,128)(2,1)}, u32[]{:S(2)}, u32[]{:S(2)}) collective-permute-start(bf16[2560,512]{1,0:T(8,128)(2,1)} %convolution_convert_fusion), channel_id=1, source_target_pairs={{0,1},{1,0},{32,33},{33,32},{64,65},{65,64},{96,97},{97,96},{128,1... | collective-permute-start | bytes 7864328 | tf_op jit(solution)/shard_map/ppermute | solution.py:35
  79.7 17.1 %slice-start.1 = ((s8[4587520]{0:T(1024)(128)(4,1)}), s8[4194304]{0:T(1024)(128)(4,1)S(1)}, s32[]{:S(2)}) async-start(s8[4587520]{0:T(1024)(128)(4,1)} %bitcast.59), calls=%async_computation.4 | async-start | bytes 8388608
  90.5 6.3 %copy-start.5 = (bf16[2560,512]{1,0:T(8,128)(2,1)S(1)}, bf16[2560,512]{1,0:T(8,128)(2,1)}, u32[]{:S(2)}) copy-start(bf16[2560,512]{1,0:T(8,128)(2,1)} %get-tuple-element.38) | copy-start | bytes 7864324
  90.7 18.0 %copy-start = (bf16[2560,512]{1,0:T(8,128)(2,1)S(1)}, bf16[2560,512]{1,0:T(8,128)(2,1)}, u32[]{:S(2)}) copy-start(bf16[2560,512]{1,0:T(8,128)(2,1)} %get-tuple-element.37) | copy-start | bytes 7864324
  90.7 10.1 %collective-permute-start.10 = (bf16[320,512]{1,0:T(8,128)(2,1)S(1)}, bf16[320,512]{1,0:T(8,128)(2,1)S(1)}, u32[]{:S(2)}, u32[]{:S(2)}) collective-permute-start(bf16[320,512]{1,0:T(8,128)(2,1)S(1)} %get-tuple-element.46), channel_id=1, source_target_pairs={{0,12},{1,13},{32,44},{33,45},{64,76},{65,77},{96,108},{97,109},{1... | collective-permute-start | bytes 983048 | tf_op jit(solution)/shard_map/ppermute | solution.py:35
  94.1 9.9 %collective-permute-start.9 = (bf16[320,512]{1,0:T(8,128)(2,1)S(1)}, bf16[320,512]{1,0:T(8,128)(2,1)S(1)}, u32[]{:S(2)}, u32[]{:S(2)}) collective-permute-start(bf16[320,512]{1,0:T(8,128)(2,1)S(1)} %get-tuple-element.45), channel_id=1, source_target_pairs={{0,4},{1,5},{32,36},{33,37},{64,68},{65,69},{96,100},{97,101},{128... | collective-permute-start | bytes 983048 | tf_op jit(solution)/shard_map/ppermute | solution.py:35
  94.1 17.1 %collective-permute-start.13 = (bf16[320,512]{1,0:T(8,128)(2,1)S(1)}, bf16[320,512]{1,0:T(8,128)(2,1)S(1)}, u32[]{:S(2)}, u32[]{:S(2)}) collective-permute-start(bf16[320,512]{1,0:T(8,128)(2,1)S(1)} %get-tuple-element.47), channel_id=1, source_target_pairs={{0,4},{1,5},{32,36},{33,37},{64,68},{65,69},{96,100},{97,101},{128... | collective-permute-start | bytes 983048 | tf_op jit(solution)/shard_map/ppermute | solution.py:35
  94.1 17.1 %collective-permute-start.14 = (bf16[320,512]{1,0:T(8,128)(2,1)S(1)}, bf16[320,512]{1,0:T(8,128)(2,1)S(1)}, u32[]{:S(2)}, u32[]{:S(2)}) collective-permute-start(bf16[320,512]{1,0:T(8,128)(2,1)S(1)} %get-tuple-element.48), channel_id=1, source_target_pairs={{0,12},{1,13},{32,44},{33,45},{64,76},{65,77},{96,108},{97,109},{1... | collective-permute-start | bytes 983048 | tf_op jit(solution)/shard_map/ppermute | solution.py:35
  104.2 13.9 %collective-permute-start.11 = (bf16[320,512]{1,0:T(8,128)(2,1)S(1)}, bf16[320,512]{1,0:T(8,128)(2,1)S(1)}, u32[]{:S(2)}, u32[]{:S(2)}) collective-permute-start(bf16[320,512]{1,0:T(8,128)(2,1)S(1)} %get-tuple-element.53), channel_id=1, source_target_pairs={{0,4},{1,5},{32,36},{33,37},{64,68},{65,69},{96,100},{97,101},{128... | collective-permute-start | bytes 983048 | tf_op jit(solution)/shard_map/ppermute | solution.py:35
  104.3 13.8 %collective-permute-start.12 = (bf16[320,512]{1,0:T(8,128)(2,1)S(1)}, bf16[320,512]{1,0:T(8,128)(2,1)S(1)}, u32[]{:S(2)}, u32[]{:S(2)}) collective-permute-start(bf16[320,512]{1,0:T(8,128)(2,1)S(1)} %get-tuple-element.54), channel_id=1, source_target_pairs={{0,12},{1,13},{32,44},{33,45},{64,76},{65,77},{96,108},{97,109},{1... | collective-permute-start | bytes 983048 | tf_op jit(solution)/shard_map/ppermute | solution.py:35
  106.9 31.4 %collective-permute-start.17 = (bf16[864,512]{1,0:T(8,128)(2,1)S(1)}, bf16[864,512]{1,0:T(8,128)(2,1)S(1)}, u32[]{:S(2)}, u32[]{:S(2)}) collective-permute-start(bf16[864,512]{1,0:T(8,128)(2,1)S(1)} %convolution_convert_fusion.1), channel_id=1, source_target_pairs={{0,16},{1,17},{32,48},{33,49},{64,80},{65,81},{96,112},{97,113},{1... | collective-permute-start | bytes 2654216 | tf_op jit(solution)/shard_map/ppermute | solution.py:35
  111.2 27.2 %copy-start.1 = (bf16[512,864]{0,1:T(8,128)(2,1)S(1)}, bf16[512,864]{0,1:T(8,128)(2,1)}, u32[]{:S(2)}) copy-start(bf16[512,864]{0,1:T(8,128)(2,1)} %param.5) | copy-start | bytes 2654212
  111.2 27.2 %copy-start.2 = (bf16[512,864]{0,1:T(8,128)(2,1)S(1)}, bf16[512,864]{0,1:T(8,128)(2,1)}, u32[]{:S(2)}) copy-start(bf16[512,864]{0,1:T(8,128)(2,1)} %param.4) | copy-start | bytes 2654212
  118.4 18.6 %collective-permute-start.15 = (bf16[320,512]{1,0:T(8,128)(2,1)S(1)}, bf16[320,512]{1,0:T(8,128)(2,1)S(1)}, u32[]{:S(2)}, u32[]{:S(2)}) collective-permute-start(bf16[320,512]{1,0:T(8,128)(2,1)S(1)} %get-tuple-element.64), channel_id=1, source_target_pairs={{0,0},{1,16},{32,32},{33,48},{64,64},{65,80},{96,96},{97,112},{128... | collective-permute-start | bytes 983048 | tf_op jit(solution)/shard_map/ppermute | solution.py:35
  123.3 14.2 %collective-permute-start.16 = (bf16[320,512]{1,0:T(8,128)(2,1)S(1)}, bf16[320,512]{1,0:T(8,128)(2,1)S(1)}, u32[]{:S(2)}, u32[]{:S(2)}) collective-permute-start(bf16[320,512]{1,0:T(8,128)(2,1)S(1)} %get-tuple-element.65), channel_id=1, source_target_pairs={{0,2},{1,18},{32,34},{33,50},{64,66},{65,82},{96,98},{97,114},{128... | collective-permute-start | bytes 983048 | tf_op jit(solution)/shard_map/ppermute | solution.py:35
Sparse Core Ops, SparseCore 0:
  9.8 62.2 all-gather.1
  74.7 57.6 reduce-scatter.1

commit v5 on v4

--- a/solution.py
+++ b/solution.py
@@ -133,6 +133,7 @@
 
     keep, give = block(lo == 0), block(lo == 1)
     keep, give = send(keep, TURN), send(give, TURN_LO)
+    keep, give, grad_down = lax.optimization_barrier((keep, give, grad_down))
     mixed = bf16(f32(keep) + f32(give)).T
 
     d_hidden = keep_dh + f32(send(away, PARTNER))

time: 150 us -> 143 us (0.953)
  waiting for transfers between devices: 62.5 us -> 54.4 us
    ppermute x18, waiting for transfers between devices: 61.8 us -> 44.5 us  [send(): return lax.ppermute(value, AXES, pairs)]
    reduce_scatter x1, waiting for transfers between devices: 0.01 us -> 6.82 us  [body(): lax.psum_scatter(grad, 'blk', axis_index_groups=PLANES, scatter_dimension...]
    all_gather x1, waiting for transfers between devices: 0.01 us -> 2.39 us  [body(): lax.all_gather(down_weight, 'blk', axis_index_groups=PLANES, axis=0, tile...]
  transfers between devices with their start and end apart: 20 -> 20, of which waited for: 12 -> 14; matrix products, arithmetic and copies ran while one was open for 26% -> 28% of each run, Pallas kernels for 0% -> 0%
where the time goes in v5:
time: 143 us; the launch traced here: 142 us
  waiting for transfers between devices  54.4 us (38%)
  starting transfers between devices  30.4 us (21%)
  matrix products  26.8 us (19%)
  between operations  14.3 us (10%)
  other arithmetic  13.6 us (10%)
  local copies, waits for them, and re-layouts  2.79 us (2%)
    ppermute x18, waiting for transfers between devices, send(): return lax.ppermute(value, AXES, pairs)  44.5 us
    ppermute x18, starting transfers between devices, send(): return lax.ppermute(value, AXES, pairs)  30.3 us
    dot_general x6, matrix products, dot(): lax.dot_general(left, right, ((dims[0], dims[1]), ((), ())), preferred_el...  26.8 us
    reduce_scatter x1, waiting for transfers between devices, body(): lax.psum_scatter(grad, 'blk', axis_index_groups=PLANES, scatter_dimension...  6.82 us
    select_n x1, other arithmetic, body(): jnp.where(same, cot_b, cot_a)  4.56 us
  transfers between devices with their start and end apart: 20, of which 14 were waited for; matrix products, arithmetic and copies ran while one was open for 28% of the time, Pallas kernels for 0%

profile of v5, /device:TPU:1, one launch (start us, length us, event | category | flops | bytes accessed | tf_op | source)
XLA Modules:
  0.0 142.3 jit_solution(15864571020441374332)
XLA Ops:
  7.2 0.7 all-gather.2.cloned.1.call-update
  7.9 4.2 %collective-permute-start.1 = (bf16[320,512]{1,0:T(8,128)(2,1)}, bf16[320,512]{1,0:T(8,128)(2,1)S(1)}, u32[]{:S(2)}, u32[]{:S(2)}) collective-permute-start(bf16[320,512]{1,0:T(8,128)(2,1)} %bitcast.66), channel_id=1, source_target_pairs={{0,2},{1,18},{32,34},{33,50},{64,66},{65,82},{96,98},{97,114},{128... | collective-permute-start | bytes 983048 | tf_op jit(solution)/shard_map/ppermute | solution.py:35
  12.2 2.1 %collective-permute-start = (bf16[320,512]{1,0:T(8,128)(2,1)}, bf16[320,512]{1,0:T(8,128)(2,1)S(1)}, u32[]{:S(2)}, u32[]{:S(2)}) collective-permute-start(bf16[320,512]{1,0:T(8,128)(2,1)} %bitcast.67), channel_id=1, source_target_pairs={{0,0},{1,16},{32,32},{33,48},{64,64},{65,80},{96,96},{97,112},{128... | collective-permute-start | bytes 983048 | tf_op jit(solution)/shard_map/ppermute | solution.py:35
  14.3 2.0 %fusion = bf16[864,512]{1,0:T(8,128)(2,1)S(1)} fusion(bf16[512,864]{0,1:T(8,128)(2,1)} %param.5, bf16[512,864]{0,1:T(8,128)(2,1)} %param.4), kind=kLoop, calls=%fused_computation.7 | loop fusion | flops 3538944 | bytes 2654208 | tf_op jit(solution)/shard_map/convert_element_type | solution.py:43
  16.3 1.3 collective-permute-done.1
  17.6 4.7 %collective-permute-done = bf16[320,512]{1,0:T(8,128)(2,1)S(1)} collective-permute-done((bf16[320,512]{1,0:T(8,128)(2,1)}, bf16[320,512]{1,0:T(8,128)(2,1)S(1)}, u32[]{:S(2)}, u32[]{:S(2)}) %collective-permute-start) | collective-permute-done | bytes 327712 | tf_op jit(solution)/shard_map/ppermute | solution.py:35
  22.4 1.3 collective-permute-start.2
  23.7 1.5 %collective-permute-start.3 = (bf16[640,512]{1,0:T(8,128)(2,1)S(1)}, bf16[640,512]{1,0:T(8,128)(2,1)S(1)}, u32[]{:S(2)}, u32[]{:S(2)}) collective-permute-start(bf16[640,512]{1,0:T(8,128)(2,1)S(1)} %bitcast.62), channel_id=1, source_target_pairs={{0,12},{1,13},{32,44},{33,45},{64,76},{65,77},{96,108},{97,109},{1... | collective-permute-start | bytes 1966088 | tf_op jit(solution)/shard_map/ppermute | solution.py:35
  25.1 14.2 %collective-permute-done.2 = bf16[640,512]{1,0:T(8,128)(2,1)S(1)} collective-permute-done((bf16[640,512]{1,0:T(8,128)(2,1)S(1)}, bf16[640,512]{1,0:T(8,128)(2,1)S(1)}, u32[]{:S(2)}, u32[]{:S(2)}) %collective-permute-start.2) | collective-permute-done | bytes 655392 | tf_op jit(solution)/shard_map/ppermute | solution.py:35
  39.5 0.7 copy-done.6
  40.1 0.2 copy-done.8
  40.3 2.7 %collective-permute-start.5 = (bf16[320,512]{1,0:T(8,128)(2,1)S(1)}, bf16[320,512]{1,0:T(8,128)(2,1)S(1)}, u32[]{:S(2)}, u32[]{:S(2)}) collective-permute-start(bf16[320,512]{1,0:T(8,128)(2,1)S(1)} %slice.10), channel_id=1, source_target_pairs={{0,12},{1,13},{32,44},{33,45},{64,76},{65,77},{96,108},{97,109},{1... | collective-permute-start | bytes 983048 | tf_op jit(solution)/shard_map/ppermute | solution.py:35
  43.1 0.2 broadcast_in_dim.3
  43.3 0.9 copy-done.4
  44.6 2.8 %collective-permute-done.6 = bf16[864,512]{1,0:T(8,128)(2,1)} collective-permute-done((bf16[864,512]{1,0:T(8,128)(2,1)S(1)}, bf16[864,512]{1,0:T(8,128)(2,1)}, u32[]{:S(2)}, u32[]{:S(2)}) %collective-permute-start.6) | collective-permute-done | bytes 884768 | tf_op jit(solution)/shard_map/ppermute | solution.py:35
  47.4 2.5 %collective-permute-done.4 = bf16[320,512]{1,0:T(8,128)(2,1)S(1)} collective-permute-done((bf16[320,512]{1,0:T(8,128)(2,1)S(1)}, bf16[320,512]{1,0:T(8,128)(2,1)S(1)}, u32[]{:S(2)}, u32[]{:S(2)}) %collective-permute-start.4) | collective-permute-done | bytes 327712 | tf_op jit(solution)/shard_map/ppermute | solution.py:35
  49.9 0.5 collective-permute-done.5
  50.5 0.4 collective-permute-start.7
  51.0 1.3 broadcast_select_fusion.2
  52.3 3.5 %collective-permute-done.7 = bf16[2560,512]{1,0:T(8,128)(2,1)} collective-permute-done((bf16[2560,512]{1,0:T(8,128)(2,1)S(1)}, bf16[2560,512]{1,0:T(8,128)(2,1)}, u32[]{:S(2)}, u32[]{:S(2)}) %collective-permute-start.7) | collective-permute-done | bytes 2621472 | tf_op jit(solution)/shard_map/ppermute | solution.py:35
  55.9 4.7 %fusion.12 = f32[2560,864]{1,0:T(8,128)S(1)} fusion(bf16[2560,512]{1,0:T(8,128)(2,1)} %collective-permute-done.7, bf16[864,512]{1,0:T(8,128)(2,1)S(1)} %get-tuple-element.44), kind=kOutput, calls=%fused_computation.44 | convolution fusion | flops 2264924160 | bytes 12353536 | tf_op jit(solution)/shard_map/dot_general | solution.py:51
  60.5 4.6 %add_convert_fusion = bf16[2560,864]{1,0:T(8,128)(2,1)} fusion(f32[2560,864]{1,0:T(8,128)S(1)} %fusion.12, bf16[2560,512]{1,0:T(8,128)(2,1)S(1)} %constant_dynamic-update-slice_fusion, bf16[864,512]{1,0:T(8,128)(2,1)S(1)} %get-tuple-element.46), kind=kOutput, calls=%fused_computation | convolution fusion | flops 2269347840 | bytes 16777216 | tf_op jit(solution)/shard_map/dot_general | solution.py:51
  65.2 4.6 %broadcast_select_fusion = (bf16[2560,512]{1,0:T(8,128)(2,1)}, bf16[2560,512]{1,0:T(8,128)(2,1)}) fusion(bf16[2560,512]{1,0:T(8,128)(2,1)} %collective-permute-done.7, bf16[2560,512]{1,0:T(8,128)(2,1)S(1)} %constant_dynamic-update-slice_fusion, pred[]{:T(512)S(6)} %eq.10), kind=kLoop, calls=%fused_computation.3 | loop fusion | flops 2621440 | bytes 10485761 | tf_op jit(solution)/shard_map/jit(_where)/select_n | solution.py:105
  69.7 2.4 %all-gather.2.cloned.1.call-done = bf16[2560,864]{1,0:T(8,128)(2,1)} async-done(((bf16[320,864]{1,0:T(8,128)(2,1)}), bf16[2560,864]{1,0:T(8,128)(2,1)}) %all-gather.2.cloned.1.call-update) | async-done | bytes 4423696 | tf_op jit(solution)/shard_map/all_gather | solution.py:73
  72.1 6.5 %convolution_convert_fusion = bf16[2560,512]{1,0:T(8,128)(2,1)} fusion(bf16[2560,864]{1,0:T(8,128)(2,1)} %all-gather.2.cloned.1.call-done, bf16[864,512]{1,0:T(8,128)(2,1)S(1)} %copy-done.13), kind=kOutput, calls=%fused_computation.2 | convolution fusion | flops 2266234880 | bytes 7929856 | tf_op jit(solution)/shard_map/dot_general | solution.py:51
  78.7 0.7 collective-permute-start.8
  79.3 4.9 %collective-permute-done.8 = bf16[2560,512]{1,0:T(8,128)(2,1)} collective-permute-done((bf16[2560,512]{1,0:T(8,128)(2,1)}, bf16[2560,512]{1,0:T(8,128)(2,1)}, u32[]{:S(2)}, u32[]{:S(2)}) %collective-permute-start.8) | collective-permute-done | bytes 2621472 | tf_op jit(solution)/shard_map/ppermute | solution.py:35
  84.2 6.1 %add_convert_fusion.1 = bf16[2560,512]{1,0:T(8,128)(2,1)S(1)} fusion(bf16[2560,512]{1,0:T(8,128)(2,1)} %collective-permute-done.8, bf16[2560,864]{1,0:T(8,128)(2,1)} %all-gather.2.cloned.1.call-done, bf16[864,512]{1,0:T(8,128)(2,1)S(1)} %copy-done.11), kind=kOutput, calls=%fused_computation.1 | convolution fusion | flops 2268856320 | bytes 10551296 | tf_op jit(solution)/shard_map/dot_general | solution.py:51
  90.3 0.2 constant_dynamic-slice_fusion
  90.6 1.4 collective-permute-start.9
  91.9 1.4 collective-permute-start.10
  93.4 2.6 %collective-permute-start.14 = (bf16[320,512]{1,0:T(8,128)(2,1)S(1)}, bf16[320,512]{1,0:T(8,128)(2,1)S(1)}, u32[]{:S(2)}, u32[]{:S(2)}) collective-permute-start(bf16[320,512]{1,0:T(8,128)(2,1)S(1)} %get-tuple-element.51), channel_id=1, source_target_pairs={{0,12},{1,13},{32,44},{33,45},{64,76},{65,77},{96,108},{97,109},{1... | collective-permute-start | bytes 983048 | tf_op jit(solution)/shard_map/ppermute | solution.py:35
  96.0 2.5 %convolution_convert_fusion.1 = bf16[864,512]{1,0:T(8,128)(2,1)S(1)} fusion(bf16[2560,864]{1,0:T(8,128)(2,1)S(1)} %bitcast.60, bf16[2560,512]{1,0:T(8,128)(2,1)S(1)} %copy-done.5), kind=kOutput, calls=%fused_computation.20 | convolution fusion | flops 2265366528 | bytes 7929856 | tf_op jit(solution)/shard_map/dot_general | solution.py:51
  98.5 2.2 %collective-permute-done.9 = bf16[320,512]{1,0:T(8,128)(2,1)S(1)} collective-permute-done((bf16[320,512]{1,0:T(8,128)(2,1)S(1)}, bf16[320,512]{1,0:T(8,128)(2,1)S(1)}, u32[]{:S(2)}, u32[]{:S(2)}) %collective-permute-start.9) | collective-permute-done | bytes 327712 | tf_op jit(solution)/shard_map/ppermute | solution.py:35
  100.7 0.2 add_convert_fusion.5
  100.9 1.2 collective-permute-start.11
  102.1 1.6 %collective-permute-start.12 = (bf16[320,512]{1,0:T(8,128)(2,1)S(1)}, bf16[320,512]{1,0:T(8,128)(2,1)S(1)}, u32[]{:S(2)}, u32[]{:S(2)}) collective-permute-start(bf16[320,512]{1,0:T(8,128)(2,1)S(1)} %get-tuple-element.57), channel_id=1, source_target_pairs={{0,12},{1,13},{32,44},{33,45},{64,76},{65,77},{96,108},{97,109},{1... | collective-permute-start | bytes 983048 | tf_op jit(solution)/shard_map/ppermute | solution.py:35
  103.7 3.0 %collective-permute-start.17 = (bf16[864,512]{1,0:T(8,128)(2,1)S(1)}, bf16[864,512]{1,0:T(8,128)(2,1)S(1)}, u32[]{:S(2)}, u32[]{:S(2)}) collective-permute-start(bf16[864,512]{1,0:T(8,128)(2,1)S(1)} %convolution_convert_fusion.1), channel_id=1, source_target_pairs={{0,16},{1,17},{32,48},{33,49},{64,80},{65,81},{96,112},{97,113},{1... | collective-permute-start | bytes 2654216 | tf_op jit(solution)/shard_map/ppermute | solution.py:35
  106.7 2.5 %fusion.11 = f32[864,512]{1,0:T(8,128)S(1)} fusion(bf16[2560,864]{1,0:T(8,128)(2,1)S(1)} %bitcast.60, bf16[2560,512]{1,0:T(8,128)(2,1)S(1)} %copy-done), kind=kOutput, calls=%fused_computation.43 | convolution fusion | flops 2264924160 | bytes 8814592 | tf_op jit(solution)/shard_map/dot_general | solution.py:51
  109.2 5.6 %collective-permute-done.11 = bf16[320,512]{1,0:T(8,128)(2,1)S(1)} collective-permute-done((bf16[320,512]{1,0:T(8,128)(2,1)S(1)}, bf16[320,512]{1,0:T(8,128)(2,1)S(1)}, u32[]{:S(2)}, u32[]{:S(2)}) %collective-permute-start.11) | collective-permute-done | bytes 327712 | tf_op jit(solution)/shard_map/ppermute | solution.py:35
  114.8 0.3 add_convert_fusion.3
  115.1 5.9 %collective-permute-start.15 = (bf16[320,512]{1,0:T(8,128)(2,1)S(1)}, bf16[320,512]{1,0:T(8,128)(2,1)S(1)}, u32[]{:S(2)}, u32[]{:S(2)}) collective-permute-start(bf16[320,512]{1,0:T(8,128)(2,1)S(1)} %get-tuple-element.71), channel_id=1, source_target_pairs={{0,0},{1,16},{32,32},{33,48},{64,64},{65,80},{96,96},{97,112},{128... | collective-permute-start | bytes 983048 | tf_op jit(solution)/shard_map/ppermute | solution.py:35
  121.0 0.3 collective-permute-start.16
  121.3 2.1 %collective-permute-done.17 = bf16[864,512]{1,0:T(8,128)(2,1)S(1)} collective-permute-done((bf16[864,512]{1,0:T(8,128)(2,1)S(1)}, bf16[864,512]{1,0:T(8,128)(2,1)S(1)}, u32[]{:S(2)}, u32[]{:S(2)}) %collective-permute-start.17) | collective-permute-done | bytes 884768 | tf_op jit(solution)/shard_map/ppermute | solution.py:35
  123.4 2.2 %fusion.8 = (bf16[512,864]{0,1:T(8,128)(2,1)}, bf16[512,864]{0,1:T(8,128)(2,1)}) fusion(f32[864,512]{1,0:T(8,128)S(1)} %fusion.11, bf16[864,512]{1,0:T(8,128)(2,1)S(1)} %collective-permute-done.17, bf16[512,864]{0,1:T(8,128)(2,1)S(1)} %copy-done.2, bf16[512,864]{0,1:T(8,128)(2,1)S(1)} %copy-done.1), kind=kLoop, calls=%fused_computation.21 | loop fusion | flops 7520256 | bytes 6193152 | tf_op jit(solution)/shard_map/transpose | solution.py:141
  125.6 6.8 %reduce-scatter.2.cloned.1.call-done = bf16[320,864]{1,0:T(8,128)(2,1)} async-done(((bf16[2560,864]{1,0:T(8,128)(2,1)}), bf16[320,864]{1,0:T(8,128)(2,1)}) %reduce-scatter.2.cloned.1.call-update) | async-done | bytes 552976 | tf_op jit(solution)/shard_map/reduce_scatter | solution.py:103
  132.4 2.1 %convert_element_type.125 = f32[320,864]{1,0:T(8,128)} convert(bf16[320,864]{1,0:T(8,128)(2,1)} %reduce-scatter.2.cloned.1.call-done) | non-fusion elementwise | flops 276480 | bytes 1658880 | tf_op jit(solution)/shard_map/convert_element_type | solution.py:39
  134.7 0.8 fusion.10
  (51 shorter events, 1.1 us)
Async XLA Ops:
  7.2 65.0 %all-gather.2.cloned.1.call-start = ((), (), s32[]{:S(2)}) async-start(), calls=%async_computation.1 | async-start | bytes 5160960 | tf_op jit(solution)/shard_map/all_gather | solution.py:73
  7.9 124.5 %reduce-scatter.2.cloned.1.call-start = ((), (), s32[]{:S(2)}) async-start(), calls=%async_computation.2 | async-start | bytes 5160960 | tf_op jit(solution)/shard_map/reduce_scatter | solution.py:103
  7.9 9.6 %collective-permute-start.1 = (bf16[320,512]{1,0:T(8,128)(2,1)}, bf16[320,512]{1,0:T(8,128)(2,1)S(1)}, u32[]{:S(2)}, u32[]{:S(2)}) collective-permute-start(bf16[320,512]{1,0:T(8,128)(2,1)} %bitcast.66), channel_id=1, source_target_pairs={{0,2},{1,18},{32,34},{33,50},{64,66},{65,82},{96,98},{97,114},{128... | collective-permute-start | bytes 983048 | tf_op jit(solution)/shard_map/ppermute | solution.py:35
  12.2 10.1 %collective-permute-start = (bf16[320,512]{1,0:T(8,128)(2,1)}, bf16[320,512]{1,0:T(8,128)(2,1)S(1)}, u32[]{:S(2)}, u32[]{:S(2)}) collective-permute-start(bf16[320,512]{1,0:T(8,128)(2,1)} %bitcast.67), channel_id=1, source_target_pairs={{0,0},{1,16},{32,32},{33,48},{64,64},{65,80},{96,96},{97,112},{128... | collective-permute-start | bytes 983048 | tf_op jit(solution)/shard_map/ppermute | solution.py:35
  22.4 17.1 %copy-start.3 = (bf16[2,320,512]{2,1,0:T(8,128)(2,1)}, bf16[2,320,512]{2,1,0:T(8,128)(2,1)S(1)}, u32[]{:S(2)}) copy-start(bf16[2,320,512]{2,1,0:T(8,128)(2,1)S(1)} %maximum_select_fusion) | copy-start | bytes 1966084
  22.4 16.9 %collective-permute-start.2 = (bf16[640,512]{1,0:T(8,128)(2,1)S(1)}, bf16[640,512]{1,0:T(8,128)(2,1)S(1)}, u32[]{:S(2)}, u32[]{:S(2)}) collective-permute-start(bf16[640,512]{1,0:T(8,128)(2,1)S(1)} %bitcast.61), channel_id=1, source_target_pairs={{0,4},{1,5},{32,36},{33,37},{64,68},{65,69},{96,100},{97,101},{128... | collective-permute-start | bytes 1966088 | tf_op jit(solution)/shard_map/ppermute | solution.py:35
  23.7 15.8 %collective-permute-start.3 = (bf16[640,512]{1,0:T(8,128)(2,1)S(1)}, bf16[640,512]{1,0:T(8,128)(2,1)S(1)}, u32[]{:S(2)}, u32[]{:S(2)}) collective-permute-start(bf16[640,512]{1,0:T(8,128)(2,1)S(1)} %bitcast.62), channel_id=1, source_target_pairs={{0,12},{1,13},{32,44},{33,45},{64,76},{65,77},{96,108},{97,109},{1... | collective-permute-start | bytes 1966088 | tf_op jit(solution)/shard_map/ppermute | solution.py:35
  25.1 22.3 %collective-permute-start.6 = (bf16[864,512]{1,0:T(8,128)(2,1)S(1)}, bf16[864,512]{1,0:T(8,128)(2,1)}, u32[]{:S(2)}, u32[]{:S(2)}) collective-permute-start(bf16[864,512]{1,0:T(8,128)(2,1)S(1)} %fusion), channel_id=1, source_target_pairs={{0,16},{1,17},{32,48},{33,49},{64,80},{65,81},{96,112},{97,113},{1... | collective-permute-start | bytes 2654216 | tf_op jit(solution)/shard_map/ppermute | solution.py:35
  39.3 0.8 copy-start.6
  39.3 10.6 %collective-permute-start.4 = (bf16[320,512]{1,0:T(8,128)(2,1)S(1)}, bf16[320,512]{1,0:T(8,128)(2,1)S(1)}, u32[]{:S(2)}, u32[]{:S(2)}) collective-permute-start(bf16[320,512]{1,0:T(8,128)(2,1)S(1)} %slice.9), channel_id=1, source_target_pairs={{0,4},{1,5},{32,36},{33,37},{64,68},{65,69},{96,100},{97,101},{128... | collective-permute-start | bytes 983048 | tf_op jit(solution)/shard_map/ppermute | solution.py:35
  39.4 0.9 copy-start.8
  40.3 10.1 %collective-permute-start.5 = (bf16[320,512]{1,0:T(8,128)(2,1)S(1)}, bf16[320,512]{1,0:T(8,128)(2,1)S(1)}, u32[]{:S(2)}, u32[]{:S(2)}) collective-permute-start(bf16[320,512]{1,0:T(8,128)(2,1)S(1)} %slice.10), channel_id=1, source_target_pairs={{0,12},{1,13},{32,44},{33,45},{64,76},{65,77},{96,108},{97,109},{1... | collective-permute-start | bytes 983048 | tf_op jit(solution)/shard_map/ppermute | solution.py:35
  43.1 1.1 copy-start.4
  43.1 1.3 copy-start.7
  43.1 1.5 %copy-start.9 = (bf16[640,512]{1,0:T(8,128)(2,1)S(1)}, bf16[640,512]{1,0:T(8,128)(2,1)}, u32[]{:S(2)}) copy-start(bf16[640,512]{1,0:T(8,128)(2,1)} %copy-done.8) | copy-start | bytes 1966084
  50.5 5.3 %collective-permute-start.7 = (bf16[2560,512]{1,0:T(8,128)(2,1)S(1)}, bf16[2560,512]{1,0:T(8,128)(2,1)}, u32[]{:S(2)}, u32[]{:S(2)}) collective-permute-start(bf16[2560,512]{1,0:T(8,128)(2,1)S(1)} %constant_dynamic-update-slice_fusion), channel_id=1, source_target_pairs={{0,1},{1,0},{32,33},{33,32},{64,65},{65,64},{96,97},{97,96},{128,1... | collective-permute-start | bytes 7864328 | tf_op jit(solution)/shard_map/ppermute | solution.py:35
  52.3 3.6 %copy-start.12 = (bf16[864,512]{1,0:T(8,128)(2,1)}, bf16[864,512]{1,0:T(8,128)(2,1)S(1)}, u32[]{:S(2)}) copy-start(bf16[864,512]{1,0:T(8,128)(2,1)S(1)} %get-tuple-element.44) | copy-start | bytes 2654212
  52.3 8.2 %copy-start.10 = (bf16[864,512]{1,0:T(8,128)(2,1)}, bf16[864,512]{1,0:T(8,128)(2,1)S(1)}, u32[]{:S(2)}) copy-start(bf16[864,512]{1,0:T(8,128)(2,1)S(1)} %get-tuple-element.46) | copy-start | bytes 2654212
  65.2 7.0 %copy-start.13 = (bf16[864,512]{1,0:T(8,128)(2,1)S(1)}, bf16[864,512]{1,0:T(8,128)(2,1)}, u32[]{:S(2)}) copy-start(bf16[864,512]{1,0:T(8,128)(2,1)} %copy-done.12) | copy-start | bytes 2654212
  69.7 14.5 %copy-start.11 = (bf16[864,512]{1,0:T(8,128)(2,1)S(1)}, bf16[864,512]{1,0:T(8,128)(2,1)}, u32[]{:S(2)}) copy-start(bf16[864,512]{1,0:T(8,128)(2,1)} %copy-done.10) | copy-start | bytes 2654212
  72.1 23.9 %slice-start = ((s8[4587520]{0:T(1024)(128)(4,1)}), s8[393216]{0:T(1024)(128)(4,1)S(1)}, s32[]{:S(2)}) async-start(s8[4587520]{0:T(1024)(128)(4,1)} %bitcast.59), calls=%async_computation.3 | async-start | bytes 786432
  78.7 5.6 %collective-permute-start.8 = (bf16[2560,512]{1,0:T(8,128)(2,1)}, bf16[2560,512]{1,0:T(8,128)(2,1)}, u32[]{:S(2)}, u32[]{:S(2)}) collective-permute-start(bf16[2560,512]{1,0:T(8,128)(2,1)} %convolution_convert_fusion), channel_id=1, source_target_pairs={{0,1},{1,0},{32,33},{33,32},{64,65},{65,64},{96,97},{97,96},{128,1... | collective-permute-start | bytes 7864328 | tf_op jit(solution)/shard_map/ppermute | solution.py:35
  79.3 16.7 %slice-start.1 = ((s8[4587520]{0:T(1024)(128)(4,1)}), s8[4194304]{0:T(1024)(128)(4,1)S(1)}, s32[]{:S(2)}) async-start(s8[4587520]{0:T(1024)(128)(4,1)} %bitcast.59), calls=%async_computation.4 | async-start | bytes 8388608
  90.3 5.7 %copy-start.5 = (bf16[2560,512]{1,0:T(8,128)(2,1)S(1)}, bf16[2560,512]{1,0:T(8,128)(2,1)}, u32[]{:S(2)}) copy-start(bf16[2560,512]{1,0:T(8,128)(2,1)} %get-tuple-element.41) | copy-start | bytes 7864324
  90.6 16.1 %copy-start = (bf16[2560,512]{1,0:T(8,128)(2,1)S(1)}, bf16[2560,512]{1,0:T(8,128)(2,1)}, u32[]{:S(2)}) copy-start(bf16[2560,512]{1,0:T(8,128)(2,1)} %get-tuple-element.40) | copy-start | bytes 7864324
  90.6 10.2 %collective-permute-start.9 = (bf16[320,512]{1,0:T(8,128)(2,1)S(1)}, bf16[320,512]{1,0:T(8,128)(2,1)S(1)}, u32[]{:S(2)}, u32[]{:S(2)}) collective-permute-start(bf16[320,512]{1,0:T(8,128)(2,1)S(1)} %get-tuple-element.48), channel_id=1, source_target_pairs={{0,4},{1,5},{32,36},{33,37},{64,68},{65,69},{96,100},{97,101},{128... | collective-permute-start | bytes 983048 | tf_op jit(solution)/shard_map/ppermute | solution.py:35
  91.9 8.8 %collective-permute-start.10 = (bf16[320,512]{1,0:T(8,128)(2,1)S(1)}, bf16[320,512]{1,0:T(8,128)(2,1)S(1)}, u32[]{:S(2)}, u32[]{:S(2)}) collective-permute-start(bf16[320,512]{1,0:T(8,128)(2,1)S(1)} %get-tuple-element.49), channel_id=1, source_target_pairs={{0,12},{1,13},{32,44},{33,45},{64,76},{65,77},{96,108},{97,109},{1... | collective-permute-start | bytes 983048 | tf_op jit(solution)/shard_map/ppermute | solution.py:35
  93.3 15.8 %collective-permute-start.13 = (bf16[320,512]{1,0:T(8,128)(2,1)S(1)}, bf16[320,512]{1,0:T(8,128)(2,1)S(1)}, u32[]{:S(2)}, u32[]{:S(2)}) collective-permute-start(bf16[320,512]{1,0:T(8,128)(2,1)S(1)} %get-tuple-element.50), channel_id=1, source_target_pairs={{0,4},{1,5},{32,36},{33,37},{64,68},{65,69},{96,100},{97,101},{128... | collective-permute-start | bytes 983048 | tf_op jit(solution)/shard_map/ppermute | solution.py:35
  93.4 15.8 %collective-permute-start.14 = (bf16[320,512]{1,0:T(8,128)(2,1)S(1)}, bf16[320,512]{1,0:T(8,128)(2,1)S(1)}, u32[]{:S(2)}, u32[]{:S(2)}) collective-permute-start(bf16[320,512]{1,0:T(8,128)(2,1)S(1)} %get-tuple-element.51), channel_id=1, source_target_pairs={{0,12},{1,13},{32,44},{33,45},{64,76},{65,77},{96,108},{97,109},{1... | collective-permute-start | bytes 983048 | tf_op jit(solution)/shard_map/ppermute | solution.py:35
  100.9 13.9 %collective-permute-start.11 = (bf16[320,512]{1,0:T(8,128)(2,1)S(1)}, bf16[320,512]{1,0:T(8,128)(2,1)S(1)}, u32[]{:S(2)}, u32[]{:S(2)}) collective-permute-start(bf16[320,512]{1,0:T(8,128)(2,1)S(1)} %get-tuple-element.56), channel_id=1, source_target_pairs={{0,4},{1,5},{32,36},{33,37},{64,68},{65,69},{96,100},{97,101},{128... | collective-permute-start | bytes 983048 | tf_op jit(solution)/shard_map/ppermute | solution.py:35
  102.1 12.7 %collective-permute-start.12 = (bf16[320,512]{1,0:T(8,128)(2,1)S(1)}, bf16[320,512]{1,0:T(8,128)(2,1)S(1)}, u32[]{:S(2)}, u32[]{:S(2)}) collective-permute-start(bf16[320,512]{1,0:T(8,128)(2,1)S(1)} %get-tuple-element.57), channel_id=1, source_target_pairs={{0,12},{1,13},{32,44},{33,45},{64,76},{65,77},{96,108},{97,109},{1... | collective-permute-start | bytes 983048 | tf_op jit(solution)/shard_map/ppermute | solution.py:35
  103.7 19.7 %collective-permute-start.17 = (bf16[864,512]{1,0:T(8,128)(2,1)S(1)}, bf16[864,512]{1,0:T(8,128)(2,1)S(1)}, u32[]{:S(2)}, u32[]{:S(2)}) collective-permute-start(bf16[864,512]{1,0:T(8,128)(2,1)S(1)} %convolution_convert_fusion.1), channel_id=1, source_target_pairs={{0,16},{1,17},{32,48},{33,49},{64,80},{65,81},{96,112},{97,113},{1... | collective-permute-start | bytes 2654216 | tf_op jit(solution)/shard_map/ppermute | solution.py:35
  109.1 14.2 %copy-start.1 = (bf16[512,864]{0,1:T(8,128)(2,1)S(1)}, bf16[512,864]{0,1:T(8,128)(2,1)}, u32[]{:S(2)}) copy-start(bf16[512,864]{0,1:T(8,128)(2,1)} %param.5) | copy-start | bytes 2654212
  109.1 14.2 %copy-start.2 = (bf16[512,864]{0,1:T(8,128)(2,1)S(1)}, bf16[512,864]{0,1:T(8,128)(2,1)}, u32[]{:S(2)}) copy-start(bf16[512,864]{0,1:T(8,128)(2,1)} %param.4) | copy-start | bytes 2654212
  115.1 19.4 %collective-permute-start.15 = (bf16[320,512]{1,0:T(8,128)(2,1)S(1)}, bf16[320,512]{1,0:T(8,128)(2,1)S(1)}, u32[]{:S(2)}, u32[]{:S(2)}) collective-permute-start(bf16[320,512]{1,0:T(8,128)(2,1)S(1)} %get-tuple-element.71), channel_id=1, source_target_pairs={{0,0},{1,16},{32,32},{33,48},{64,64},{65,80},{96,96},{97,112},{128... | collective-permute-start | bytes 983048 | tf_op jit(solution)/shard_map/ppermute | solution.py:35
  121.0 13.7 %collective-permute-start.16 = (bf16[320,512]{1,0:T(8,128)(2,1)S(1)}, bf16[320,512]{1,0:T(8,128)(2,1)S(1)}, u32[]{:S(2)}, u32[]{:S(2)}) collective-permute-start(bf16[320,512]{1,0:T(8,128)(2,1)S(1)} %get-tuple-element.70), channel_id=1, source_target_pairs={{0,2},{1,18},{32,34},{33,50},{64,66},{65,82},{96,98},{97,114},{128... | collective-permute-start | bytes 983048 | tf_op jit(solution)/shard_map/ppermute | solution.py:35
Sparse Core Ops, SparseCore 0:
  9.8 62.2 all-gather.1
  74.7 57.6 reduce-scatter.1

commit v6 on v5

--- a/solution.py
+++ b/solution.py
@@ -103,8 +103,7 @@
         lax.psum_scatter(grad, "blk", axis_index_groups=PLANES, scatter_dimension=0, tiled=True)
     )
     cot_keep, cot_away = jnp.where(same, cot_a, cot_b), jnp.where(same, cot_b, cot_a)
-    cot_keep, cot_away = lax.optimization_barrier((cot_keep, cot_away, grad[:8, :128]))[:2]
-    weight = first(weight, cot_keep, cot_away)
+    weight = first(weight, grad[:8, :128])
 
     part_b = row_major(bf16(dot(weight, hid_b, ((1,), (0,)))))
     got = send(part_b, SIBLING)

time: 143 us -> 143 us (level)
  other arithmetic: 13.6 us -> 9.05 us
  waiting for transfers between devices: 54.4 us -> 58.6 us
  matrix products: 26.8 us -> 29 us
  starting transfers between devices: 30.4 us -> 28.7 us
    all_gather x1, waiting for transfers between devices: 2.39 us -> 7.71 us  [body(): lax.all_gather(down_weight, 'blk', axis_index_groups=PLANES, axis=0, tile...]
    select_n x1 -> x0, other arithmetic: 4.56 us -> none  [body(): jnp.where(same, cot_b, cot_a)]
    dot_general x6, matrix products: 26.8 us -> 29 us  [dot(): lax.dot_general(left, right, ((dims[0], dims[1]), ((), ())), preferred_el...]
    ppermute x18, starting transfers between devices: 30.3 us -> 28.6 us  [send(): return lax.ppermute(value, AXES, pairs)]
  transfers between devices with their start and end apart: 20 -> 20, of which waited for: 14 -> 14; matrix products, arithmetic and copies ran while one was open for 28% -> 27% of each run, Pallas kernels for 0% -> 0%
where the time goes in v6:
time: 143 us; the launch traced here: 142 us
  waiting for transfers between devices  58.6 us (41%)
  matrix products  29 us (20%)
  starting transfers between devices  28.7 us (20%)
  between operations  14.3 us (10%)
  other arithmetic  9.05 us (6%)
  local copies, waits for them, and re-layouts  2.67 us (2%)
    ppermute x18, waiting for transfers between devices, send(): return lax.ppermute(value, AXES, pairs)  43.7 us
    dot_general x6, matrix products, dot(): lax.dot_general(left, right, ((dims[0], dims[1]), ((), ())), preferred_el...  29 us
    ppermute x18, starting transfers between devices, send(): return lax.ppermute(value, AXES, pairs)  28.6 us
    all_gather x1, waiting for transfers between devices, body(): lax.all_gather(down_weight, 'blk', axis_index_groups=PLANES, axis=0, tile...  7.71 us
    reduce_scatter x1, waiting for transfers between devices, body(): lax.psum_scatter(grad, 'blk', axis_index_groups=PLANES, scatter_dimension...  6.42 us
  transfers between devices with their start and end apart: 20, of which 14 were waited for; matrix products, arithmetic and copies ran while one was open for 27% of the time, Pallas kernels for 0%

profile of v6, /device:TPU:1, one launch (start us, length us, event | category | flops | bytes accessed | tf_op | source)
XLA Modules:
  0.0 142.2 jit_solution(3122867776778976566)
XLA Ops:
  7.2 0.7 all-gather.2.cloned.1.call-update
  7.9 4.2 %collective-permute-start.1 = (bf16[320,512]{1,0:T(8,128)(2,1)}, bf16[320,512]{1,0:T(8,128)(2,1)S(1)}, u32[]{:S(2)}, u32[]{:S(2)}) collective-permute-start(bf16[320,512]{1,0:T(8,128)(2,1)} %bitcast.64), channel_id=1, source_target_pairs={{0,2},{1,18},{32,34},{33,50},{64,66},{65,82},{96,98},{97,114},{128... | collective-permute-start | bytes 983048 | tf_op jit(solution)/shard_map/ppermute | solution.py:35
  12.2 2.1 %collective-permute-start = (bf16[320,512]{1,0:T(8,128)(2,1)}, bf16[320,512]{1,0:T(8,128)(2,1)S(1)}, u32[]{:S(2)}, u32[]{:S(2)}) collective-permute-start(bf16[320,512]{1,0:T(8,128)(2,1)} %bitcast.65), channel_id=1, source_target_pairs={{0,0},{1,16},{32,32},{33,48},{64,64},{65,80},{96,96},{97,112},{128... | collective-permute-start | bytes 983048 | tf_op jit(solution)/shard_map/ppermute | solution.py:35
  14.3 2.0 %fusion.7 = bf16[864,512]{1,0:T(8,128)(2,1)S(1)} fusion(bf16[512,864]{0,1:T(8,128)(2,1)} %param.5, bf16[512,864]{0,1:T(8,128)(2,1)} %param.4), kind=kLoop, calls=%fused_computation.12 | loop fusion | flops 3538944 | bytes 2654208 | tf_op jit(solution)/shard_map/convert_element_type | solution.py:43
  16.3 1.3 collective-permute-done.1
  17.6 4.7 %collective-permute-done = bf16[320,512]{1,0:T(8,128)(2,1)S(1)} collective-permute-done((bf16[320,512]{1,0:T(8,128)(2,1)}, bf16[320,512]{1,0:T(8,128)(2,1)S(1)}, u32[]{:S(2)}, u32[]{:S(2)}) %collective-permute-start) | collective-permute-done | bytes 327712 | tf_op jit(solution)/shard_map/ppermute | solution.py:35
  22.4 2.6 %collective-permute-start.3 = (bf16[640,512]{1,0:T(8,128)(2,1)S(1)}, bf16[640,512]{1,0:T(8,128)(2,1)S(1)}, u32[]{:S(2)}, u32[]{:S(2)}) collective-permute-start(bf16[640,512]{1,0:T(8,128)(2,1)S(1)} %bitcast.59), channel_id=1, source_target_pairs={{0,12},{1,13},{32,44},{33,45},{64,76},{65,77},{96,108},{97,109},{1... | collective-permute-start | bytes 1966088 | tf_op jit(solution)/shard_map/ppermute | solution.py:35
  24.9 13.2 %collective-permute-done.3 = bf16[640,512]{1,0:T(8,128)(2,1)S(1)} collective-permute-done((bf16[640,512]{1,0:T(8,128)(2,1)S(1)}, bf16[640,512]{1,0:T(8,128)(2,1)S(1)}, u32[]{:S(2)}, u32[]{:S(2)}) %collective-permute-start.3) | collective-permute-done | bytes 655392 | tf_op jit(solution)/shard_map/ppermute | solution.py:35
  38.1 1.0 collective-permute-start.5
  39.1 0.3 collective-permute-done.2
  39.4 0.8 copy-done.6
  40.2 0.4 collective-permute-start.4
  40.7 0.2 broadcast_in_dim.3
  40.9 0.9 copy-done.3
  42.0 0.2 copy-done.5
  42.2 4.1 %collective-permute-done.6 = bf16[864,512]{1,0:T(8,128)(2,1)} collective-permute-done((bf16[864,512]{1,0:T(8,128)(2,1)S(1)}, bf16[864,512]{1,0:T(8,128)(2,1)}, u32[]{:S(2)}, u32[]{:S(2)}) %collective-permute-start.6) | collective-permute-done | bytes 884768 | tf_op jit(solution)/shard_map/ppermute | solution.py:35
  46.3 1.2 collective-permute-done.5
  47.5 2.2 %collective-permute-done.4 = bf16[320,512]{1,0:T(8,128)(2,1)S(1)} collective-permute-done((bf16[320,512]{1,0:T(8,128)(2,1)S(1)}, bf16[320,512]{1,0:T(8,128)(2,1)S(1)}, u32[]{:S(2)}, u32[]{:S(2)}) %collective-permute-start.4) | collective-permute-done | bytes 327712 | tf_op jit(solution)/shard_map/ppermute | solution.py:35
  49.7 0.3 collective-permute-start.10
  50.0 1.3 broadcast_select_fusion
  51.4 3.7 %collective-permute-done.10 = bf16[2560,512]{1,0:T(8,128)(2,1)} collective-permute-done((bf16[2560,512]{1,0:T(8,128)(2,1)S(1)}, bf16[2560,512]{1,0:T(8,128)(2,1)}, u32[]{:S(2)}, u32[]{:S(2)}) %collective-permute-start.10) | collective-permute-done | bytes 2621472 | tf_op jit(solution)/shard_map/ppermute | solution.py:35
  55.1 4.7 %fusion.21 = f32[2560,864]{1,0:T(8,128)S(1)} fusion(bf16[2560,512]{1,0:T(8,128)(2,1)} %collective-permute-done.10, bf16[864,512]{1,0:T(8,128)(2,1)S(1)} %get-tuple-element.35), kind=kOutput, calls=%fused_computation.48 | convolution fusion | flops 2264924160 | bytes 12353536 | tf_op jit(solution)/shard_map/dot_general | solution.py:51
  59.8 4.6 %add_convert_fusion = bf16[2560,864]{1,0:T(8,128)(2,1)} fusion(f32[2560,864]{1,0:T(8,128)S(1)} %fusion.21, bf16[2560,512]{1,0:T(8,128)(2,1)S(1)} %constant_dynamic-update-slice_fusion, bf16[864,512]{1,0:T(8,128)(2,1)S(1)} %get-tuple-element.37), kind=kOutput, calls=%fused_computation | convolution fusion | flops 2269347840 | bytes 16777216 | tf_op jit(solution)/shard_map/dot_general | solution.py:51
  64.4 7.7 %all-gather.2.cloned.1.call-done = bf16[2560,864]{1,0:T(8,128)(2,1)} async-done(((bf16[320,864]{1,0:T(8,128)(2,1)}), bf16[2560,864]{1,0:T(8,128)(2,1)}) %all-gather.2.cloned.1.call-update) | async-done | bytes 4423696 | tf_op jit(solution)/shard_map/all_gather | solution.py:73
  72.1 7.0 %fusion = bf16[2560,512]{1,0:T(8,128)(2,1)} fusion(bf16[2560,864]{1,0:T(8,128)(2,1)} %all-gather.2.cloned.1.call-done, bf16[864,512]{1,0:T(8,128)(2,1)} %copy-done.10), kind=kOutput, calls=%fused_computation.3 | convolution fusion | flops 2266234880 | bytes 7929856 | tf_op jit(solution)/shard_map/dot_general | solution.py:51
  79.1 0.7 collective-permute-start.7
  79.8 4.9 %collective-permute-done.7 = bf16[2560,512]{1,0:T(8,128)(2,1)} collective-permute-done((bf16[2560,512]{1,0:T(8,128)(2,1)}, bf16[2560,512]{1,0:T(8,128)(2,1)}, u32[]{:S(2)}, u32[]{:S(2)}) %collective-permute-start.7) | collective-permute-done | bytes 2621472 | tf_op jit(solution)/shard_map/ppermute | solution.py:35
  84.7 6.0 %add_convert_fusion.1 = bf16[2560,512]{1,0:T(8,128)(2,1)S(1)} fusion(bf16[2560,512]{1,0:T(8,128)(2,1)} %collective-permute-done.7, bf16[2560,864]{1,0:T(8,128)(2,1)} %all-gather.2.cloned.1.call-done, bf16[864,512]{1,0:T(8,128)(2,1)S(1)} %copy-done.9), kind=kOutput, calls=%fused_computation.1 | convolution fusion | flops 2268856320 | bytes 10551296 | tf_op jit(solution)/shard_map/dot_general | solution.py:51
  90.7 0.2 constant_dynamic-slice_fusion
  90.9 1.4 collective-permute-start.8
  92.2 1.4 collective-permute-start.9
  93.7 2.6 %collective-permute-start.14 = (bf16[320,512]{1,0:T(8,128)(2,1)S(1)}, bf16[320,512]{1,0:T(8,128)(2,1)S(1)}, u32[]{:S(2)}, u32[]{:S(2)}) collective-permute-start(bf16[320,512]{1,0:T(8,128)(2,1)S(1)} %get-tuple-element.42), channel_id=1, source_target_pairs={{0,12},{1,13},{32,44},{33,45},{64,76},{65,77},{96,108},{97,109},{1... | collective-permute-start | bytes 983048 | tf_op jit(solution)/shard_map/ppermute | solution.py:35
  96.3 2.5 %fusion.15 = bf16[864,512]{1,0:T(8,128)(2,1)S(1)} fusion(bf16[2560,864]{1,0:T(8,128)(2,1)S(1)} %copy-done.11, bf16[2560,512]{1,0:T(8,128)(2,1)} %collective-permute-done.10, bf16[2560,512]{1,0:T(8,128)(2,1)S(1)} %constant_dynamic-update-slice_fusion, pred[]{:T(512)S(6)} %eq.10), kind=kOutput, calls=%fused_computation.25 | convolution fusion | flops 2266677248 | bytes 10551297 | tf_op jit(solution)/shard_map/dot_general | solution.py:51
  98.8 2.2 %collective-permute-done.8 = bf16[320,512]{1,0:T(8,128)(2,1)S(1)} collective-permute-done((bf16[320,512]{1,0:T(8,128)(2,1)S(1)}, bf16[320,512]{1,0:T(8,128)(2,1)S(1)}, u32[]{:S(2)}, u32[]{:S(2)}) %collective-permute-start.8) | collective-permute-done | bytes 327712 | tf_op jit(solution)/shard_map/ppermute | solution.py:35
  101.0 0.2 add_convert_fusion.5
  101.2 1.2 collective-permute-start.11
  102.4 1.5 %collective-permute-start.12 = (bf16[320,512]{1,0:T(8,128)(2,1)S(1)}, bf16[320,512]{1,0:T(8,128)(2,1)S(1)}, u32[]{:S(2)}, u32[]{:S(2)}) collective-permute-start(bf16[320,512]{1,0:T(8,128)(2,1)S(1)} %get-tuple-element.51), channel_id=1, source_target_pairs={{0,12},{1,13},{32,44},{33,45},{64,76},{65,77},{96,108},{97,109},{1... | collective-permute-start | bytes 983048 | tf_op jit(solution)/shard_map/ppermute | solution.py:35
  103.9 3.1 %collective-permute-start.17 = (bf16[864,512]{1,0:T(8,128)(2,1)S(1)}, bf16[864,512]{1,0:T(8,128)(2,1)S(1)}, u32[]{:S(2)}, u32[]{:S(2)}) collective-permute-start(bf16[864,512]{1,0:T(8,128)(2,1)S(1)} %fusion.15), channel_id=1, source_target_pairs={{0,16},{1,17},{32,48},{33,49},{64,80},{65,81},{96,112},{97,113},{1... | collective-permute-start | bytes 2654216 | tf_op jit(solution)/shard_map/ppermute | solution.py:35
  107.0 4.3 %fusion.1 = f32[864,512]{1,0:T(8,128)S(1)} fusion(bf16[2560,864]{1,0:T(8,128)(2,1)S(1)} %copy-done.11, bf16[2560,512]{1,0:T(8,128)(2,1)S(1)} %constant_dynamic-update-slice_fusion, bf16[2560,512]{1,0:T(8,128)(2,1)} %collective-permute-done.10, pred[]{:T(512)S(6)} %eq.10), kind=kOutput, calls=%fused_computation.4 | convolution fusion | flops 2266234880 | bytes 11436033 | tf_op jit(solution)/shard_map/dot_general | solution.py:51
  111.3 3.7 %collective-permute-done.11 = bf16[320,512]{1,0:T(8,128)(2,1)S(1)} collective-permute-done((bf16[320,512]{1,0:T(8,128)(2,1)S(1)}, bf16[320,512]{1,0:T(8,128)(2,1)S(1)}, u32[]{:S(2)}, u32[]{:S(2)}) %collective-permute-start.11) | collective-permute-done | bytes 327712 | tf_op jit(solution)/shard_map/ppermute | solution.py:35
  115.0 0.3 add_convert_fusion.3
  115.4 3.8 %collective-permute-start.16 = (bf16[320,512]{1,0:T(8,128)(2,1)S(1)}, bf16[320,512]{1,0:T(8,128)(2,1)S(1)}, u32[]{:S(2)}, u32[]{:S(2)}) collective-permute-start(bf16[320,512]{1,0:T(8,128)(2,1)S(1)} %get-tuple-element.62), channel_id=1, source_target_pairs={{0,2},{1,18},{32,34},{33,50},{64,66},{65,82},{96,98},{97,114},{128... | collective-permute-start | bytes 983048 | tf_op jit(solution)/shard_map/ppermute | solution.py:35
  119.2 2.2 %collective-permute-start.15 = (bf16[320,512]{1,0:T(8,128)(2,1)S(1)}, bf16[320,512]{1,0:T(8,128)(2,1)S(1)}, u32[]{:S(2)}, u32[]{:S(2)}) collective-permute-start(bf16[320,512]{1,0:T(8,128)(2,1)S(1)} %get-tuple-element.63), channel_id=1, source_target_pairs={{0,0},{1,16},{32,32},{33,48},{64,64},{65,80},{96,96},{97,112},{128... | collective-permute-start | bytes 983048 | tf_op jit(solution)/shard_map/ppermute | solution.py:35
  121.4 2.4 %collective-permute-done.17 = bf16[864,512]{1,0:T(8,128)(2,1)S(1)} collective-permute-done((bf16[864,512]{1,0:T(8,128)(2,1)S(1)}, bf16[864,512]{1,0:T(8,128)(2,1)S(1)}, u32[]{:S(2)}, u32[]{:S(2)}) %collective-permute-start.17) | collective-permute-done | bytes 884768 | tf_op jit(solution)/shard_map/ppermute | solution.py:35
  123.8 2.2 %fusion.18 = (bf16[512,864]{0,1:T(8,128)(2,1)}, bf16[512,864]{0,1:T(8,128)(2,1)}) fusion(f32[864,512]{1,0:T(8,128)S(1)} %fusion.1, bf16[864,512]{1,0:T(8,128)(2,1)S(1)} %collective-permute-done.17, bf16[512,864]{0,1:T(8,128)(2,1)S(1)} %copy-done.1, bf16[512,864]{0,1:T(8,128)(2,1)S(1)} %copy-done), kind=kLoop, calls=%fused_computation.26 | loop fusion | flops 7520256 | bytes 6193152 | tf_op jit(solution)/shard_map/transpose | solution.py:140
  126.0 6.4 %reduce-scatter.2.cloned.1.call-done = bf16[320,864]{1,0:T(8,128)(2,1)} async-done(((bf16[2560,864]{1,0:T(8,128)(2,1)}), bf16[320,864]{1,0:T(8,128)(2,1)}) %reduce-scatter.2.cloned.1.call-update) | async-done | bytes 552976 | tf_op jit(solution)/shard_map/reduce_scatter | solution.py:103
  132.4 2.1 %convert_element_type.129 = f32[320,864]{1,0:T(8,128)} convert(bf16[320,864]{1,0:T(8,128)(2,1)} %reduce-scatter.2.cloned.1.call-done) | non-fusion elementwise | flops 276480 | bytes 1658880 | tf_op jit(solution)/shard_map/convert_element_type | solution.py:39
  134.6 0.8 fusion.20
  (41 shorter events, 0.7 us)
Async XLA Ops:
  7.2 65.0 %all-gather.2.cloned.1.call-start = ((), (), s32[]{:S(2)}) async-start(), calls=%async_computation.1 | async-start | bytes 5160960 | tf_op jit(solution)/shard_map/all_gather | solution.py:73
  7.9 124.5 %reduce-scatter.2.cloned.1.call-start = ((), (), s32[]{:S(2)}) async-start(), calls=%async_computation.2 | async-start | bytes 5160960 | tf_op jit(solution)/shard_map/reduce_scatter | solution.py:103
  7.9 9.6 %collective-permute-start.1 = (bf16[320,512]{1,0:T(8,128)(2,1)}, bf16[320,512]{1,0:T(8,128)(2,1)S(1)}, u32[]{:S(2)}, u32[]{:S(2)}) collective-permute-start(bf16[320,512]{1,0:T(8,128)(2,1)} %bitcast.64), channel_id=1, source_target_pairs={{0,2},{1,18},{32,34},{33,50},{64,66},{65,82},{96,98},{97,114},{128... | collective-permute-start | bytes 983048 | tf_op jit(solution)/shard_map/ppermute | solution.py:35
  12.2 10.1 %collective-permute-start = (bf16[320,512]{1,0:T(8,128)(2,1)}, bf16[320,512]{1,0:T(8,128)(2,1)S(1)}, u32[]{:S(2)}, u32[]{:S(2)}) collective-permute-start(bf16[320,512]{1,0:T(8,128)(2,1)} %bitcast.65), channel_id=1, source_target_pairs={{0,0},{1,16},{32,32},{33,48},{64,64},{65,80},{96,96},{97,112},{128... | collective-permute-start | bytes 983048 | tf_op jit(solution)/shard_map/ppermute | solution.py:35
  22.4 17.1 %copy-start.2 = (bf16[2,320,512]{2,1,0:T(8,128)(2,1)}, bf16[2,320,512]{2,1,0:T(8,128)(2,1)S(1)}, u32[]{:S(2)}) copy-start(bf16[2,320,512]{2,1,0:T(8,128)(2,1)S(1)} %maximum_select_fusion) | copy-start | bytes 1966084
  22.4 15.7 %collective-permute-start.3 = (bf16[640,512]{1,0:T(8,128)(2,1)S(1)}, bf16[640,512]{1,0:T(8,128)(2,1)S(1)}, u32[]{:S(2)}, u32[]{:S(2)}) collective-permute-start(bf16[640,512]{1,0:T(8,128)(2,1)S(1)} %bitcast.59), channel_id=1, source_target_pairs={{0,12},{1,13},{32,44},{33,45},{64,76},{65,77},{96,108},{97,109},{1... | collective-permute-start | bytes 1966088 | tf_op jit(solution)/shard_map/ppermute | solution.py:35
  24.9 14.5 %collective-permute-start.2 = (bf16[640,512]{1,0:T(8,128)(2,1)S(1)}, bf16[640,512]{1,0:T(8,128)(2,1)S(1)}, u32[]{:S(2)}, u32[]{:S(2)}) collective-permute-start(bf16[640,512]{1,0:T(8,128)(2,1)S(1)} %bitcast.60), channel_id=1, source_target_pairs={{0,4},{1,5},{32,36},{33,37},{64,68},{65,69},{96,100},{97,101},{128... | collective-permute-start | bytes 1966088 | tf_op jit(solution)/shard_map/ppermute | solution.py:35
  24.9 21.4 %collective-permute-start.6 = (bf16[864,512]{1,0:T(8,128)(2,1)S(1)}, bf16[864,512]{1,0:T(8,128)(2,1)}, u32[]{:S(2)}, u32[]{:S(2)}) collective-permute-start(bf16[864,512]{1,0:T(8,128)(2,1)S(1)} %fusion.7), channel_id=1, source_target_pairs={{0,16},{1,17},{32,48},{33,49},{64,80},{65,81},{96,112},{97,113},{1... | collective-permute-start | bytes 2654216 | tf_op jit(solution)/shard_map/ppermute | solution.py:35
  38.1 1.3 copy-start.4
  38.1 9.4 %collective-permute-start.5 = (bf16[320,512]{1,0:T(8,128)(2,1)S(1)}, bf16[320,512]{1,0:T(8,128)(2,1)S(1)}, u32[]{:S(2)}, u32[]{:S(2)}) collective-permute-start(bf16[320,512]{1,0:T(8,128)(2,1)S(1)} %slice.10), channel_id=1, source_target_pairs={{0,12},{1,13},{32,44},{33,45},{64,76},{65,77},{96,108},{97,109},{1... | collective-permute-start | bytes 983048 | tf_op jit(solution)/shard_map/ppermute | solution.py:35
  39.4 0.8 copy-start.6
  40.2 9.5 %collective-permute-start.4 = (bf16[320,512]{1,0:T(8,128)(2,1)S(1)}, bf16[320,512]{1,0:T(8,128)(2,1)S(1)}, u32[]{:S(2)}, u32[]{:S(2)}) collective-permute-start(bf16[320,512]{1,0:T(8,128)(2,1)S(1)} %slice.9), channel_id=1, source_target_pairs={{0,4},{1,5},{32,36},{33,37},{64,68},{65,69},{96,100},{97,101},{128... | collective-permute-start | bytes 983048 | tf_op jit(solution)/shard_map/ppermute | solution.py:35
  40.7 1.1 copy-start.3
  40.7 1.3 copy-start.7
  40.7 1.5 %copy-start.5 = (bf16[640,512]{1,0:T(8,128)(2,1)S(1)}, bf16[640,512]{1,0:T(8,128)(2,1)}, u32[]{:S(2)}) copy-start(bf16[640,512]{1,0:T(8,128)(2,1)} %copy-done.4) | copy-start | bytes 1966084
  49.7 5.3 %collective-permute-start.10 = (bf16[2560,512]{1,0:T(8,128)(2,1)S(1)}, bf16[2560,512]{1,0:T(8,128)(2,1)}, u32[]{:S(2)}, u32[]{:S(2)}) collective-permute-start(bf16[2560,512]{1,0:T(8,128)(2,1)S(1)} %constant_dynamic-update-slice_fusion), channel_id=1, source_target_pairs={{0,1},{1,0},{32,33},{33,32},{64,65},{65,64},{96,97},{97,96},{128,1... | collective-permute-start | bytes 7864328 | tf_op jit(solution)/shard_map/ppermute | solution.py:35
  51.3 3.7 %copy-start.10 = (bf16[864,512]{1,0:T(8,128)(2,1)}, bf16[864,512]{1,0:T(8,128)(2,1)S(1)}, u32[]{:S(2)}) copy-start(bf16[864,512]{1,0:T(8,128)(2,1)S(1)} %get-tuple-element.35) | copy-start | bytes 2654212
  51.3 8.4 %copy-start.8 = (bf16[864,512]{1,0:T(8,128)(2,1)}, bf16[864,512]{1,0:T(8,128)(2,1)S(1)}, u32[]{:S(2)}) copy-start(bf16[864,512]{1,0:T(8,128)(2,1)S(1)} %get-tuple-element.37) | copy-start | bytes 2654212
  64.4 20.2 %copy-start.9 = (bf16[864,512]{1,0:T(8,128)(2,1)S(1)}, bf16[864,512]{1,0:T(8,128)(2,1)}, u32[]{:S(2)}) copy-start(bf16[864,512]{1,0:T(8,128)(2,1)} %copy-done.8) | copy-start | bytes 2654212
  79.1 5.6 %collective-permute-start.7 = (bf16[2560,512]{1,0:T(8,128)(2,1)}, bf16[2560,512]{1,0:T(8,128)(2,1)}, u32[]{:S(2)}, u32[]{:S(2)}) collective-permute-start(bf16[2560,512]{1,0:T(8,128)(2,1)} %fusion), channel_id=1, source_target_pairs={{0,1},{1,0},{32,33},{33,32},{64,65},{65,64},{96,97},{97,96},{128,1... | collective-permute-start | bytes 7864328 | tf_op jit(solution)/shard_map/ppermute | solution.py:35
  84.6 11.7 %copy-start.11 = (bf16[2560,864]{1,0:T(8,128)(2,1)S(1)}, bf16[2560,864]{1,0:T(8,128)(2,1)}, u32[]{:S(2)}) copy-start(bf16[2560,864]{1,0:T(8,128)(2,1)} %all-gather.2.cloned.1.call-done) | copy-start | bytes 13271044
  90.9 10.1 %collective-permute-start.8 = (bf16[320,512]{1,0:T(8,128)(2,1)S(1)}, bf16[320,512]{1,0:T(8,128)(2,1)S(1)}, u32[]{:S(2)}, u32[]{:S(2)}) collective-permute-start(bf16[320,512]{1,0:T(8,128)(2,1)S(1)} %get-tuple-element.39), channel_id=1, source_target_pairs={{0,4},{1,5},{32,36},{33,37},{64,68},{65,69},{96,100},{97,101},{128... | collective-permute-start | bytes 983048 | tf_op jit(solution)/shard_map/ppermute | solution.py:35
  92.2 8.7 %collective-permute-start.9 = (bf16[320,512]{1,0:T(8,128)(2,1)S(1)}, bf16[320,512]{1,0:T(8,128)(2,1)S(1)}, u32[]{:S(2)}, u32[]{:S(2)}) collective-permute-start(bf16[320,512]{1,0:T(8,128)(2,1)S(1)} %get-tuple-element.40), channel_id=1, source_target_pairs={{0,12},{1,13},{32,44},{33,45},{64,76},{65,77},{96,108},{97,109},{1... | collective-permute-start | bytes 983048 | tf_op jit(solution)/shard_map/ppermute | solution.py:35
  93.6 17.6 %collective-permute-start.13 = (bf16[320,512]{1,0:T(8,128)(2,1)S(1)}, bf16[320,512]{1,0:T(8,128)(2,1)S(1)}, u32[]{:S(2)}, u32[]{:S(2)}) collective-permute-start(bf16[320,512]{1,0:T(8,128)(2,1)S(1)} %get-tuple-element.41), channel_id=1, source_target_pairs={{0,4},{1,5},{32,36},{33,37},{64,68},{65,69},{96,100},{97,101},{128... | collective-permute-start | bytes 983048 | tf_op jit(solution)/shard_map/ppermute | solution.py:35
  93.7 17.6 %collective-permute-start.14 = (bf16[320,512]{1,0:T(8,128)(2,1)S(1)}, bf16[320,512]{1,0:T(8,128)(2,1)S(1)}, u32[]{:S(2)}, u32[]{:S(2)}) collective-permute-start(bf16[320,512]{1,0:T(8,128)(2,1)S(1)} %get-tuple-element.42), channel_id=1, source_target_pairs={{0,12},{1,13},{32,44},{33,45},{64,76},{65,77},{96,108},{97,109},{1... | collective-permute-start | bytes 983048 | tf_op jit(solution)/shard_map/ppermute | solution.py:35
  101.2 13.9 %collective-permute-start.11 = (bf16[320,512]{1,0:T(8,128)(2,1)S(1)}, bf16[320,512]{1,0:T(8,128)(2,1)S(1)}, u32[]{:S(2)}, u32[]{:S(2)}) collective-permute-start(bf16[320,512]{1,0:T(8,128)(2,1)S(1)} %get-tuple-element.50), channel_id=1, source_target_pairs={{0,4},{1,5},{32,36},{33,37},{64,68},{65,69},{96,100},{97,101},{128... | collective-permute-start | bytes 983048 | tf_op jit(solution)/shard_map/ppermute | solution.py:35
  102.4 12.6 %collective-permute-start.12 = (bf16[320,512]{1,0:T(8,128)(2,1)S(1)}, bf16[320,512]{1,0:T(8,128)(2,1)S(1)}, u32[]{:S(2)}, u32[]{:S(2)}) collective-permute-start(bf16[320,512]{1,0:T(8,128)(2,1)S(1)} %get-tuple-element.51), channel_id=1, source_target_pairs={{0,12},{1,13},{32,44},{33,45},{64,76},{65,77},{96,108},{97,109},{1... | collective-permute-start | bytes 983048 | tf_op jit(solution)/shard_map/ppermute | solution.py:35
  103.9 19.9 %collective-permute-start.17 = (bf16[864,512]{1,0:T(8,128)(2,1)S(1)}, bf16[864,512]{1,0:T(8,128)(2,1)S(1)}, u32[]{:S(2)}, u32[]{:S(2)}) collective-permute-start(bf16[864,512]{1,0:T(8,128)(2,1)S(1)} %fusion.15), channel_id=1, source_target_pairs={{0,16},{1,17},{32,48},{33,49},{64,80},{65,81},{96,112},{97,113},{1... | collective-permute-start | bytes 2654216 | tf_op jit(solution)/shard_map/ppermute | solution.py:35
  111.3 12.5 %copy-start = (bf16[512,864]{0,1:T(8,128)(2,1)S(1)}, bf16[512,864]{0,1:T(8,128)(2,1)}, u32[]{:S(2)}) copy-start(bf16[512,864]{0,1:T(8,128)(2,1)} %param.5) | copy-start | bytes 2654212
  111.3 12.5 %copy-start.1 = (bf16[512,864]{0,1:T(8,128)(2,1)S(1)}, bf16[512,864]{0,1:T(8,128)(2,1)}, u32[]{:S(2)}) copy-start(bf16[512,864]{0,1:T(8,128)(2,1)} %param.4) | copy-start | bytes 2654212
  115.4 19.2 %collective-permute-start.16 = (bf16[320,512]{1,0:T(8,128)(2,1)S(1)}, bf16[320,512]{1,0:T(8,128)(2,1)S(1)}, u32[]{:S(2)}, u32[]{:S(2)}) collective-permute-start(bf16[320,512]{1,0:T(8,128)(2,1)S(1)} %get-tuple-element.62), channel_id=1, source_target_pairs={{0,2},{1,18},{32,34},{33,50},{64,66},{65,82},{96,98},{97,114},{128... | collective-permute-start | bytes 983048 | tf_op jit(solution)/shard_map/ppermute | solution.py:35
  119.2 15.4 %collective-permute-start.15 = (bf16[320,512]{1,0:T(8,128)(2,1)S(1)}, bf16[320,512]{1,0:T(8,128)(2,1)S(1)}, u32[]{:S(2)}, u32[]{:S(2)}) collective-permute-start(bf16[320,512]{1,0:T(8,128)(2,1)S(1)} %get-tuple-element.63), channel_id=1, source_target_pairs={{0,0},{1,16},{32,32},{33,48},{64,64},{65,80},{96,96},{97,112},{128... | collective-permute-start | bytes 983048 | tf_op jit(solution)/shard_map/ppermute | solution.py:35
Sparse Core Ops, SparseCore 0:
  9.8 62.2 all-gather.1
  74.7 57.6 reduce-scatter.1
